TPU v7x, 256 devices: a whole 4x4x8 slice. The times are simulated.
256 devices in a mesh: dp: 32 (over x, y, core), seq: 8 (over z).
Axes of the slice: x: 4, y: 4, z: 8, core: 2. Of those that a mesh axis runs over, the one named last changes fastest.
Arguments:
- features: bfloat16 [65536, 1024], P(('dp', 'seq')), may hold values from -16 to 16
- out_grad: bfloat16 [65536, 1024], P(('dp', 'seq')), may hold values from -6 to 6
- norm_gain: float32 [1024], replicated, may hold values from 0.25 to 1.75
- w_qkv: bfloat16 [1024, 1536], replicated, may hold values from -0.1875 to 0.1875
- w_out: bfloat16 [512, 1024], replicated, may hold values from -0.25 to 0.25
- w_msg: bfloat16 [1024, 1024], replicated, may hold values from -0.1875 to 0.1875
- block_ids: int32 [512, 4], P(('dp', 'seq')), may hold values from 0 to 15, as said below
- block_counts: int32 [512], P(('dp', 'seq')), may hold values from 1 to 4, as said below
- edge_tiles: bfloat16 [512, 4, 128, 128], P(('dp', 'seq')), may hold values from -0.375 to 0.375
Outputs:
- block_result_array: bfloat16 [65536, 1024], P(('dp', 'seq'))
- grad_input: bfloat16 [65536, 1024], P(('dp', 'seq'))
- grad_gain: float32 [1024], P('dp')
- grad_qkv: float32 [1024, 1536], P('dp')
- grad_w_out: float32 [512, 1024], P('dp')
- grad_msg: float32 [1024, 1024], P('dp')
Inputs may be any that keep to these rules, and one draw needn't show every extreme that they name: `block_ids`: slot 0 of a block's list is the block itself; every entry names a block of the same cluster at most 2 blocks away, and that distance is reached in every cluster. `block_counts`: every cluster has a block with all 4 slots live.
All inputs are finite; a program needn't handle non-finite values.
Results may differ from a plain program's by a relative error of at most 0.035.
Values may be sent and summed in bfloat16 or wider, within the bound.
No kernel may reach another device: no remote copies, remote signals or barrier semaphores. Data moves between devices by JAX's collectives and lax.ppermute only.
A program may use at most 128 MiB of HBM per device.

v0:
```python
import jax
import jax.numpy as jnp
from jax import lax
from jax.experimental import pallas as pl
from jax.experimental.pallas import tpu as pltpu
from jax.sharding import Mesh
from jax.sharding import PartitionSpec as P

HEAD_DIM = 64
BLOCK = 128
SLOTS = 4
N_SEQ = 8
N_XY = 16
CHUNK = 256
ONES = 16

exponent_divisor = 32.0
epsilon = 1e-06
SCALE = exponent_divisor / HEAD_DIM


def matmul(left, right):
    return jnp.dot(left, right, preferred_element_type=jnp.float32)


def contract_rows(left, right):
    return lax.dot_general(
        left, right, (((0,), (0,)), ((), ())), preferred_element_type=jnp.float32
    )


def contract_cols(left, right):
    return lax.dot_general(
        left, right, (((1,), (1,)), ((), ())), preferred_element_type=jnp.float32
    )


def unit_factor(wide, axis):
    return lax.rsqrt(jnp.mean(wide * wide, axis=axis, keepdims=True) + epsilon)


def call(kernel, name, out_shape, scalars, arrays, scratch=(), flops=0, exps=0, moved=0):
    specs = [pl.BlockSpec(memory_space=pltpu.SMEM)] * len(scalars)
    specs += [pl.BlockSpec(memory_space=pltpu.VMEM)] * len(arrays)
    return pl.pallas_call(
        kernel,
        out_shape=tuple(jax.ShapeDtypeStruct(s, t) for s, t in out_shape),
        in_specs=specs,
        out_specs=tuple(pl.BlockSpec(memory_space=pltpu.VMEM) for _ in out_shape),
        scratch_shapes=list(scratch),
        compiler_params=pltpu.CompilerParams(vmem_limit_bytes=50 * 1024 * 1024),
        cost_estimate=pl.CostEstimate(flops=flops, bytes_accessed=moved, transcendentals=exps),
        name=name,
    )(*scalars, *arrays)


def normalize_kernel(x_ref, gain_ref, out_ref):
    wide = x_ref[...].astype(jnp.float32)
    out_ref[...] = (wide * unit_factor(wide, -1) * gain_ref[...]).astype(jnp.bfloat16)


def d_out_kernel(grad_ref, w_ref, out_ref):
    turned = contract_cols(w_ref[...], grad_ref[...]).astype(jnp.bfloat16)
    for h in range(N_SEQ):
        out_ref[h] = turned[h * HEAD_DIM : (h + 1) * HEAD_DIM]


def pick_kernel(place_ref, q_ref, k_ref, v_ref, out_ref, turned):
    odd = lax.rem(place_ref[0], 2)
    for t, ref in enumerate((q_ref, k_ref, v_ref)):
        turned[...] = ref[...].astype(jnp.float32).T
        out_ref[t * HEAD_DIM : (t + 1) * HEAD_DIM] = turned[
            pl.ds(odd * HEAD_DIM, HEAD_DIM), :
        ].astype(jnp.bfloat16)


def pick_head(place, w_qkv):
    width, columns = w_qkv.shape
    step = columns // 3 // (2 * HEAD_DIM)

    def block(t):
        return pl.BlockSpec((width, 2 * HEAD_DIM), lambda i, place: (0, t * step + place[0] // 2))

    return pl.pallas_call(
        pick_kernel,
        grid_spec=pltpu.PrefetchScalarGridSpec(
            num_scalar_prefetch=1,
            grid=(1,),
            in_specs=[block(0), block(1), block(2)],
            out_specs=pl.BlockSpec((3 * HEAD_DIM, width), lambda i, place: (0, 0)),
            scratch_shapes=[pltpu.VMEM((2 * HEAD_DIM, width), jnp.float32)],
        ),
        out_shape=jax.ShapeDtypeStruct((3 * HEAD_DIM, width), jnp.bfloat16),
        cost_estimate=pl.CostEstimate(flops=0, bytes_accessed=4 << 20, transcendentals=0),
        name="pick_head",
    )(place, w_qkv, w_qkv, w_qkv)


def message_kernel(*refs):
    place_ref, ids_ref, counts_ref, low_ref, own_ref, high_ref, w_ref, tiles_ref, grad_ref = refs[:9]
    act_ref, to_low_ref, mid_ref, to_high_ref, msg, landed = refs[9:]
    z = place_ref[0]
    for t, ref in enumerate((low_ref, own_ref, high_ref)):
        rows = matmul(ref[...], w_ref[...]).astype(jnp.bfloat16)
        msg[2 * t] = rows[:BLOCK]
        msg[2 * t + 1] = rows[BLOCK:]
    landed[...] = jnp.zeros_like(landed)
    for b in range(2):
        spots = []
        live = []
        for s in range(SLOTS):
            spots.append(jnp.clip(ids_ref[b, s] - 2 * (z - 1), 0, 5))
            mask = jnp.where(s < counts_ref[b], 1.0, 0.0)
            live.append(tiles_ref[b, s].astype(jnp.float32) * mask)
        source = jnp.concatenate([msg[spot] for spot in spots], axis=0)
        agg = matmul(jnp.concatenate(live, axis=1).astype(jnp.bfloat16), source)
        sigma = 1.0 / (1.0 + jnp.exp(-agg))
        rows = slice(b * BLOCK, (b + 1) * BLOCK)
        act_ref[rows] = agg * sigma
        d_agg = grad_ref[rows].astype(jnp.float32) * sigma * (1.0 + agg * (1.0 - sigma))
        d_agg = d_agg.astype(jnp.bfloat16)
        for s in range(SLOTS):
            landed[spots[s]] += matmul(live[s].T.astype(jnp.bfloat16), d_agg)
    for b in range(2):
        rows = slice(b * BLOCK, (b + 1) * BLOCK)
        to_low_ref[rows] = landed[b].astype(jnp.bfloat16)
        mid_ref[rows] = landed[2 + b]
        to_high_ref[rows] = landed[4 + b].astype(jnp.bfloat16)


def split_rows(core, source, keep_ref, give_ref, offset=0):
    rows = source.shape[0] // (2 * N_XY)
    for i in range(N_XY):
        for t in range(source.shape[1] // BLOCK):
            spot = slice(offset + t * rows, offset + (t + 1) * rows)
            columns = slice(t * BLOCK, (t + 1) * BLOCK)
            keep_ref[i, spot] = source[pl.ds((2 * i + core) * rows, rows), columns].astype(jnp.bfloat16)
            give_ref[i, spot] = source[pl.ds((2 * i + 1 - core) * rows, rows), columns].astype(
                jnp.bfloat16
            )


def message_grad_kernel(*refs):
    mid_ref, above_ref, below_ref, w_ref = refs[:4]
    cut_ref, d_norm_ref = refs[4:]
    total = mid_ref[...] + above_ref[...].astype(jnp.float32) + below_ref[...].astype(jnp.float32)
    d_msg = total.astype(jnp.bfloat16)
    for t in range(N_SEQ):
        cut_ref[t] = d_msg[:, t * BLOCK : (t + 1) * BLOCK]
    d_norm_ref[...] = contract_cols(d_msg, w_ref[...])


def place_of(z, j):
    return lax.rem(z - j + N_SEQ, N_SEQ)


def forward_kernel(*refs):
    z = refs[0][0]
    chunks = refs[1:9]
    w_ref, d_ref = refs[9:11]
    out_ref, kv_ref, qd_ref, hq_ref, ku_ref, raw_ref, stats_ref = refs[11:18]
    v_ext = refs[18]
    for j in range(N_SEQ):
        proj = contract_cols(w_ref[...], chunks[j][...]).astype(jnp.bfloat16)
        raw_ref[j] = proj[: 2 * HEAD_DIM]
        query = proj[:HEAD_DIM].astype(jnp.float32)
        keyrow = proj[HEAD_DIM : 2 * HEAD_DIM].astype(jnp.float32)
        val = proj[2 * HEAD_DIM :]
        q_unit = (query * unit_factor(query, 0)).astype(jnp.bfloat16).astype(jnp.float32) * SCALE
        k_unit = keyrow * unit_factor(keyrow, 0)
        hq_ref[j] = q_unit.astype(jnp.bfloat16)
        ku_ref[j] = k_unit.astype(jnp.bfloat16)
        v_ext[j, :HEAD_DIM] = val
        v_ext[j, HEAD_DIM:] = jnp.ones((ONES, CHUNK), jnp.bfloat16)
        kv_ref[j] = jnp.concatenate([k_unit, val.astype(jnp.float32)], axis=0).T.astype(jnp.bfloat16)
        d_head = d_ref[place_of(z, j)].astype(jnp.float32)
        qd_ref[j] = jnp.concatenate([q_unit, d_head], axis=0).T.astype(jnp.bfloat16)

    def step(i, carry):
        query = jnp.concatenate([hq_ref[i], jnp.zeros_like(hq_ref[i])], axis=0)
        out = jnp.zeros((HEAD_DIM + ONES, CHUNK), jnp.float32)
        for j in range(N_SEQ):
            exps = jnp.exp(matmul(kv_ref[j], query)).astype(jnp.bfloat16)
            out += matmul(v_ext[j], exps)
        inverse = 1.0 / out[HEAD_DIM : HEAD_DIM + 1]
        stats_ref[i, 0:1] = inverse
        out_ref[place_of(z, i)] = (out[:HEAD_DIM] * inverse).astype(jnp.bfloat16)
        return carry

    lax.fori_loop(0, N_SEQ, step, 0)
    for j in range(N_SEQ):
        out = out_ref[place_of(z, j)].astype(jnp.float32)
        d_head = d_ref[place_of(z, j)].astype(jnp.float32)
        stats_ref[j, 1:2] = jnp.sum(out * d_head, axis=0, keepdims=True)


def backward_kernel(*refs):
    place_ref = refs[0]
    chunks = refs[1:9]
    kv_ref, qd_ref, hq_ref, ku_ref, raw_ref, stats_ref = refs[9:15]
    d_ref = refs[15]
    stacks = refs[16:24]
    keep_ref, give_ref = refs[24:26]
    sums, dqt, grad_t, grad = refs[26:30]
    z = place_ref[0]
    sums[...] = jnp.zeros_like(sums)

    def step(i, carry):
        zero = jnp.zeros_like(hq_ref[i])
        query = jnp.concatenate([hq_ref[i], zero], axis=0)
        d_head = jnp.concatenate([zero, d_ref[place_of(z, i)]], axis=0)
        rows = qd_ref[i].astype(jnp.float32)
        left = lax.broadcasted_iota(jnp.int32, rows.shape, 1) < HEAD_DIM
        rhs = jnp.concatenate([jnp.where(left, 0.0, rows), jnp.where(left, rows, 0.0)], axis=0)
        rhs = rhs.astype(jnp.bfloat16)
        inverse = stats_ref[i, 0:1]
        row_dot = stats_ref[i, 1:2]
        d_qunit = jnp.zeros((HEAD_DIM, CHUNK), jnp.float32)
        for j in range(N_SEQ):
            prob = jnp.exp(matmul(kv_ref[j], query)) * inverse
            d_scores = (prob * (matmul(kv_ref[j], d_head) - row_dot)).astype(jnp.bfloat16)
            d_qunit += matmul(ku_ref[j], d_scores)
            both = jnp.concatenate([prob.astype(jnp.bfloat16), d_scores], axis=1)
            sums[j] += matmul(both, rhs)
        dqt[i] = d_qunit * SCALE
        return carry

    lax.fori_loop(0, N_SEQ, step, 0)
    for j in range(N_SEQ):
        turned = sums[j].T
        pieces = []
        for t, d_unit in enumerate((dqt[j], turned[:HEAD_DIM])):
            wide = raw_ref[j, t * HEAD_DIM : (t + 1) * HEAD_DIM].astype(jnp.float32)
            factor = unit_factor(wide, 0)
            mean = jnp.mean(d_unit * wide, axis=0, keepdims=True)
            pieces.append(factor * d_unit - factor * factor * factor * wide * mean)
        stacked = jnp.concatenate(pieces + [turned[HEAD_DIM:]], axis=0).astype(jnp.bfloat16)
        stacks[j][...] = stacked
        term = matmul(stacked, chunks[j][...])
        if j == 0:
            grad_t[: 3 * HEAD_DIM] = term
        else:
            grad_t[: 3 * HEAD_DIM] += term
    grad_t[3 * HEAD_DIM :] = jnp.zeros((HEAD_DIM, grad_t.shape[1]), jnp.float32)
    grad[...] = grad_t[...].T
    split_rows(place_ref[1], grad, keep_ref, give_ref)


def result_kernel(*refs):
    place_ref = refs[0]
    chunks = refs[1:9]
    heads_ref, w_ref, grad_ref, x_ref, act_ref, cut_ref = refs[9:15]
    out_ref, keep_ref, give_ref, grad_t, grad_msg, grad_out = refs[15:]
    z = place_ref[0]
    every = jnp.concatenate([heads_ref[h] for h in range(N_SEQ)], axis=0)
    grad_out[...] = matmul(every, grad_ref[...])
    for j in range(N_SEQ):
        columns = cut_ref[place_of(z, j)].astype(jnp.float32).T.astype(jnp.bfloat16)
        term = matmul(columns, chunks[j][...])
        if j == 0:
            grad_t[...] = term
        else:
            grad_t[...] += term
    grad_msg[...] = grad_t[...].T
    split_rows(place_ref[1], grad_msg, keep_ref, give_ref)
    split_rows(place_ref[1], grad_out, keep_ref, give_ref, grad_msg.shape[0] // (2 * N_XY))
    attn = contract_rows(every, w_ref[...])
    out_ref[...] = (x_ref[...].astype(jnp.float32) + attn + act_ref[...]).astype(jnp.bfloat16)


def pair_kernel(keep_a, got_a, keep_b, got_b, out_ref):
    cut = keep_a.shape[1]
    for i in range(N_XY):
        out_ref[i, :cut] = (keep_a[i].astype(jnp.float32) + got_a[i].astype(jnp.float32)).astype(jnp.bfloat16)
        out_ref[i, cut:] = (keep_b[i].astype(jnp.float32) + got_b[i].astype(jnp.float32)).astype(jnp.bfloat16)


def share_kernel(shares_ref, out_ref):
    total = jnp.zeros(shares_ref.shape[1:], jnp.float32)
    for i in range(N_XY):
        total += shares_ref[i].astype(jnp.float32)
    for h in range(N_SEQ):
        out_ref[h] = total.astype(jnp.bfloat16)


def finish_kernel(every_ref, w_ref, m_ref, gain_ref, qkv_ref, out_ref, msg_ref, gain_out_ref):
    rows = msg_ref.shape[0]
    hd = N_SEQ * HEAD_DIM
    nodes = N_SEQ * CHUNK
    gain_sum = jnp.zeros((rows, BLOCK), jnp.float32)
    low = slice(0, HEAD_DIM)
    high = slice(HEAD_DIM, 2 * HEAD_DIM)
    for t, (band, half) in enumerate(((0, low), (0, high), (1, low))):
        for p in range(N_SEQ // 2):
            pieces = [every_ref[h, band * rows : (band + 1) * rows, half] for h in (2 * p, 2 * p + 1)]
            block = jnp.concatenate(pieces, axis=1).astype(jnp.float32) * (1.0 / nodes)
            columns = slice(t * hd + p * BLOCK, t * hd + (p + 1) * BLOCK)
            qkv_ref[:, columns] = block
            gain_sum += block * w_ref[:, columns].astype(jnp.float32)
    total = jnp.zeros((every_ref.shape[1] - 3 * rows, BLOCK), jnp.float32)
    for h in range(N_SEQ):
        columns = slice(h * BLOCK, (h + 1) * BLOCK)
        block = every_ref[h, 2 * rows : 3 * rows].astype(jnp.float32) * (1.0 / nodes)
        msg_ref[:, columns] = block
        gain_sum += block * m_ref[:, columns].astype(jnp.float32)
        total += every_ref[h, 3 * rows :].astype(jnp.float32)
    half_rows = out_ref.shape[0]
    for t in range(N_SEQ):
        out_ref[:, t * BLOCK : (t + 1) * BLOCK] = total[t * half_rows : (t + 1) * half_rows] * (1.0 / nodes)
    gain_out_ref[...] = jnp.sum(gain_sum, axis=1, keepdims=True) / gain_ref[...]


def input_grad_kernel(*refs):
    place_ref = refs[0]
    stacks = refs[1:9]
    w_ref, d_norm_ref, x_ref, grad_ref, gain_ref = refs[9:14]
    out_ref, gathered = refs[14:]
    z = place_ref[0]
    hd = N_SEQ * HEAD_DIM
    for j in range(N_SEQ):
        head = lax.rem(z + j, N_SEQ)
        for t in range(3):
            gathered[pl.ds(t * hd + head * HEAD_DIM, HEAD_DIM), :] = stacks[j][
                t * HEAD_DIM : (t + 1) * HEAD_DIM
            ]
    d_norm = matmul(w_ref[...], gathered[...]).T + d_norm_ref[...]
    wide = x_ref[...].astype(jnp.float32)
    inv_rms = unit_factor(wide, -1)
    x_hat = wide * inv_rms
    scaled = d_norm * gain_ref[...]
    d_feat = inv_rms * (scaled - x_hat * jnp.mean(scaled * x_hat, axis=-1, keepdims=True))
    out_ref[...] = (grad_ref[...].astype(jnp.float32) + d_feat).astype(jnp.bfloat16)


def after(value, *others):
    return lax.optimization_barrier((value,) + others)[0]


def exchange(array, axis):
    return lax.all_to_all(array, axis, split_axis=0, concat_axis=0, tiled=True)


def shift(array, distance):
    return lax.ppermute(array, "z", [(i, (i + distance) % N_SEQ) for i in range(N_SEQ)])


def up(array):
    return shift(array, 1)


def down(array):
    return shift(array, -1)


def sum_over_cores(keep, give):
    got = lax.ppermute(give, "c", [(0, 1), (1, 0)])
    return (keep.astype(jnp.float32) + got.astype(jnp.float32)).astype(jnp.bfloat16)


def sum_over_chips(pair):
    return jnp.sum(exchange(pair, ("x", "y")).astype(jnp.float32), axis=0)


def on_device(
    features, out_grad, norm_gain, w_qkv, w_out, w_msg, block_ids, block_counts, edge_tiles
):
    node_rows, width = features.shape
    hd = w_out.shape[0]
    nodes = N_SEQ * node_rows
    bf16, f32 = jnp.bfloat16, jnp.float32
    z = lax.axis_index("z")
    core = lax.axis_index("c")
    place = jnp.stack([z, core]).astype(jnp.int32)
    gain = norm_gain.reshape(1, width)
    wide_shape = ((node_rows, width), f32)
    low_shape = ((node_rows, width), bf16)

    (normed,) = call(normalize_kernel, "normalize", (low_shape,), (), (features, gain), moved=1 << 20)

    a1, b1 = up(normed), down(normed)
    (d_out,) = call(
        d_out_kernel, "d_out", (((N_SEQ, HEAD_DIM, node_rows), bf16),), (), (out_grad, w_out),
        flops=2 * node_rows * width * hd, moved=2 << 20,
    )
    d_heads = exchange(d_out, "z")
    w_head = pick_head(place, w_qkv)
    a1, b1, d_heads = lax.optimization_barrier((a1, b1, d_heads))
    a2, b2 = up(a1), down(b1)

    act, to_low, mid, to_high = call(
        message_kernel, "messages", (wide_shape, low_shape, wide_shape, low_shape),
        (place, block_ids, block_counts), (a1, normed, b1, w_msg, edge_tiles, out_grad),
        [pltpu.VMEM((6, BLOCK, width), bf16), pltpu.VMEM((6, BLOCK, width), f32)],
        flops=8 * node_rows * width * width, exps=node_rows * width, moved=8 << 20,
    )
    a2, b2, w_head, to_low, to_high = lax.optimization_barrier((a2, b2, w_head, to_low, to_high))
    a3, b3 = up(a2), down(b2)
    above, below = down(to_low), up(to_high)
    a3, b3, above, below = lax.optimization_barrier((a3, b3, above, below))
    half = node_rows // 2
    c4 = (up(a3[:half]), down(b3[half:]))
    d_msg_cut, d_norm = call(
        message_grad_kernel, "message_grad", (((N_SEQ, node_rows, width // N_SEQ), bf16), wide_shape),
        (), (mid, above, below, w_msg), flops=2 * node_rows * width * width, moved=8 << 20,
    )
    *c4, d_msg_cut, d_norm = lax.optimization_barrier((*c4, d_msg_cut, d_norm))
    c4 = jnp.concatenate(c4, axis=0)
    chunks = (normed, a1, a2, a3, c4, b3, b2, b1)
    d_msg_cut = exchange(d_msg_cut, "z")

    lanes_in = ((N_SEQ, CHUNK, 2 * HEAD_DIM), bf16)
    turned = ((N_SEQ, HEAD_DIM, CHUNK), bf16)
    out_t, *saved = call(
        forward_kernel, "attend_forward",
        (turned, lanes_in, lanes_in, turned, turned,
         ((N_SEQ, 2 * HEAD_DIM, CHUNK), bf16), ((N_SEQ, 8, CHUNK), f32)),
        (place,), chunks + (w_head, d_heads),
        [pltpu.VMEM((N_SEQ, HEAD_DIM + ONES, CHUNK), bf16)],
        flops=12 * nodes * nodes * HEAD_DIM, exps=nodes * nodes, moved=8 << 20,
    )
    out_t, d_msg_cut = lax.optimization_barrier((out_t, d_msg_cut))
    heads = exchange(out_t, "z")

    rows_here = width // (2 * N_XY)
    rows_out = hd // (2 * N_XY)
    part_head = ((N_XY, 2 * rows_here, BLOCK), bf16)
    *stacks, keep, give = call(
        backward_kernel, "attend_backward",
        (((3 * HEAD_DIM, CHUNK), bf16),) * N_SEQ + (part_head, part_head),
        (place,), chunks + (*saved, d_heads),
        [
            pltpu.VMEM((N_SEQ, CHUNK, 2 * HEAD_DIM), f32),
            pltpu.VMEM((N_SEQ, HEAD_DIM, CHUNK), f32),
            pltpu.VMEM((4 * HEAD_DIM, width), f32),
            pltpu.VMEM((width, 4 * HEAD_DIM), f32),
        ],
        flops=24 * nodes * nodes * HEAD_DIM, exps=nodes * nodes, moved=8 << 20,
    )
    got = lax.ppermute(give, "c", [(0, 1), (1, 0)])

    part_out = ((N_XY, rows_here + rows_out * width // BLOCK, BLOCK), bf16)
    block_result_array, keep_out, give_out = call(
        result_kernel, "result", (low_shape, part_out, part_out), (place,),
        chunks + (after(heads, keep), w_out, out_grad, features, act, d_msg_cut),
        [pltpu.VMEM((BLOCK, width), f32), pltpu.VMEM((width, BLOCK), f32), pltpu.VMEM((hd, width), f32)],
        flops=6 * node_rows * width * width, moved=10 << 20,
    )
    got_out = lax.ppermute(give_out, "c", [(0, 1), (1, 0)])
    all_rows = part_head[0][1] + part_out[0][1]
    (pair,) = call(
        pair_kernel, "pair_sum", (((N_XY, all_rows, BLOCK), bf16),), (), (keep, got, keep_out, got_out),
        moved=3 << 20,
    )
    pair, *stacks = lax.optimization_barrier((pair, *stacks))
    shares = exchange(pair, ("x", "y"))
    stacks = [stacks[0]] + [shift(stacks[j], -j) for j in range(1, N_SEQ)]
    (mine,) = call(
        share_kernel, "share_sum", (((N_SEQ, all_rows, BLOCK), bf16),), (), (shares,), moved=2 << 20,
    )
    every = exchange(mine, "z")

    (grad_input,) = call(
        input_grad_kernel, "input_grad", (low_shape,), (place,),
        (*stacks, w_qkv, d_norm, features, out_grad, gain),
        [pltpu.VMEM((3 * hd, node_rows), bf16)],
        flops=6 * node_rows * width * hd, moved=8 << 20,
    )

    first = ((lax.axis_index("x") * 4 + lax.axis_index("y")) * 2 + core) * rows_here
    w_rows = lax.dynamic_slice_in_dim(w_qkv, first, rows_here, 0)
    m_rows = lax.dynamic_slice_in_dim(w_msg, first, rows_here, 0)
    gain_rows = lax.dynamic_slice_in_dim(norm_gain, first, rows_here, 0).reshape(rows_here, 1)
    grad_qkv, grad_out, grad_msg, grad_gain = call(
        finish_kernel, "finish",
        (((rows_here, 3 * hd), f32), ((rows_out, width), f32), ((rows_here, width), f32), ((rows_here, 1), f32)),
        (), (every, w_rows, m_rows, gain_rows), moved=2 << 20,
    )
    return block_result_array, grad_input, grad_gain.reshape(rows_here), grad_qkv, grad_out, grad_msg


def solution(mesh):
    fine = Mesh(mesh.devices.reshape(4, 4, 2, N_SEQ), ("x", "y", "c", "z"))
    dp = ("x", "y", "c")
    rows = ("x", "y", "c", "z")
    return jax.shard_map(
        on_device,
        mesh=fine,
        in_specs=(
            P(rows, None),
            P(rows, None),
            P(),
            P(),
            P(),
            P(),
            P(rows, None),
            P(rows),
            P(rows, None, None, None),
        ),
        out_specs=(
            P(rows, None),
            P(rows, None),
            P(dp),
            P(dp, None),
            P(dp, None),
            P(dp, None),
        ),
        check_vma=False,
    )
```

profile of v0, /device:TPU:6, one launch (start us, length us, event | category | flops | bytes accessed | tf_op | source)
XLA Modules:
  0.0 212.3 jit_solution(13446745165782342167)
XLA Ops:
  4.6 4.0 %collective-permute-start.1 = (bf16[256,1024]{1,0:T(8,128)(2,1)S(1)}, bf16[256,1024]{1,0:T(8,128)(2,1)S(1)}, u32[]{:S(2)}, u32[]{:S(2)}) collective-permute-start(bf16[256,1024]{1,0:T(8,128)(2,1)S(1)} %normalize.1.refs_4_.refs_1_), channel_id=1, source_target_pairs={{0,7},{1,0},{2,1},{3,2},{4,3},{5,4},{6,5},{7,6},{8,15},{9,8},{10,9... | collective-permute-start | bytes 1572872 | tf_op jit(solution)/shard_map/ppermute | solution.py:344
  11.3 15.4 %all_to_all.25.refs_10_.refs_15_ = bf16[8,64,256]{2,1,0:T(8,128)(2,1)} all-to-all(bf16[8,64,256]{2,1,0:T(8,128)(2,1)S(1)} %d_out.1), channel_id=1, replica_groups=mesh['x'=4,'y'=4,'c'=2,'z'=8] {'z'}, dimensions={0} | all-to-all | bytes 524288 | tf_op jit(solution)/shard_map/all_to_all | solution.py:340
  26.8 4.0 %collective-permute-start.2 = (bf16[256,1024]{1,0:T(8,128)(2,1)S(1)}, bf16[256,1024]{1,0:T(8,128)(2,1)S(1)}, u32[]{:S(2)}, u32[]{:S(2)}) collective-permute-start(bf16[256,1024]{1,0:T(8,128)(2,1)S(1)} %collective-permute-done.refs_3_.refs_2_), channel_id=1, source_target_pairs={{0,1},{1,2},{2,3},{3,4},{4,5},{5,6},{6,7},{7,0},{8,9},{9,10},{10,1... | collective-permute-start | bytes 1572872 | tf_op jit(solution)/shard_map/ppermute | solution.py:344
  31.4 3.1 %pick_head.1.refs_9_ = bf16[192,1024]{1,0:T(8,128)(2,1)} custom-call(s32[2]{0:T(128)} %pad_add_fusion.place_ref.refs_0_, bf16[1024,1536]{1,0:T(8,128)(2,1)} %refs_9_.1, bf16[1024,1536]{1,0:T(8,128)(2,1)} %refs_9_.1, bf16[1024,1536]{1,0:T(8,128)(2,1)} %refs_9_.1), custom_call_target="tpu_custom_call" | custom-call | bytes 4194304 | tf_op jit(solution)/shard_map/pick_head/pallas_call | solution.py:84
  34.6 6.4 %messages.1 = (f32[256,1024]{1,0:T(8,128)}, bf16[256,1024]{1,0:T(8,128)(2,1)S(1)}, f32[256,1024]{1,0:T(8,128)}, bf16[256,1024]{1,0:T(8,128)(2,1)S(1)}) custom-call(s32[2]{0:T(128)S(1)} %copy-done.30, s32[2,4]{1,0:T(2,128)S(1)} %copy-done.39, s32[2]{0:T(128)S(1)} %copy-done.40, bf16[256,1024]{1,0:T(8,128)(2,1)S(1)} %collective-permute-done.refs_3_.refs_2_, ...), custom_call_target="tpu_custom_call" | custom-call | flops 2147483648 | bytes 8388608 | tf_op jit(solution)/shard_map/messages/pallas_call | solution.py:45
  41.0 2.1 collective-permute-start.4
  46.3 10.8 %collective-permute-done.4.refs_4_ = bf16[256,1024]{1,0:T(8,128)(2,1)S(1)} collective-permute-done((bf16[256,1024]{1,0:T(8,128)(2,1)S(1)}, bf16[256,1024]{1,0:T(8,128)(2,1)S(1)}, u32[]{:S(2)}, u32[]{:S(2)}) %collective-permute-start.4) | collective-permute-done | bytes 524320 | tf_op jit(solution)/shard_map/ppermute | solution.py:344
  58.0 6.3 %collective-permute-done.6.refs_1_ = bf16[256,1024]{1,0:T(8,128)(2,1)S(1)} collective-permute-done((bf16[256,1024]{1,0:T(8,128)(2,1)S(1)}, bf16[256,1024]{1,0:T(8,128)(2,1)S(1)}, u32[]{:S(2)}, u32[]{:S(2)}) %collective-permute-start.6) | collective-permute-done | bytes 524320 | tf_op jit(solution)/shard_map/ppermute | solution.py:344
  64.3 2.5 %collective-permute-start.8 = (bf16[128,1024]{1,0:T(8,128)(2,1)S(1)}, bf16[128,1024]{1,0:T(8,128)(2,1)}, u32[]{:S(2)}, u32[]{:S(2)}) collective-permute-start(bf16[128,1024]{1,0:T(8,128)(2,1)S(1)} %slice.6), channel_id=1, source_target_pairs={{0,1},{1,2},{2,3},{3,4},{4,5},{5,6},{6,7},{7,0},{8,9},{9,10},{10,1... | collective-permute-start | bytes 786440 | tf_op jit(solution)/shard_map/ppermute | solution.py:344
  69.1 2.8 %message_grad.1 = (bf16[8,256,128]{2,1,0:T(8,128)(2,1)}, f32[256,1024]{1,0:T(8,128)S(1)}) custom-call(f32[256,1024]{1,0:T(8,128)S(1)} %copy-done.12, bf16[256,1024]{1,0:T(8,128)(2,1)S(1)} %collective-permute-done.6.refs_1_, bf16[256,1024]{1,0:T(8,128)(2,1)S(1)} %collective-permute-done.7.refs_2_, bf16[1024,1024]{1,0:T(8,128)(2,1)} %refs_3_.1), custom_call_target="tpu_custom_call" | custom-call | flops 536870912 | bytes 8388608 | tf_op jit(solution)/shard_map/message_grad/pallas_call | solution.py:45
  73.5 5.2 %all-to-all-start.1 = ((bf16[8,256,128]{2,1,0:T(8,128)(2,1)}), bf16[8,256,128]{2,1,0:T(8,128)(2,1)}, u32[]{:S(2)}, u32[]{:S(2)}) async-start(bf16[8,256,128]{2,1,0:T(8,128)(2,1)} %get-tuple-element.84), calls=%async_computation.1 | async-start | bytes 1048576 | tf_op jit(solution)/shard_map/all_to_all | solution.py:340
  82.5 11.2 %attend_forward.1 = (bf16[8,64,256]{2,1,0:T(8,128)(2,1)}, bf16[8,256,128]{2,1,0:T(8,128)(2,1)S(1)}, bf16[8,256,128]{2,1,0:T(8,128)(2,1)S(1)}, bf16[8,64,256]{2,1...) custom-call(s32[2]{0:T(128)S(1)} %copy-done.30, ...), custom_call_target="tpu_custom_call" | custom-call | flops 3221225472 | bytes 8388608 | tf_op jit(solution)/shard_map/attend_forward/pallas_call | solution.py:45
  97.6 7.2 %all-to-all-start.2 = ((bf16[8,64,256]{2,1,0:T(8,128)(2,1)}), bf16[8,64,256]{2,1,0:T(8,128)(2,1)S(1)}, u32[]{:S(2)}, u32[]{:S(2)}) async-start(bf16[8,64,256]{2,1,0:T(8,128)(2,1)} %get-tuple-element.85), calls=%async_computation.2 | async-start | bytes 524288 | tf_op jit(solution)/shard_map/all_to_all | solution.py:340
  110.6 22.0 %attend_backward.1 = (bf16[192,256]{1,0:T(8,128)(2,1)S(1)}, bf16[192,256]{1,0:T(8,128)(2,1)S(1)}, bf16[192,256]{1,0:T(8,128)(2,1)S(1)}, bf16[192,256]{1,0:T(8,12...) custom-call(s32[2]{0:T(128)S(1)} %copy-done.30, ...), custom_call_target="tpu_custom_call" | custom-call | flops 6442450944 | bytes 8388608 | tf_op jit(solution)/shard_map/attend_backward/pallas_call | solution.py:45
  139.0 4.6 %result.1 = (bf16[256,1024]{1,0:T(8,128)(2,1)}, bf16[16,160,128]{2,1,0:T(8,128)(2,1)}, bf16[16,160,128]{2,1,0:T(8,128)(2,1)}) custom-call(s32[2]{0:T(128)S(1)} %copy-done.30, bf16[256,1024]{1,0:T(8,128)(2,1)S(1)} %normalize.1.refs_4_.refs_1_, bf16[256,1024]{1,0:T(8,128)(2,1)S(1)} %copy-done.16, bf16[256,1024]{1,0:T(8,128)(2,1)S(1)} %copy-done.20, ...), custom_call_target="tpu_custom_call" | custom-call | flops 1610612736 | bytes 10485760 | tf_op jit(solution)/shard_map/result/pallas_call | solution.py:45
  147.5 21.2 %all_to_all.26.shares_ref = bf16[16,224,128]{2,1,0:T(8,128)(2,1)S(1)} all-to-all(bf16[16,224,128]{2,1,0:T(8,128)(2,1)S(1)} %pair_sum.1), channel_id=1, replica_groups=mesh['x'=4,'y'=4,'c'=2,'z'=8] {'x','y'}, dimensions={0} | all-to-all | bytes 1835008 | tf_op jit(solution)/shard_map/all_to_all | solution.py:340
  169.7 7.2 %all-to-all-start.4 = ((bf16[8,224,128]{2,1,0:T(8,128)(2,1)}), bf16[8,224,128]{2,1,0:T(8,128)(2,1)S(1)}, u32[]{:S(2)}, u32[]{:S(2)}) async-start(bf16[8,224,128]{2,1,0:T(8,128)(2,1)} %share_sum.1), calls=%async_computation.4 | async-start | bytes 917504 | tf_op jit(solution)/shard_map/all_to_all | solution.py:340
  177.8 3.3 %collective-permute-start.12 = (bf16[192,256]{1,0:T(8,128)(2,1)S(1)}, bf16[192,256]{1,0:T(8,128)(2,1)S(1)}, u32[]{:S(2)}, u32[]{:S(2)}) collective-permute-start(bf16[192,256]{1,0:T(8,128)(2,1)S(1)} %copy-done.38), channel_id=1, source_target_pairs={{0,7},{1,0},{2,1},{3,2},{4,3},{5,4},{6,5},{7,6},{8,15},{9,8},{10,9... | collective-permute-start | bytes 294920 | tf_op jit(solution)/shard_map/ppermute | solution.py:344
  181.1 2.4 %collective-permute-start.13 = (bf16[192,256]{1,0:T(8,128)(2,1)S(1)}, bf16[192,256]{1,0:T(8,128)(2,1)S(1)}, u32[]{:S(2)}, u32[]{:S(2)}) collective-permute-start(bf16[192,256]{1,0:T(8,128)(2,1)S(1)} %copy-done.36), channel_id=1, source_target_pairs={{0,6},{1,7},{2,0},{3,1},{4,2},{5,3},{6,4},{7,5},{8,14},{9,15},{10,... | collective-permute-start | bytes 294920 | tf_op jit(solution)/shard_map/ppermute | solution.py:344
  185.1 3.6 %collective-permute-start.15 = (bf16[192,256]{1,0:T(8,128)(2,1)}, bf16[192,256]{1,0:T(8,128)(2,1)S(1)}, u32[]{:S(2)}, u32[]{:S(2)}) collective-permute-start(bf16[192,256]{1,0:T(8,128)(2,1)} %get-tuple-element.112), channel_id=1, source_target_pairs={{0,4},{1,5},{2,6},{3,7},{4,0},{5,1},{6,2},{7,3},{8,12},{9,13},{10,... | collective-permute-start | bytes 294920 | tf_op jit(solution)/shard_map/ppermute | solution.py:344
  188.9 5.4 %collective-permute-done.12.refs_2_ = bf16[192,256]{1,0:T(8,128)(2,1)S(1)} collective-permute-done((bf16[192,256]{1,0:T(8,128)(2,1)S(1)}, bf16[192,256]{1,0:T(8,128)(2,1)S(1)}, u32[]{:S(2)}, u32[]{:S(2)}) %collective-permute-start.12) | collective-permute-done | bytes 98336 | tf_op jit(solution)/shard_map/ppermute | solution.py:344
  195.8 3.3 %collective-permute-done.13.refs_3_ = bf16[192,256]{1,0:T(8,128)(2,1)S(1)} collective-permute-done((bf16[192,256]{1,0:T(8,128)(2,1)S(1)}, bf16[192,256]{1,0:T(8,128)(2,1)S(1)}, u32[]{:S(2)}, u32[]{:S(2)}) %collective-permute-start.13) | collective-permute-done | bytes 98336 | tf_op jit(solution)/shard_map/ppermute | solution.py:344
  203.0 2.6 %collective-permute-done.17.refs_7_ = bf16[192,256]{1,0:T(8,128)(2,1)S(1)} collective-permute-done((bf16[192,256]{1,0:T(8,128)(2,1)}, bf16[192,256]{1,0:T(8,128)(2,1)S(1)}, u32[]{:S(2)}, u32[]{:S(2)}) %collective-permute-start.17) | collective-permute-done | bytes 98336 | tf_op jit(solution)/shard_map/ppermute | solution.py:344
  206.8 4.1 %input_grad.1 = bf16[256,1024]{1,0:T(8,128)(2,1)} custom-call(s32[2]{0:T(128)S(1)} %copy-done.30, bf16[192,256]{1,0:T(8,128)(2,1)S(1)} %get-tuple-element.108.refs_1_, bf16[192,256]{1,0:T(8,128)(2,1)S(1)} %collective-permute-done.12.refs_2_, bf16[192,256]{1,0:T(8,128)(2,1)S(1)} %collective-permute-done.13.refs_3_, ...), custom_call_target="tpu_custom_call" | custom-call | flops 805306368 | bytes 8388608 | tf_op jit(solution)/shard_map/input_grad/pallas_call | solution.py:45
  (144 shorter events, 50.7 us)
Async XLA Ops:
  2.6 24.2 %collective-permute-start = (bf16[256,1024]{1,0:T(8,128)(2,1)S(1)}, bf16[256,1024]{1,0:T(8,128)(2,1)S(1)}, u32[]{:S(2)}, u32[]{:S(2)}) collective-permute-start(bf16[256,1024]{1,0:T(8,128)(2,1)S(1)} %normalize.1.refs_4_.refs_1_), channel_id=1, source_target_pairs={{0,1},{1,2},{2,3},{3,4},{4,5},{5,6},{6,7},{7,0},{8,9},{9,10},{10,1... | collective-permute-start | bytes 1572872 | tf_op jit(solution)/shard_map/ppermute | solution.py:344
  4.6 22.2 %collective-permute-start.1 = (bf16[256,1024]{1,0:T(8,128)(2,1)S(1)}, bf16[256,1024]{1,0:T(8,128)(2,1)S(1)}, u32[]{:S(2)}, u32[]{:S(2)}) collective-permute-start(bf16[256,1024]{1,0:T(8,128)(2,1)S(1)} %normalize.1.refs_4_.refs_1_), channel_id=1, source_target_pairs={{0,7},{1,0},{2,1},{3,2},{4,3},{5,4},{6,5},{7,6},{8,15},{9,8},{10,9... | collective-permute-start | bytes 1572872 | tf_op jit(solution)/shard_map/ppermute | solution.py:344
  26.8 14.2 %collective-permute-start.2 = (bf16[256,1024]{1,0:T(8,128)(2,1)S(1)}, bf16[256,1024]{1,0:T(8,128)(2,1)S(1)}, u32[]{:S(2)}, u32[]{:S(2)}) collective-permute-start(bf16[256,1024]{1,0:T(8,128)(2,1)S(1)} %collective-permute-done.refs_3_.refs_2_), channel_id=1, source_target_pairs={{0,1},{1,2},{2,3},{3,4},{4,5},{5,6},{6,7},{7,0},{8,9},{9,10},{10,1... | collective-permute-start | bytes 1572872 | tf_op jit(solution)/shard_map/ppermute | solution.py:344
  30.8 10.2 %collective-permute-start.3 = (bf16[256,1024]{1,0:T(8,128)(2,1)S(1)}, bf16[256,1024]{1,0:T(8,128)(2,1)S(1)}, u32[]{:S(2)}, u32[]{:S(2)}) collective-permute-start(bf16[256,1024]{1,0:T(8,128)(2,1)S(1)} %collective-permute-done.1.refs_5_.refs_8_), channel_id=1, source_target_pairs={{0,7},{1,0},{2,1},{3,2},{4,3},{5,4},{6,5},{7,6},{8,15},{9,8},{10,9... | collective-permute-start | bytes 1572872 | tf_op jit(solution)/shard_map/ppermute | solution.py:344
  41.0 16.1 %collective-permute-start.4 = (bf16[256,1024]{1,0:T(8,128)(2,1)S(1)}, bf16[256,1024]{1,0:T(8,128)(2,1)S(1)}, u32[]{:S(2)}, u32[]{:S(2)}) collective-permute-start(bf16[256,1024]{1,0:T(8,128)(2,1)S(1)} %collective-permute-done.2.refs_3_), channel_id=1, source_target_pairs={{0,1},{1,2},{2,3},{3,4},{4,5},{5,6},{6,7},{7,0},{8,9},{9,10},{10,1... | collective-permute-start | bytes 1572872 | tf_op jit(solution)/shard_map/ppermute | solution.py:344
  43.1 14.9 %collective-permute-start.5 = (bf16[256,1024]{1,0:T(8,128)(2,1)S(1)}, bf16[256,1024]{1,0:T(8,128)(2,1)S(1)}, u32[]{:S(2)}, u32[]{:S(2)}) collective-permute-start(bf16[256,1024]{1,0:T(8,128)(2,1)S(1)} %collective-permute-done.3.refs_7_), channel_id=1, source_target_pairs={{0,7},{1,0},{2,1},{3,2},{4,3},{5,4},{6,5},{7,6},{8,15},{9,8},{10,9... | collective-permute-start | bytes 1572872 | tf_op jit(solution)/shard_map/ppermute | solution.py:344
  44.3 20.0 %collective-permute-start.6 = (bf16[256,1024]{1,0:T(8,128)(2,1)S(1)}, bf16[256,1024]{1,0:T(8,128)(2,1)S(1)}, u32[]{:S(2)}, u32[]{:S(2)}) collective-permute-start(bf16[256,1024]{1,0:T(8,128)(2,1)S(1)} %get-tuple-element.70), channel_id=1, source_target_pairs={{0,7},{1,0},{2,1},{3,2},{4,3},{5,4},{6,5},{7,6},{8,15},{9,8},{10,9... | collective-permute-start | bytes 1572872 | tf_op jit(solution)/shard_map/ppermute | solution.py:344
  44.5 19.8 %collective-permute-start.7 = (bf16[256,1024]{1,0:T(8,128)(2,1)S(1)}, bf16[256,1024]{1,0:T(8,128)(2,1)S(1)}, u32[]{:S(2)}, u32[]{:S(2)}) collective-permute-start(bf16[256,1024]{1,0:T(8,128)(2,1)S(1)} %get-tuple-element.71), channel_id=1, source_target_pairs={{0,1},{1,2},{2,3},{3,4},{4,5},{5,6},{6,7},{7,0},{8,9},{9,10},{10,1... | collective-permute-start | bytes 1572872 | tf_op jit(solution)/shard_map/ppermute | solution.py:344
  64.3 7.8 %collective-permute-start.8 = (bf16[128,1024]{1,0:T(8,128)(2,1)S(1)}, bf16[128,1024]{1,0:T(8,128)(2,1)}, u32[]{:S(2)}, u32[]{:S(2)}) collective-permute-start(bf16[128,1024]{1,0:T(8,128)(2,1)S(1)} %slice.6), channel_id=1, source_target_pairs={{0,1},{1,2},{2,3},{3,4},{4,5},{5,6},{6,7},{7,0},{8,9},{9,10},{10,1... | collective-permute-start | bytes 786440 | tf_op jit(solution)/shard_map/ppermute | solution.py:344
  66.8 6.7 %collective-permute-start.9 = (bf16[128,1024]{1,0:T(8,128)(2,1)S(1)}, bf16[128,1024]{1,0:T(8,128)(2,1)}, u32[]{:S(2)}, u32[]{:S(2)}) collective-permute-start(bf16[128,1024]{1,0:T(8,128)(2,1)S(1)} %slice.7), channel_id=1, source_target_pairs={{0,7},{1,0},{2,1},{3,2},{4,3},{5,4},{6,5},{7,6},{8,15},{9,8},{10,9... | collective-permute-start | bytes 786440 | tf_op jit(solution)/shard_map/ppermute | solution.py:344
  73.5 24.0 %all-to-all-start.1 = ((bf16[8,256,128]{2,1,0:T(8,128)(2,1)}), bf16[8,256,128]{2,1,0:T(8,128)(2,1)}, u32[]{:S(2)}, u32[]{:S(2)}) async-start(bf16[8,256,128]{2,1,0:T(8,128)(2,1)} %get-tuple-element.84), calls=%async_computation.1 | async-start | bytes 1048576 | tf_op jit(solution)/shard_map/all_to_all | solution.py:340
  97.6 38.3 %all-to-all-start.2 = ((bf16[8,64,256]{2,1,0:T(8,128)(2,1)}), bf16[8,64,256]{2,1,0:T(8,128)(2,1)S(1)}, u32[]{:S(2)}, u32[]{:S(2)}) async-start(bf16[8,64,256]{2,1,0:T(8,128)(2,1)} %get-tuple-element.85), calls=%async_computation.2 | async-start | bytes 524288 | tf_op jit(solution)/shard_map/all_to_all | solution.py:340
  143.7 2.5 %collective-permute-start.11 = (bf16[16,160,128]{2,1,0:T(8,128)(2,1)}, bf16[16,160,128]{2,1,0:T(8,128)(2,1)S(1)}, u32[]{:S(2)}, u32[]{:S(2)}) collective-permute-start(bf16[16,160,128]{2,1,0:T(8,128)(2,1)} %get-tuple-element.99), channel_id=1, source_target_pairs={{0,8},{8,0},{1,9},{9,1},{2,10},{10,2},{3,11},{11,3},{4,12},{12,4},... | collective-permute-start | bytes 1966088 | tf_op jit(solution)/shard_map/ppermute | solution.py:448
  143.7 2.5 %collective-permute-start.10 = (bf16[16,64,128]{2,1,0:T(8,128)(2,1)S(1)}, bf16[16,64,128]{2,1,0:T(8,128)(2,1)S(1)}, u32[]{:S(2)}, u32[]{:S(2)}) collective-permute-start(bf16[16,64,128]{2,1,0:T(8,128)(2,1)S(1)} %copy-done.33), channel_id=1, source_target_pairs={{0,8},{8,0},{1,9},{9,1},{2,10},{10,2},{3,11},{11,3},{4,12},{12,4},... | collective-permute-start | bytes 786440 | tf_op jit(solution)/shard_map/ppermute | solution.py:439
  147.2 59.5 %copy-start.2 = (bf16[256,1024]{1,0:T(8,128)(2,1)S(1)}, bf16[256,1024]{1,0:T(8,128)(2,1)}, u32[]{:S(2)}) copy-start(bf16[256,1024]{1,0:T(8,128)(2,1)} %refs_12_.3) | copy-start | bytes 1572868
  147.3 59.5 %copy-start.4 = (bf16[256,1024]{1,0:T(8,128)(2,1)S(1)}, bf16[256,1024]{1,0:T(8,128)(2,1)}, u32[]{:S(2)}) copy-start(bf16[256,1024]{1,0:T(8,128)(2,1)} %refs_11_.3) | copy-start | bytes 1572868
  169.7 41.2 %all-to-all-start.4 = ((bf16[8,224,128]{2,1,0:T(8,128)(2,1)}), bf16[8,224,128]{2,1,0:T(8,128)(2,1)S(1)}, u32[]{:S(2)}, u32[]{:S(2)}) async-start(bf16[8,224,128]{2,1,0:T(8,128)(2,1)} %share_sum.1), calls=%async_computation.4 | async-start | bytes 917504 | tf_op jit(solution)/shard_map/all_to_all | solution.py:340
  177.8 16.5 %collective-permute-start.12 = (bf16[192,256]{1,0:T(8,128)(2,1)S(1)}, bf16[192,256]{1,0:T(8,128)(2,1)S(1)}, u32[]{:S(2)}, u32[]{:S(2)}) collective-permute-start(bf16[192,256]{1,0:T(8,128)(2,1)S(1)} %copy-done.38), channel_id=1, source_target_pairs={{0,7},{1,0},{2,1},{3,2},{4,3},{5,4},{6,5},{7,6},{8,15},{9,8},{10,9... | collective-permute-start | bytes 294920 | tf_op jit(solution)/shard_map/ppermute | solution.py:344
  181.1 18.0 %collective-permute-start.13 = (bf16[192,256]{1,0:T(8,128)(2,1)S(1)}, bf16[192,256]{1,0:T(8,128)(2,1)S(1)}, u32[]{:S(2)}, u32[]{:S(2)}) collective-permute-start(bf16[192,256]{1,0:T(8,128)(2,1)S(1)} %copy-done.36), channel_id=1, source_target_pairs={{0,6},{1,7},{2,0},{3,1},{4,2},{5,3},{6,4},{7,5},{8,14},{9,15},{10,... | collective-permute-start | bytes 294920 | tf_op jit(solution)/shard_map/ppermute | solution.py:344
  183.6 18.4 %collective-permute-start.14 = (bf16[192,256]{1,0:T(8,128)(2,1)}, bf16[192,256]{1,0:T(8,128)(2,1)S(1)}, u32[]{:S(2)}, u32[]{:S(2)}) collective-permute-start(bf16[192,256]{1,0:T(8,128)(2,1)} %get-tuple-element.111), channel_id=1, source_target_pairs={{0,5},{1,6},{2,7},{3,0},{4,1},{5,2},{6,3},{7,4},{8,13},{9,14},{10,... | collective-permute-start | bytes 294920 | tf_op jit(solution)/shard_map/ppermute | solution.py:344
  185.1 16.9 %collective-permute-start.15 = (bf16[192,256]{1,0:T(8,128)(2,1)}, bf16[192,256]{1,0:T(8,128)(2,1)S(1)}, u32[]{:S(2)}, u32[]{:S(2)}) collective-permute-start(bf16[192,256]{1,0:T(8,128)(2,1)} %get-tuple-element.112), channel_id=1, source_target_pairs={{0,4},{1,5},{2,6},{3,7},{4,0},{5,1},{6,2},{7,3},{8,12},{9,13},{10,... | collective-permute-start | bytes 294920 | tf_op jit(solution)/shard_map/ppermute | solution.py:344
  188.6 14.4 %collective-permute-start.16 = (bf16[192,256]{1,0:T(8,128)(2,1)}, bf16[192,256]{1,0:T(8,128)(2,1)S(1)}, u32[]{:S(2)}, u32[]{:S(2)}) collective-permute-start(bf16[192,256]{1,0:T(8,128)(2,1)} %get-tuple-element.113), channel_id=1, source_target_pairs={{0,3},{1,4},{2,5},{3,6},{4,7},{5,0},{6,1},{7,2},{8,11},{9,12},{10,... | collective-permute-start | bytes 294920 | tf_op jit(solution)/shard_map/ppermute | solution.py:344
  194.3 11.4 %collective-permute-start.17 = (bf16[192,256]{1,0:T(8,128)(2,1)}, bf16[192,256]{1,0:T(8,128)(2,1)S(1)}, u32[]{:S(2)}, u32[]{:S(2)}) collective-permute-start(bf16[192,256]{1,0:T(8,128)(2,1)} %get-tuple-element.114), channel_id=1, source_target_pairs={{0,2},{1,3},{2,4},{3,5},{4,6},{5,7},{6,0},{7,1},{8,10},{9,11},{10,... | collective-permute-start | bytes 294920 | tf_op jit(solution)/shard_map/ppermute | solution.py:344
  199.0 7.7 %collective-permute-start.18 = (bf16[192,256]{1,0:T(8,128)(2,1)}, bf16[192,256]{1,0:T(8,128)(2,1)S(1)}, u32[]{:S(2)}, u32[]{:S(2)}) collective-permute-start(bf16[192,256]{1,0:T(8,128)(2,1)} %copy-done.34), channel_id=1, source_target_pairs={{0,1},{1,2},{2,3},{3,4},{4,5},{5,6},{6,7},{7,0},{8,9},{9,10},{10,1... | collective-permute-start | bytes 294920 | tf_op jit(solution)/shard_map/ppermute | solution.py:344
  (48 other events, 349.1 us)
where the time goes:
time: 215 us; the launch traced here: 212 us
  Pallas kernels  56.8 us (26%)
  starting transfers between devices  51.6 us (24%)
  waiting for transfers between devices  37.1 us (17%)
  blocking collectives  36.7 us (17%)
  local copies, waits for them, and re-layouts  28.1 us (13%)
    pallas_call x11, Pallas kernels, call(): pl.pallas_call(kernel, out_shape=tuple((jax.ShapeDtypeStruct(s, t) for s,...  53.8 us
    all_to_all x2, blocking collectives, exchange(): return lax.all_to_all(array, axis, split_axis=0, concat_axis=0, tiled=True)  36.7 us
    ppermute x17, waiting for transfers between devices, shift(): lax.ppermute(array, 'z', [(i, (i + distance) % N_SEQ) for i in range(N_SE...  35.1 us
    ppermute x17, starting transfers between devices, shift(): lax.ppermute(array, 'z', [(i, (i + distance) % N_SEQ) for i in range(N_SE...  31.4 us
    unnamed x101, local copies, waits for them, and re-layouts  25.2 us
    all_to_all x3, starting transfers between devices, exchange(): return lax.all_to_all(array, axis, split_axis=0, concat_axis=0, tiled=True)  19.6 us
  transfers between devices with their start and end apart: 22, of which 12 were waited for; matrix products, arithmetic and copies ran while one was open for 2% of the time, Pallas kernels for 24%

commit v1 on v0

--- a/solution.py
+++ b/solution.py
@@ -48,7 +48,7 @@
         in_specs=specs,
         out_specs=tuple(pl.BlockSpec(memory_space=pltpu.VMEM) for _ in out_shape),
         scratch_shapes=list(scratch),
-        compiler_params=pltpu.CompilerParams(vmem_limit_bytes=50 * 1024 * 1024),
+        compiler_params=pltpu.CompilerParams(vmem_limit_bytes=24 * 1024 * 1024),
         cost_estimate=pl.CostEstimate(flops=flops, bytes_accessed=moved, transcendentals=exps),
         name=name,
     )(*scalars, *arrays)
@@ -146,7 +146,8 @@
     total = mid_ref[...] + above_ref[...].astype(jnp.float32) + below_ref[...].astype(jnp.float32)
     d_msg = total.astype(jnp.bfloat16)
     for t in range(N_SEQ):
-        cut_ref[t] = d_msg[:, t * BLOCK : (t + 1) * BLOCK]
+        columns = d_msg[:, t * BLOCK : (t + 1) * BLOCK]
+        cut_ref[t] = jnp.concatenate([columns[:BLOCK], columns[BLOCK:]], axis=1)
     d_norm_ref[...] = contract_cols(d_msg, w_ref[...])
 
 
@@ -154,14 +155,26 @@
     return lax.rem(z - j + N_SEQ, N_SEQ)
 
 
+def read_chunks(refs):
+    def whole(ref):
+        return lambda: ref[...]
+
+    def halves():
+        return jnp.concatenate([refs[4][...], refs[5][...]], axis=0)
+
+    return [whole(ref) for ref in refs[:4]] + [halves] + [whole(ref) for ref in refs[6:9]]
+
+
 def forward_kernel(*refs):
     z = refs[0][0]
-    chunks = refs[1:9]
-    w_ref, d_ref = refs[9:11]
-    out_ref, kv_ref, qd_ref, hq_ref, ku_ref, raw_ref, stats_ref = refs[11:18]
-    v_ext = refs[18]
+    chunks = read_chunks(refs[1:10])
+    w_ref, cut_ref = refs[10:12]
+    send_ref, kv_ref, hq_ref, ku_ref, raw_ref, out_ref, stats_ref = refs[12:19]
+    v_ext = refs[19]
+    for h in range(N_SEQ):
+        send_ref[h, HEAD_DIM:] = cut_ref[h]
     for j in range(N_SEQ):
-        proj = contract_cols(w_ref[...], chunks[j][...]).astype(jnp.bfloat16)
+        proj = contract_cols(w_ref[...], chunks[j]()).astype(jnp.bfloat16)
         raw_ref[j] = proj[: 2 * HEAD_DIM]
         query = proj[:HEAD_DIM].astype(jnp.float32)
         keyrow = proj[HEAD_DIM : 2 * HEAD_DIM].astype(jnp.float32)
@@ -173,8 +186,6 @@
         v_ext[j, :HEAD_DIM] = val
         v_ext[j, HEAD_DIM:] = jnp.ones((ONES, CHUNK), jnp.bfloat16)
         kv_ref[j] = jnp.concatenate([k_unit, val.astype(jnp.float32)], axis=0).T.astype(jnp.bfloat16)
-        d_head = d_ref[place_of(z, j)].astype(jnp.float32)
-        qd_ref[j] = jnp.concatenate([q_unit, d_head], axis=0).T.astype(jnp.bfloat16)
 
     def step(i, carry):
         query = jnp.concatenate([hq_ref[i], jnp.zeros_like(hq_ref[i])], axis=0)
@@ -184,37 +195,36 @@
             out += matmul(v_ext[j], exps)
         inverse = 1.0 / out[HEAD_DIM : HEAD_DIM + 1]
         stats_ref[i, 0:1] = inverse
-        out_ref[place_of(z, i)] = (out[:HEAD_DIM] * inverse).astype(jnp.bfloat16)
+        head_out = (out[:HEAD_DIM] * inverse).astype(jnp.bfloat16)
+        out_ref[i] = head_out
+        send_ref[place_of(z, i), :HEAD_DIM] = head_out
         return carry
 
     lax.fori_loop(0, N_SEQ, step, 0)
-    for j in range(N_SEQ):
-        out = out_ref[place_of(z, j)].astype(jnp.float32)
-        d_head = d_ref[place_of(z, j)].astype(jnp.float32)
-        stats_ref[j, 1:2] = jnp.sum(out * d_head, axis=0, keepdims=True)
 
 
 def backward_kernel(*refs):
     place_ref = refs[0]
-    chunks = refs[1:9]
-    kv_ref, qd_ref, hq_ref, ku_ref, raw_ref, stats_ref = refs[9:15]
-    d_ref = refs[15]
-    stacks = refs[16:24]
-    keep_ref, give_ref = refs[24:26]
-    sums, dqt, grad_t, grad = refs[26:30]
+    chunks = read_chunks(refs[1:10])
+    kv_ref, hq_ref, ku_ref, raw_ref, head_ref, stats_ref, d_ref = refs[10:17]
+    stacks = refs[17:25]
+    keep_ref, give_ref = refs[25:27]
+    sums, dqt, grad_t, grad = refs[27:31]
     z = place_ref[0]
     sums[...] = jnp.zeros_like(sums)
 
     def step(i, carry):
         zero = jnp.zeros_like(hq_ref[i])
         query = jnp.concatenate([hq_ref[i], zero], axis=0)
-        d_head = jnp.concatenate([zero, d_ref[place_of(z, i)]], axis=0)
-        rows = qd_ref[i].astype(jnp.float32)
+        d_out = d_ref[place_of(z, i)]
+        d_wide = d_out.astype(jnp.float32)
+        d_head = jnp.concatenate([zero, d_out], axis=0)
+        rows = jnp.concatenate([hq_ref[i].astype(jnp.float32), d_wide], axis=0).T
         left = lax.broadcasted_iota(jnp.int32, rows.shape, 1) < HEAD_DIM
         rhs = jnp.concatenate([jnp.where(left, 0.0, rows), jnp.where(left, rows, 0.0)], axis=0)
         rhs = rhs.astype(jnp.bfloat16)
         inverse = stats_ref[i, 0:1]
-        row_dot = stats_ref[i, 1:2]
+        row_dot = jnp.sum(head_ref[i].astype(jnp.float32) * d_wide, axis=0, keepdims=True)
         d_qunit = jnp.zeros((HEAD_DIM, CHUNK), jnp.float32)
         for j in range(N_SEQ):
             prob = jnp.exp(matmul(kv_ref[j], query)) * inverse
@@ -236,7 +246,7 @@
             pieces.append(factor * d_unit - factor * factor * factor * wide * mean)
         stacked = jnp.concatenate(pieces + [turned[HEAD_DIM:]], axis=0).astype(jnp.bfloat16)
         stacks[j][...] = stacked
-        term = matmul(stacked, chunks[j][...])
+        term = matmul(stacked, chunks[j]())
         if j == 0:
             grad_t[: 3 * HEAD_DIM] = term
         else:
@@ -248,15 +258,16 @@
 
 def result_kernel(*refs):
     place_ref = refs[0]
-    chunks = refs[1:9]
-    heads_ref, w_ref, grad_ref, x_ref, act_ref, cut_ref = refs[9:15]
+    chunks = read_chunks(refs[1:10])
+    home_ref, w_ref, grad_ref, x_ref, act_ref = refs[10:15]
     out_ref, keep_ref, give_ref, grad_t, grad_msg, grad_out = refs[15:]
     z = place_ref[0]
-    every = jnp.concatenate([heads_ref[h] for h in range(N_SEQ)], axis=0)
+    every = jnp.concatenate([home_ref[h, :HEAD_DIM] for h in range(N_SEQ)], axis=0)
     grad_out[...] = matmul(every, grad_ref[...])
     for j in range(N_SEQ):
-        columns = cut_ref[place_of(z, j)].astype(jnp.float32).T.astype(jnp.bfloat16)
-        term = matmul(columns, chunks[j][...])
+        folded = home_ref[place_of(z, j), HEAD_DIM:].astype(jnp.float32)
+        columns = jnp.concatenate([folded[:, :BLOCK].T, folded[:, BLOCK:].T], axis=1)
+        term = matmul(columns.astype(jnp.bfloat16), chunks[j]())
         if j == 0:
             grad_t[...] = term
         else:
@@ -382,9 +393,8 @@
         d_out_kernel, "d_out", (((N_SEQ, HEAD_DIM, node_rows), bf16),), (), (out_grad, w_out),
         flops=2 * node_rows * width * hd, moved=2 << 20,
     )
-    d_heads = exchange(d_out, "z")
     w_head = pick_head(place, w_qkv)
-    a1, b1, d_heads = lax.optimization_barrier((a1, b1, d_heads))
+    a1, b1, d_out, w_head = lax.optimization_barrier((a1, b1, d_out, w_head))
     a2, b2 = up(a1), down(b1)
 
     act, to_low, mid, to_high = call(
@@ -393,33 +403,32 @@
         [pltpu.VMEM((6, BLOCK, width), bf16), pltpu.VMEM((6, BLOCK, width), f32)],
         flops=8 * node_rows * width * width, exps=node_rows * width, moved=8 << 20,
     )
-    a2, b2, w_head, to_low, to_high = lax.optimization_barrier((a2, b2, w_head, to_low, to_high))
+    a2, b2, to_low, to_high = lax.optimization_barrier((a2, b2, to_low, to_high))
     a3, b3 = up(a2), down(b2)
     above, below = down(to_low), up(to_high)
     a3, b3, above, below = lax.optimization_barrier((a3, b3, above, below))
     half = node_rows // 2
     c4 = (up(a3[:half]), down(b3[half:]))
     d_msg_cut, d_norm = call(
-        message_grad_kernel, "message_grad", (((N_SEQ, node_rows, width // N_SEQ), bf16), wide_shape),
+        message_grad_kernel, "message_grad", (((N_SEQ, BLOCK, CHUNK), bf16), wide_shape),
         (), (mid, above, below, w_msg), flops=2 * node_rows * width * width, moved=8 << 20,
     )
-    *c4, d_msg_cut, d_norm = lax.optimization_barrier((*c4, d_msg_cut, d_norm))
-    c4 = jnp.concatenate(c4, axis=0)
-    chunks = (normed, a1, a2, a3, c4, b3, b2, b1)
-    d_msg_cut = exchange(d_msg_cut, "z")
+    *c4, d_msg_cut, d_norm, d_out = lax.optimization_barrier((*c4, d_msg_cut, d_norm, d_out))
+    chunks = (normed, a1, a2, a3, *c4, b3, b2, b1)
+    d_heads = exchange(d_out, "z")
 
     lanes_in = ((N_SEQ, CHUNK, 2 * HEAD_DIM), bf16)
     turned = ((N_SEQ, HEAD_DIM, CHUNK), bf16)
-    out_t, *saved = call(
+    send, *saved = call(
         forward_kernel, "attend_forward",
-        (turned, lanes_in, lanes_in, turned, turned,
-         ((N_SEQ, 2 * HEAD_DIM, CHUNK), bf16), ((N_SEQ, 8, CHUNK), f32)),
-        (place,), chunks + (w_head, d_heads),
+        (((N_SEQ, HEAD_DIM + BLOCK, CHUNK), bf16), lanes_in, turned, turned,
+         ((N_SEQ, 2 * HEAD_DIM, CHUNK), bf16), turned, ((N_SEQ, 8, CHUNK), f32)),
+        (place,), chunks + (w_head, d_msg_cut),
         [pltpu.VMEM((N_SEQ, HEAD_DIM + ONES, CHUNK), bf16)],
         flops=12 * nodes * nodes * HEAD_DIM, exps=nodes * nodes, moved=8 << 20,
     )
-    out_t, d_msg_cut = lax.optimization_barrier((out_t, d_msg_cut))
-    heads = exchange(out_t, "z")
+    send, d_heads = lax.optimization_barrier((send, d_heads))
+    home = exchange(send, "z")
 
     rows_here = width // (2 * N_XY)
     rows_out = hd // (2 * N_XY)
@@ -441,7 +450,7 @@
     part_out = ((N_XY, rows_here + rows_out * width // BLOCK, BLOCK), bf16)
     block_result_array, keep_out, give_out = call(
         result_kernel, "result", (low_shape, part_out, part_out), (place,),
-        chunks + (after(heads, keep), w_out, out_grad, features, act, d_msg_cut),
+        chunks + (after(home, keep), w_out, out_grad, features, act),
         [pltpu.VMEM((BLOCK, width), f32), pltpu.VMEM((width, BLOCK), f32), pltpu.VMEM((hd, width), f32)],
         flops=6 * node_rows * width * width, moved=10 << 20,
     )
@@ -454,6 +463,7 @@
     pair, *stacks = lax.optimization_barrier((pair, *stacks))
     shares = exchange(pair, ("x", "y"))
     stacks = [stacks[0]] + [shift(stacks[j], -j) for j in range(1, N_SEQ)]
+    shares, *stacks = lax.optimization_barrier((shares, *stacks))
     (mine,) = call(
         share_kernel, "share_sum", (((N_SEQ, all_rows, BLOCK), bf16),), (), (shares,), moved=2 << 20,
     )

time: 215 us -> 222 us (1.033)
  blocking collectives: 36.7 us -> 0 us
  local copies, waits for them, and re-layouts: 28.1 us -> 63.6 us
  waiting for transfers between devices: 37.1 us -> 47.1 us
  Pallas kernels: 56.8 us -> 48.2 us
  starting transfers between devices: 51.6 us -> 58.4 us
    unnamed x101 -> x176, local copies, waits for them, and re-layouts: 25.2 us -> 62.6 us
    all_to_all x2 -> x0, blocking collectives: 36.7 us -> none  [exchange(): return lax.all_to_all(array, axis, split_axis=0, concat_axis=0, tiled=True)]
    pallas_call x11, Pallas kernels: 53.8 us -> 45.1 us  [call(): pl.pallas_call(kernel, out_shape=tuple((jax.ShapeDtypeStruct(s, t) for s,...]
    ppermute x17, waiting for transfers between devices: 35.1 us -> 42.4 us  [shift(): lax.ppermute(array, 'z', [(i, (i + distance) % N_SEQ) for i in range(N_SE...]
    all_to_all x3 -> x4, starting transfers between devices: 19.6 us -> 23.8 us  [exchange(): return lax.all_to_all(array, axis, split_axis=0, concat_axis=0, tiled=True)]
    ppermute x17, starting transfers between devices: 31.4 us -> 34.2 us  [shift(): lax.ppermute(array, 'z', [(i, (i + distance) % N_SEQ) for i in range(N_SE...]
    all_to_all x3 -> x4, waiting for transfers between devices: 0.01 us -> 2.68 us  [exchange(): return lax.all_to_all(array, axis, split_axis=0, concat_axis=0, tiled=True)]
  transfers between devices with their start and end apart: 22 -> 23, of which waited for: 12 -> 12; matrix products, arithmetic and copies ran while one was open for 2% -> 1% of each run, Pallas kernels for 24% -> 19%
where the time goes in v1:
time: 222 us; the launch traced here: 220 us
  local copies, waits for them, and re-layouts  63.6 us (29%)
  starting transfers between devices  58.4 us (26%)
  Pallas kernels  48.2 us (22%)
  waiting for transfers between devices  47.1 us (21%)
    unnamed x176, local copies, waits for them, and re-layouts  62.6 us
    pallas_call x11, Pallas kernels, call(): pl.pallas_call(kernel, out_shape=tuple((jax.ShapeDtypeStruct(s, t) for s,...  45.1 us
    ppermute x17, waiting for transfers between devices, shift(): lax.ppermute(array, 'z', [(i, (i + distance) % N_SEQ) for i in range(N_SE...  42.4 us
    ppermute x17, starting transfers between devices, shift(): lax.ppermute(array, 'z', [(i, (i + distance) % N_SEQ) for i in range(N_SE...  34.2 us
    all_to_all x4, starting transfers between devices, exchange(): return lax.all_to_all(array, axis, split_axis=0, concat_axis=0, tiled=True)  23.8 us
  transfers between devices with their start and end apart: 23, of which 12 were waited for; matrix products, arithmetic and copies ran while one was open for 1% of the time, Pallas kernels for 19%

profile of v1, /device:TPU:6, one launch (start us, length us, event | category | flops | bytes accessed | tf_op | source)
XLA Modules:
  0.0 219.6 jit_solution(13023418935261389268)
XLA Ops:
  4.6 4.0 %collective-permute-start.1 = (bf16[256,1024]{1,0:T(8,128)(2,1)S(1)}, bf16[256,1024]{1,0:T(8,128)(2,1)S(1)}, u32[]{:S(2)}, u32[]{:S(2)}) collective-permute-start(bf16[256,1024]{1,0:T(8,128)(2,1)S(1)} %normalize.1.refs_4_.refs_1_), channel_id=1, source_target_pairs={{0,7},{1,0},{2,1},{3,2},{4,3},{5,4},{6,5},{7,6},{8,15},{9,8},{10,9... | collective-permute-start | bytes 1572872 | tf_op jit(solution)/shard_map/ppermute | solution.py:355
  9.2 3.1 %pick_head.1.refs_10_ = bf16[192,1024]{1,0:T(8,128)(2,1)} custom-call(s32[2]{0:T(128)} %pad_add_fusion.place_ref.refs_0_, bf16[1024,1536]{1,0:T(8,128)(2,1)} %refs_9_.1, bf16[1024,1536]{1,0:T(8,128)(2,1)} %refs_9_.1, bf16[1024,1536]{1,0:T(8,128)(2,1)} %refs_9_.1), custom_call_target="tpu_custom_call" | custom-call | bytes 4194304 | tf_op jit(solution)/shard_map/pick_head/pallas_call | solution.py:84
  13.5 6.9 %collective-permute-done.refs_3_.refs_2_ = bf16[256,1024]{1,0:T(8,128)(2,1)S(1)} collective-permute-done((bf16[256,1024]{1,0:T(8,128)(2,1)S(1)}, bf16[256,1024]{1,0:T(8,128)(2,1)S(1)}, u32[]{:S(2)}, u32[]{:S(2)}) %collective-permute-start) | collective-permute-done | bytes 524320 | tf_op jit(solution)/shard_map/ppermute | solution.py:355
  20.5 3.2 %collective-permute-start.3 = (bf16[256,1024]{1,0:T(8,128)(2,1)S(1)}, bf16[256,1024]{1,0:T(8,128)(2,1)S(1)}, u32[]{:S(2)}, u32[]{:S(2)}) collective-permute-start(bf16[256,1024]{1,0:T(8,128)(2,1)S(1)} %collective-permute-done.1.refs_5_.refs_9_), channel_id=1, source_target_pairs={{0,7},{1,0},{2,1},{3,2},{4,3},{5,4},{6,5},{7,6},{8,15},{9,8},{10,9... | collective-permute-start | bytes 1572872 | tf_op jit(solution)/shard_map/ppermute | solution.py:355
  25.4 4.2 %messages.1 = (f32[256,1024]{1,0:T(8,128)S(1)}, bf16[256,1024]{1,0:T(8,128)(2,1)S(1)}, f32[256,1024]{1,0:T(8,128)S(1)}, bf16[256,1024]{1,0:T(8,128)(2,1)S(1)}) custom-call(s32[2]{0:T(128)S(1)} %copy-done.62, s32[2,4]{1,0:T(2,128)S(1)} %copy-done.74, s32[2]{0:T(128)S(1)} %copy-done.75, bf16[256,1024]{1,0:T(8,128)(2,1)S(1)} %collective-permute-done.refs_3_.refs_2_, ...), custom_call_target="tpu_custom_call" | custom-call | flops 2147483648 | bytes 8388608 | tf_op jit(solution)/shard_map/messages/pallas_call | solution.py:45
  29.6 5.2 %collective-permute-done.2.refs_3_ = bf16[256,1024]{1,0:T(8,128)(2,1)S(1)} collective-permute-done((bf16[256,1024]{1,0:T(8,128)(2,1)S(1)}, bf16[256,1024]{1,0:T(8,128)(2,1)S(1)}, u32[]{:S(2)}, u32[]{:S(2)}) %collective-permute-start.2) | collective-permute-done | bytes 524320 | tf_op jit(solution)/shard_map/ppermute | solution.py:355
  41.7 9.2 %collective-permute-done.4.refs_4_ = bf16[256,1024]{1,0:T(8,128)(2,1)S(1)} collective-permute-done((bf16[256,1024]{1,0:T(8,128)(2,1)S(1)}, bf16[256,1024]{1,0:T(8,128)(2,1)S(1)}, u32[]{:S(2)}, u32[]{:S(2)}) %collective-permute-start.4) | collective-permute-done | bytes 524320 | tf_op jit(solution)/shard_map/ppermute | solution.py:355
  52.2 7.6 %collective-permute-done.6.refs_1_ = bf16[256,1024]{1,0:T(8,128)(2,1)S(1)} collective-permute-done((bf16[256,1024]{1,0:T(8,128)(2,1)S(1)}, bf16[256,1024]{1,0:T(8,128)(2,1)S(1)}, u32[]{:S(2)}, u32[]{:S(2)}) %collective-permute-start.6) | collective-permute-done | bytes 524320 | tf_op jit(solution)/shard_map/ppermute | solution.py:355
  69.3 4.9 %all-to-all-start = ((bf16[8,64,256]{2,1,0:T(8,128)(2,1)}), bf16[8,64,256]{2,1,0:T(8,128)(2,1)}, u32[]{:S(2)}, u32[]{:S(2)}) async-start(bf16[8,64,256]{2,1,0:T(8,128)(2,1)} %d_out.1), calls=%async_computation | async-start | bytes 524288 | tf_op jit(solution)/shard_map/all_to_all | solution.py:351
  81.3 8.9 %attend_forward.1 = (bf16[8,192,256]{2,1,0:T(8,128)(2,1)S(1)}, bf16[8,256,128]{2,1,0:T(8,128)(2,1)S(1)}, bf16[8,64,256]{2,1,0:T(8,128)(2,1)S(1)}, bf16[8,64,256]...) custom-call(s32[2]{0:T(128)S(1)} %copy-done.62, ...), custom_call_target="tpu_custom_call" | custom-call | flops 3221225472 | bytes 8388608 | tf_op jit(solution)/shard_map/attend_forward/pallas_call | solution.py:45
  95.6 7.2 %all-to-all-start.1 = ((bf16[8,192,256]{2,1,0:T(8,128)(2,1)}), bf16[8,192,256]{2,1,0:T(8,128)(2,1)S(1)}, u32[]{:S(2)}, u32[]{:S(2)}) async-start(bf16[8,192,256]{2,1,0:T(8,128)(2,1)} %copy-done.20), calls=%async_computation.1 | async-start | bytes 1572864 | tf_op jit(solution)/shard_map/all_to_all | solution.py:351
  116.7 20.8 %attend_backward.1 = (bf16[192,256]{1,0:T(8,128)(2,1)S(1)}, bf16[192,256]{1,0:T(8,128)(2,1)}, bf16[192,256]{1,0:T(8,128)(2,1)S(1)}, bf16[192,256]{1,0:T(8,128)(2...) custom-call(s32[2]{0:T(128)S(1)} %copy-done.62, ...), custom_call_target="tpu_custom_call" | custom-call | flops 6442450944 | bytes 8388608 | tf_op jit(solution)/shard_map/attend_backward/pallas_call | solution.py:45
  152.1 2.7 %result.1 = (bf16[256,1024]{1,0:T(8,128)(2,1)}, bf16[16,160,128]{2,1,0:T(8,128)(2,1)S(1)}, bf16[16,160,128]{2,1,0:T(8,128)(2,1)S(1)}) custom-call(s32[2]{0:T(128)S(1)} %copy-done.62, bf16[256,1024]{1,0:T(8,128)(2,1)S(1)} %normalize.1.refs_4_.refs_1_, bf16[256,1024]{1,0:T(8,128)(2,1)S(1)} %copy-done.24, bf16[256,1024]{1,0:T(8,128)(2,1)S(1)} %copy-done.32, ...), custom_call_target="tpu_custom_call" | custom-call | flops 1610612736 | bytes 10485760 | tf_op jit(solution)/shard_map/result/pallas_call | solution.py:45
  158.5 7.6 %all-to-all-start.2 = ((bf16[16,224,128]{2,1,0:T(8,128)(2,1)}), bf16[16,224,128]{2,1,0:T(8,128)(2,1)}, u32[]{:S(2)}, u32[]{:S(2)}) async-start(bf16[16,224,128]{2,1,0:T(8,128)(2,1)} %copy-done.7), calls=%async_computation.2 | async-start | bytes 1835008 | tf_op jit(solution)/shard_map/all_to_all | solution.py:351
  166.1 3.2 %collective-permute-start.12 = (bf16[192,256]{1,0:T(8,128)(2,1)}, bf16[192,256]{1,0:T(8,128)(2,1)S(1)}, u32[]{:S(2)}, u32[]{:S(2)}) collective-permute-start(bf16[192,256]{1,0:T(8,128)(2,1)} %get-tuple-element.121), channel_id=1, source_target_pairs={{0,7},{1,0},{2,1},{3,2},{4,3},{5,4},{6,5},{7,6},{8,15},{9,8},{10,9... | collective-permute-start | bytes 294920 | tf_op jit(solution)/shard_map/ppermute | solution.py:355
  169.3 2.4 %collective-permute-start.13 = (bf16[192,256]{1,0:T(8,128)(2,1)}, bf16[192,256]{1,0:T(8,128)(2,1)S(1)}, u32[]{:S(2)}, u32[]{:S(2)}) collective-permute-start(bf16[192,256]{1,0:T(8,128)(2,1)} %copy-done.73), channel_id=1, source_target_pairs={{0,6},{1,7},{2,0},{3,1},{4,2},{5,3},{6,4},{7,5},{8,14},{9,15},{10,... | collective-permute-start | bytes 294920 | tf_op jit(solution)/shard_map/ppermute | solution.py:355
  173.1 3.6 %collective-permute-start.15 = (bf16[192,256]{1,0:T(8,128)(2,1)}, bf16[192,256]{1,0:T(8,128)(2,1)S(1)}, u32[]{:S(2)}, u32[]{:S(2)}) collective-permute-start(bf16[192,256]{1,0:T(8,128)(2,1)} %copy-done.71), channel_id=1, source_target_pairs={{0,4},{1,5},{2,6},{3,7},{4,0},{5,1},{6,2},{7,3},{8,12},{9,13},{10,... | collective-permute-start | bytes 294920 | tf_op jit(solution)/shard_map/ppermute | solution.py:355
  176.9 3.6 %collective-permute-start.17 = (bf16[192,256]{1,0:T(8,128)(2,1)}, bf16[192,256]{1,0:T(8,128)(2,1)S(1)}, u32[]{:S(2)}, u32[]{:S(2)}) collective-permute-start(bf16[192,256]{1,0:T(8,128)(2,1)} %copy-done.69), channel_id=1, source_target_pairs={{0,2},{1,3},{2,4},{3,5},{4,6},{5,7},{6,0},{7,1},{8,10},{9,11},{10,... | collective-permute-start | bytes 294920 | tf_op jit(solution)/shard_map/ppermute | solution.py:355
  182.0 4.5 %collective-permute-done.14.refs_4_ = bf16[192,256]{1,0:T(8,128)(2,1)S(1)} collective-permute-done((bf16[192,256]{1,0:T(8,128)(2,1)}, bf16[192,256]{1,0:T(8,128)(2,1)S(1)}, u32[]{:S(2)}, u32[]{:S(2)}) %collective-permute-start.14) | collective-permute-done | bytes 98336 | tf_op jit(solution)/shard_map/ppermute | solution.py:355
  187.8 3.0 %collective-permute-done.16.refs_6_ = bf16[192,256]{1,0:T(8,128)(2,1)S(1)} collective-permute-done((bf16[192,256]{1,0:T(8,128)(2,1)}, bf16[192,256]{1,0:T(8,128)(2,1)S(1)}, u32[]{:S(2)}, u32[]{:S(2)}) %collective-permute-start.16) | collective-permute-done | bytes 98336 | tf_op jit(solution)/shard_map/ppermute | solution.py:355
  191.4 3.0 %collective-permute-done.17.refs_7_ = bf16[192,256]{1,0:T(8,128)(2,1)S(1)} collective-permute-done((bf16[192,256]{1,0:T(8,128)(2,1)}, bf16[192,256]{1,0:T(8,128)(2,1)S(1)}, u32[]{:S(2)}, u32[]{:S(2)}) %collective-permute-start.17) | collective-permute-done | bytes 98336 | tf_op jit(solution)/shard_map/ppermute | solution.py:355
  197.8 4.1 %all-to-all-start.3 = ((bf16[8,224,128]{2,1,0:T(8,128)(2,1)}), bf16[8,224,128]{2,1,0:T(8,128)(2,1)}, u32[]{:S(2)}, u32[]{:S(2)}) async-start(bf16[8,224,128]{2,1,0:T(8,128)(2,1)} %copy-done.9), calls=%async_computation.3 | async-start | bytes 917504 | tf_op jit(solution)/shard_map/all_to_all | solution.py:351
  211.6 2.8 %input_grad.1 = bf16[256,1024]{1,0:T(8,128)(2,1)} custom-call(s32[2]{0:T(128)S(1)} %copy-done.62, bf16[192,256]{1,0:T(8,128)(2,1)S(1)} %get-tuple-element.128.refs_1_, bf16[192,256]{1,0:T(8,128)(2,1)S(1)} %collective-permute-done.12.refs_2_, bf16[192,256]{1,0:T(8,128)(2,1)S(1)} %copy-done.49, bf16[192,256]{1,0:T(8,128)(2,1)S(1)} %copy-done.51, ...), custom_call_target="tpu_custom_call" | custom-call | flops 805306368 | bytes 8388608 | tf_op jit(solution)/shard_map/input_grad/pallas_call | solution.py:45
  214.4 2.7 %all-to-all-done.3.every_ref = bf16[8,224,128]{2,1,0:T(8,128)(2,1)} async-done(((bf16[8,224,128]{2,1,0:T(8,128)(2,1)}), bf16[8,224,128]{2,1,0:T(8,128)(2,1)}, u32[]{:S(2)}, u32[]{:S(2)}) %all-to-all-start.3) | async-done | bytes 458784 | tf_op jit(solution)/shard_map/all_to_all | solution.py:351
  (218 shorter events, 90.1 us)
Async XLA Ops:
  2.6 17.9 %collective-permute-start = (bf16[256,1024]{1,0:T(8,128)(2,1)S(1)}, bf16[256,1024]{1,0:T(8,128)(2,1)S(1)}, u32[]{:S(2)}, u32[]{:S(2)}) collective-permute-start(bf16[256,1024]{1,0:T(8,128)(2,1)S(1)} %normalize.1.refs_4_.refs_1_), channel_id=1, source_target_pairs={{0,1},{1,2},{2,3},{3,4},{4,5},{5,6},{6,7},{7,0},{8,9},{9,10},{10,1... | collective-permute-start | bytes 1572872 | tf_op jit(solution)/shard_map/ppermute | solution.py:355
  4.6 15.9 %collective-permute-start.1 = (bf16[256,1024]{1,0:T(8,128)(2,1)S(1)}, bf16[256,1024]{1,0:T(8,128)(2,1)S(1)}, u32[]{:S(2)}, u32[]{:S(2)}) collective-permute-start(bf16[256,1024]{1,0:T(8,128)(2,1)S(1)} %normalize.1.refs_4_.refs_1_), channel_id=1, source_target_pairs={{0,7},{1,0},{2,1},{3,2},{4,3},{5,4},{6,5},{7,6},{8,15},{9,8},{10,9... | collective-permute-start | bytes 1572872 | tf_op jit(solution)/shard_map/ppermute | solution.py:355
  20.4 14.4 %collective-permute-start.2 = (bf16[256,1024]{1,0:T(8,128)(2,1)S(1)}, bf16[256,1024]{1,0:T(8,128)(2,1)S(1)}, u32[]{:S(2)}, u32[]{:S(2)}) collective-permute-start(bf16[256,1024]{1,0:T(8,128)(2,1)S(1)} %collective-permute-done.refs_3_.refs_2_), channel_id=1, source_target_pairs={{0,1},{1,2},{2,3},{3,4},{4,5},{5,6},{6,7},{7,0},{8,9},{9,10},{10,1... | collective-permute-start | bytes 1572872 | tf_op jit(solution)/shard_map/ppermute | solution.py:355
  20.5 14.3 %collective-permute-start.3 = (bf16[256,1024]{1,0:T(8,128)(2,1)S(1)}, bf16[256,1024]{1,0:T(8,128)(2,1)S(1)}, u32[]{:S(2)}, u32[]{:S(2)}) collective-permute-start(bf16[256,1024]{1,0:T(8,128)(2,1)S(1)} %collective-permute-done.1.refs_5_.refs_9_), channel_id=1, source_target_pairs={{0,7},{1,0},{2,1},{3,2},{4,3},{5,4},{6,5},{7,6},{8,15},{9,8},{10,9... | collective-permute-start | bytes 1572872 | tf_op jit(solution)/shard_map/ppermute | solution.py:355
  34.8 16.1 %collective-permute-start.4 = (bf16[256,1024]{1,0:T(8,128)(2,1)S(1)}, bf16[256,1024]{1,0:T(8,128)(2,1)S(1)}, u32[]{:S(2)}, u32[]{:S(2)}) collective-permute-start(bf16[256,1024]{1,0:T(8,128)(2,1)S(1)} %collective-permute-done.2.refs_3_), channel_id=1, source_target_pairs={{0,1},{1,2},{2,3},{3,4},{4,5},{5,6},{6,7},{7,0},{8,9},{9,10},{10,1... | collective-permute-start | bytes 1572872 | tf_op jit(solution)/shard_map/ppermute | solution.py:355
  37.4 14.9 %collective-permute-start.5 = (bf16[256,1024]{1,0:T(8,128)(2,1)S(1)}, bf16[256,1024]{1,0:T(8,128)(2,1)S(1)}, u32[]{:S(2)}, u32[]{:S(2)}) collective-permute-start(bf16[256,1024]{1,0:T(8,128)(2,1)S(1)} %collective-permute-done.3.refs_8_), channel_id=1, source_target_pairs={{0,7},{1,0},{2,1},{3,2},{4,3},{5,4},{6,5},{7,6},{8,15},{9,8},{10,9... | collective-permute-start | bytes 1572872 | tf_op jit(solution)/shard_map/ppermute | solution.py:355
  39.7 20.2 %collective-permute-start.6 = (bf16[256,1024]{1,0:T(8,128)(2,1)S(1)}, bf16[256,1024]{1,0:T(8,128)(2,1)S(1)}, u32[]{:S(2)}, u32[]{:S(2)}) collective-permute-start(bf16[256,1024]{1,0:T(8,128)(2,1)S(1)} %get-tuple-element.80), channel_id=1, source_target_pairs={{0,7},{1,0},{2,1},{3,2},{4,3},{5,4},{6,5},{7,6},{8,15},{9,8},{10,9... | collective-permute-start | bytes 1572872 | tf_op jit(solution)/shard_map/ppermute | solution.py:355
  41.4 18.5 %collective-permute-start.7 = (bf16[256,1024]{1,0:T(8,128)(2,1)S(1)}, bf16[256,1024]{1,0:T(8,128)(2,1)S(1)}, u32[]{:S(2)}, u32[]{:S(2)}) collective-permute-start(bf16[256,1024]{1,0:T(8,128)(2,1)S(1)} %get-tuple-element.81), channel_id=1, source_target_pairs={{0,1},{1,2},{2,3},{3,4},{4,5},{5,6},{6,7},{7,0},{8,9},{9,10},{10,1... | collective-permute-start | bytes 1572872 | tf_op jit(solution)/shard_map/ppermute | solution.py:355
  59.9 7.8 %collective-permute-start.8 = (bf16[128,1024]{1,0:T(8,128)(2,1)S(1)}, bf16[128,1024]{1,0:T(8,128)(2,1)S(1)}, u32[]{:S(2)}, u32[]{:S(2)}) collective-permute-start(bf16[128,1024]{1,0:T(8,128)(2,1)S(1)} %slice.6), channel_id=1, source_target_pairs={{0,1},{1,2},{2,3},{3,4},{4,5},{5,6},{6,7},{7,0},{8,9},{9,10},{10,1... | collective-permute-start | bytes 786440 | tf_op jit(solution)/shard_map/ppermute | solution.py:355
  61.9 6.6 %collective-permute-start.9 = (bf16[128,1024]{1,0:T(8,128)(2,1)S(1)}, bf16[128,1024]{1,0:T(8,128)(2,1)S(1)}, u32[]{:S(2)}, u32[]{:S(2)}) collective-permute-start(bf16[128,1024]{1,0:T(8,128)(2,1)S(1)} %slice.7), channel_id=1, source_target_pairs={{0,7},{1,0},{2,1},{3,2},{4,3},{5,4},{6,5},{7,6},{8,15},{9,8},{10,9... | collective-permute-start | bytes 786440 | tf_op jit(solution)/shard_map/ppermute | solution.py:355
  69.3 26.3 %all-to-all-start = ((bf16[8,64,256]{2,1,0:T(8,128)(2,1)}), bf16[8,64,256]{2,1,0:T(8,128)(2,1)}, u32[]{:S(2)}, u32[]{:S(2)}) async-start(bf16[8,64,256]{2,1,0:T(8,128)(2,1)} %d_out.1), calls=%async_computation | async-start | bytes 524288 | tf_op jit(solution)/shard_map/all_to_all | solution.py:351
  95.6 47.2 %all-to-all-start.1 = ((bf16[8,192,256]{2,1,0:T(8,128)(2,1)}), bf16[8,192,256]{2,1,0:T(8,128)(2,1)S(1)}, u32[]{:S(2)}, u32[]{:S(2)}) async-start(bf16[8,192,256]{2,1,0:T(8,128)(2,1)} %copy-done.20), calls=%async_computation.1 | async-start | bytes 1572864 | tf_op jit(solution)/shard_map/all_to_all | solution.py:351
  154.9 2.5 %collective-permute-start.11 = (bf16[16,160,128]{2,1,0:T(8,128)(2,1)S(1)}, bf16[16,160,128]{2,1,0:T(8,128)(2,1)S(1)}, u32[]{:S(2)}, u32[]{:S(2)}) collective-permute-start(bf16[16,160,128]{2,1,0:T(8,128)(2,1)S(1)} %get-tuple-element.110), channel_id=1, source_target_pairs={{0,8},{8,0},{1,9},{9,1},{2,10},{10,2},{3,11},{11,3},{4,12},{12,4},... | collective-permute-start | bytes 1966088 | tf_op jit(solution)/shard_map/ppermute | solution.py:457
  154.9 2.5 %collective-permute-start.10 = (bf16[16,64,128]{2,1,0:T(8,128)(2,1)S(1)}, bf16[16,64,128]{2,1,0:T(8,128)(2,1)S(1)}, u32[]{:S(2)}, u32[]{:S(2)}) collective-permute-start(bf16[16,64,128]{2,1,0:T(8,128)(2,1)S(1)} %copy-done.67), channel_id=1, source_target_pairs={{0,8},{8,0},{1,9},{9,1},{2,10},{10,2},{3,11},{11,3},{4,12},{12,4},... | collective-permute-start | bytes 786440 | tf_op jit(solution)/shard_map/ppermute | solution.py:448
  157.3 45.6 %copy-start = (bf16[1024,1536]{1,0:T(8,128)(2,1)S(1)}, bf16[1024,1536]{1,0:T(8,128)(2,1)}, u32[]{:S(2)}) copy-start(bf16[1024,1536]{1,0:T(8,128)(2,1)} %refs_9_.1) | copy-start | bytes 9437188
  158.5 37.2 %all-to-all-start.2 = ((bf16[16,224,128]{2,1,0:T(8,128)(2,1)}), bf16[16,224,128]{2,1,0:T(8,128)(2,1)}, u32[]{:S(2)}, u32[]{:S(2)}) async-start(bf16[16,224,128]{2,1,0:T(8,128)(2,1)} %copy-done.7), calls=%async_computation.2 | async-start | bytes 1835008 | tf_op jit(solution)/shard_map/all_to_all | solution.py:351
  166.1 10.9 %collective-permute-start.12 = (bf16[192,256]{1,0:T(8,128)(2,1)}, bf16[192,256]{1,0:T(8,128)(2,1)S(1)}, u32[]{:S(2)}, u32[]{:S(2)}) collective-permute-start(bf16[192,256]{1,0:T(8,128)(2,1)} %get-tuple-element.121), channel_id=1, source_target_pairs={{0,7},{1,0},{2,1},{3,2},{4,3},{5,4},{6,5},{7,6},{8,15},{9,8},{10,9... | collective-permute-start | bytes 294920 | tf_op jit(solution)/shard_map/ppermute | solution.py:355
  169.3 11.2 %collective-permute-start.13 = (bf16[192,256]{1,0:T(8,128)(2,1)}, bf16[192,256]{1,0:T(8,128)(2,1)S(1)}, u32[]{:S(2)}, u32[]{:S(2)}) collective-permute-start(bf16[192,256]{1,0:T(8,128)(2,1)} %copy-done.73), channel_id=1, source_target_pairs={{0,6},{1,7},{2,0},{3,1},{4,2},{5,3},{6,4},{7,5},{8,14},{9,15},{10,... | collective-permute-start | bytes 294920 | tf_op jit(solution)/shard_map/ppermute | solution.py:355
  171.7 14.9 %collective-permute-start.14 = (bf16[192,256]{1,0:T(8,128)(2,1)}, bf16[192,256]{1,0:T(8,128)(2,1)S(1)}, u32[]{:S(2)}, u32[]{:S(2)}) collective-permute-start(bf16[192,256]{1,0:T(8,128)(2,1)} %copy-done.72), channel_id=1, source_target_pairs={{0,5},{1,6},{2,7},{3,0},{4,1},{5,2},{6,3},{7,4},{8,13},{9,14},{10,... | collective-permute-start | bytes 294920 | tf_op jit(solution)/shard_map/ppermute | solution.py:355
  173.1 14.0 %collective-permute-start.15 = (bf16[192,256]{1,0:T(8,128)(2,1)}, bf16[192,256]{1,0:T(8,128)(2,1)S(1)}, u32[]{:S(2)}, u32[]{:S(2)}) collective-permute-start(bf16[192,256]{1,0:T(8,128)(2,1)} %copy-done.71), channel_id=1, source_target_pairs={{0,4},{1,5},{2,6},{3,7},{4,0},{5,1},{6,2},{7,3},{8,12},{9,13},{10,... | collective-permute-start | bytes 294920 | tf_op jit(solution)/shard_map/ppermute | solution.py:355
  176.7 14.1 %collective-permute-start.16 = (bf16[192,256]{1,0:T(8,128)(2,1)}, bf16[192,256]{1,0:T(8,128)(2,1)S(1)}, u32[]{:S(2)}, u32[]{:S(2)}) collective-permute-start(bf16[192,256]{1,0:T(8,128)(2,1)} %copy-done.70), channel_id=1, source_target_pairs={{0,3},{1,4},{2,5},{3,6},{4,7},{5,0},{6,1},{7,2},{8,11},{9,12},{10,... | collective-permute-start | bytes 294920 | tf_op jit(solution)/shard_map/ppermute | solution.py:355
  176.9 17.5 %collective-permute-start.17 = (bf16[192,256]{1,0:T(8,128)(2,1)}, bf16[192,256]{1,0:T(8,128)(2,1)S(1)}, u32[]{:S(2)}, u32[]{:S(2)}) collective-permute-start(bf16[192,256]{1,0:T(8,128)(2,1)} %copy-done.69), channel_id=1, source_target_pairs={{0,2},{1,3},{2,4},{3,5},{4,6},{5,7},{6,0},{7,1},{8,10},{9,11},{10,... | collective-permute-start | bytes 294920 | tf_op jit(solution)/shard_map/ppermute | solution.py:355
  180.5 14.5 %collective-permute-start.18 = (bf16[192,256]{1,0:T(8,128)(2,1)}, bf16[192,256]{1,0:T(8,128)(2,1)S(1)}, u32[]{:S(2)}, u32[]{:S(2)}) collective-permute-start(bf16[192,256]{1,0:T(8,128)(2,1)} %copy-done.68), channel_id=1, source_target_pairs={{0,1},{1,2},{2,3},{3,4},{4,5},{5,6},{6,7},{7,0},{8,9},{9,10},{10,1... | collective-permute-start | bytes 294920 | tf_op jit(solution)/shard_map/ppermute | solution.py:355
  197.8 19.3 %all-to-all-start.3 = ((bf16[8,224,128]{2,1,0:T(8,128)(2,1)}), bf16[8,224,128]{2,1,0:T(8,128)(2,1)}, u32[]{:S(2)}, u32[]{:S(2)}) async-start(bf16[8,224,128]{2,1,0:T(8,128)(2,1)} %copy-done.9), calls=%async_computation.3 | async-start | bytes 917504 | tf_op jit(solution)/shard_map/all_to_all | solution.py:351
  (87 other events, 402.5 us)

commit v2 on v1

--- a/solution.py
+++ b/solution.py
@@ -39,8 +39,9 @@
     return lax.rsqrt(jnp.mean(wide * wide, axis=axis, keepdims=True) + epsilon)
 
 
-def call(kernel, name, out_shape, scalars, arrays, scratch=(), flops=0, exps=0, moved=0):
+def call(kernel, name, out_shape, scalars, arrays, scratch=(), flops=0, exps=0, moved=0, far=()):
     specs = [pl.BlockSpec(memory_space=pltpu.SMEM)] * len(scalars)
+    specs += [pl.BlockSpec(memory_space=pltpu.HBM)] * len(far)
     specs += [pl.BlockSpec(memory_space=pltpu.VMEM)] * len(arrays)
     return pl.pallas_call(
         kernel,
@@ -48,10 +49,10 @@
         in_specs=specs,
         out_specs=tuple(pl.BlockSpec(memory_space=pltpu.VMEM) for _ in out_shape),
         scratch_shapes=list(scratch),
-        compiler_params=pltpu.CompilerParams(vmem_limit_bytes=24 * 1024 * 1024),
+        compiler_params=pltpu.CompilerParams(vmem_limit_bytes=60 * 1024 * 1024),
         cost_estimate=pl.CostEstimate(flops=flops, bytes_accessed=moved, transcendentals=exps),
         name=name,
-    )(*scalars, *arrays)
+    )(*scalars, *far, *arrays)
 
 
 def normalize_kernel(x_ref, gain_ref, out_ref):
@@ -155,26 +156,33 @@
     return lax.rem(z - j + N_SEQ, N_SEQ)
 
 
-def read_chunks(refs):
-    def whole(ref):
-        return lambda: ref[...]
-
-    def halves():
-        return jnp.concatenate([refs[4][...], refs[5][...]], axis=0)
-
-    return [whole(ref) for ref in refs[:4]] + [halves] + [whole(ref) for ref in refs[6:9]]
+def fetch_chunks(refs, held, sems):
+    half = CHUNK // 2
+    targets = [held.at[j] for j in range(4)]
+    targets += [held.at[4, pl.ds(0, half)], held.at[4, pl.ds(half, half)]]
+    targets += [held.at[j] for j in range(5, N_SEQ)]
+    copies = [pltpu.make_async_copy(ref, to, sems.at[i]) for i, (ref, to) in enumerate(zip(refs, targets))]
+    for copy in copies:
+        copy.start()
+
+    def wait(j):
+        for copy in copies[j + (j > 4) : j + 1 + (j >= 4)]:
+            copy.wait()
+
+    return wait
 
 
 def forward_kernel(*refs):
     z = refs[0][0]
-    chunks = read_chunks(refs[1:10])
-    w_ref, cut_ref = refs[10:12]
+    cut_ref, w_ref = refs[10:12]
     send_ref, kv_ref, hq_ref, ku_ref, raw_ref, out_ref, stats_ref = refs[12:19]
-    v_ext = refs[19]
-    for h in range(N_SEQ):
-        send_ref[h, HEAD_DIM:] = cut_ref[h]
+    v_ext, held, sems = refs[19:22]
+    wait = fetch_chunks(refs[1:10], held, sems)
+    pass_on = pltpu.make_async_copy(cut_ref, send_ref.at[:, pl.ds(HEAD_DIM, BLOCK)], sems.at[9])
+    pass_on.start()
     for j in range(N_SEQ):
-        proj = contract_cols(w_ref[...], chunks[j]()).astype(jnp.bfloat16)
+        wait(j)
+        proj = contract_cols(w_ref[...], held[j]).astype(jnp.bfloat16)
         raw_ref[j] = proj[: 2 * HEAD_DIM]
         query = proj[:HEAD_DIM].astype(jnp.float32)
         keyrow = proj[HEAD_DIM : 2 * HEAD_DIM].astype(jnp.float32)
@@ -189,10 +197,9 @@
 
     def step(i, carry):
         query = jnp.concatenate([hq_ref[i], jnp.zeros_like(hq_ref[i])], axis=0)
-        out = jnp.zeros((HEAD_DIM + ONES, CHUNK), jnp.float32)
-        for j in range(N_SEQ):
-            exps = jnp.exp(matmul(kv_ref[j], query)).astype(jnp.bfloat16)
-            out += matmul(v_ext[j], exps)
+        keys = kv_ref[...].reshape(N_SEQ * CHUNK, 2 * HEAD_DIM)
+        exps = jnp.exp(matmul(keys, query)).astype(jnp.bfloat16)
+        out = matmul(jnp.concatenate([v_ext[j] for j in range(N_SEQ)], axis=1), exps)
         inverse = 1.0 / out[HEAD_DIM : HEAD_DIM + 1]
         stats_ref[i, 0:1] = inverse
         head_out = (out[:HEAD_DIM] * inverse).astype(jnp.bfloat16)
@@ -201,15 +208,16 @@
         return carry
 
     lax.fori_loop(0, N_SEQ, step, 0)
+    pass_on.wait()
 
 
 def backward_kernel(*refs):
     place_ref = refs[0]
-    chunks = read_chunks(refs[1:10])
     kv_ref, hq_ref, ku_ref, raw_ref, head_ref, stats_ref, d_ref = refs[10:17]
     stacks = refs[17:25]
     keep_ref, give_ref = refs[25:27]
-    sums, dqt, grad_t, grad = refs[27:31]
+    sums, dqt, grad_t, grad, held, sems = refs[27:33]
+    wait = fetch_chunks(refs[1:10], held, sems)
     z = place_ref[0]
     sums[...] = jnp.zeros_like(sums)
 
@@ -225,13 +233,12 @@
         rhs = rhs.astype(jnp.bfloat16)
         inverse = stats_ref[i, 0:1]
         row_dot = jnp.sum(head_ref[i].astype(jnp.float32) * d_wide, axis=0, keepdims=True)
-        d_qunit = jnp.zeros((HEAD_DIM, CHUNK), jnp.float32)
-        for j in range(N_SEQ):
-            prob = jnp.exp(matmul(kv_ref[j], query)) * inverse
-            d_scores = (prob * (matmul(kv_ref[j], d_head) - row_dot)).astype(jnp.bfloat16)
-            d_qunit += matmul(ku_ref[j], d_scores)
-            both = jnp.concatenate([prob.astype(jnp.bfloat16), d_scores], axis=1)
-            sums[j] += matmul(both, rhs)
+        keys = kv_ref[...].reshape(N_SEQ * CHUNK, 2 * HEAD_DIM)
+        prob = jnp.exp(matmul(keys, query)) * inverse
+        d_scores = (prob * (matmul(keys, d_head) - row_dot)).astype(jnp.bfloat16)
+        d_qunit = matmul(jnp.concatenate([ku_ref[j] for j in range(N_SEQ)], axis=1), d_scores)
+        both = jnp.concatenate([prob.astype(jnp.bfloat16), d_scores], axis=1)
+        sums[...] += matmul(both, rhs).reshape(N_SEQ, CHUNK, 2 * HEAD_DIM)
         dqt[i] = d_qunit * SCALE
         return carry
 
@@ -246,7 +253,8 @@
             pieces.append(factor * d_unit - factor * factor * factor * wide * mean)
         stacked = jnp.concatenate(pieces + [turned[HEAD_DIM:]], axis=0).astype(jnp.bfloat16)
         stacks[j][...] = stacked
-        term = matmul(stacked, chunks[j]())
+        wait(j)
+        term = matmul(stacked, held[j])
         if j == 0:
             grad_t[: 3 * HEAD_DIM] = term
         else:
@@ -258,16 +266,17 @@
 
 def result_kernel(*refs):
     place_ref = refs[0]
-    chunks = read_chunks(refs[1:10])
     home_ref, w_ref, grad_ref, x_ref, act_ref = refs[10:15]
-    out_ref, keep_ref, give_ref, grad_t, grad_msg, grad_out = refs[15:]
+    out_ref, keep_ref, give_ref, grad_t, grad_msg, grad_out, held, sems = refs[15:]
+    wait = fetch_chunks(refs[1:10], held, sems)
     z = place_ref[0]
     every = jnp.concatenate([home_ref[h, :HEAD_DIM] for h in range(N_SEQ)], axis=0)
     grad_out[...] = matmul(every, grad_ref[...])
     for j in range(N_SEQ):
         folded = home_ref[place_of(z, j), HEAD_DIM:].astype(jnp.float32)
         columns = jnp.concatenate([folded[:, :BLOCK].T, folded[:, BLOCK:].T], axis=1)
-        term = matmul(columns.astype(jnp.bfloat16), chunks[j]())
+        wait(j)
+        term = matmul(columns.astype(jnp.bfloat16), held[j])
         if j == 0:
             grad_t[...] = term
         else:
@@ -417,15 +426,16 @@
     chunks = (normed, a1, a2, a3, *c4, b3, b2, b1)
     d_heads = exchange(d_out, "z")
 
+    held = pltpu.VMEM((N_SEQ, CHUNK, width), bf16)
     lanes_in = ((N_SEQ, CHUNK, 2 * HEAD_DIM), bf16)
     turned = ((N_SEQ, HEAD_DIM, CHUNK), bf16)
     send, *saved = call(
         forward_kernel, "attend_forward",
         (((N_SEQ, HEAD_DIM + BLOCK, CHUNK), bf16), lanes_in, turned, turned,
          ((N_SEQ, 2 * HEAD_DIM, CHUNK), bf16), turned, ((N_SEQ, 8, CHUNK), f32)),
-        (place,), chunks + (w_head, d_msg_cut),
-        [pltpu.VMEM((N_SEQ, HEAD_DIM + ONES, CHUNK), bf16)],
-        flops=12 * nodes * nodes * HEAD_DIM, exps=nodes * nodes, moved=8 << 20,
+        (place,), (w_head,),
+        [pltpu.VMEM((N_SEQ, HEAD_DIM + ONES, CHUNK), bf16), held, pltpu.SemaphoreType.DMA((10,))],
+        flops=12 * nodes * nodes * HEAD_DIM, exps=nodes * nodes, moved=8 << 20, far=chunks + (d_msg_cut,),
     )
     send, d_heads = lax.optimization_barrier((send, d_heads))
     home = exchange(send, "z")
@@ -436,23 +446,28 @@
     *stacks, keep, give = call(
         backward_kernel, "attend_backward",
         (((3 * HEAD_DIM, CHUNK), bf16),) * N_SEQ + (part_head, part_head),
-        (place,), chunks + (*saved, d_heads),
+        (place,), (*saved, d_heads),
         [
             pltpu.VMEM((N_SEQ, CHUNK, 2 * HEAD_DIM), f32),
             pltpu.VMEM((N_SEQ, HEAD_DIM, CHUNK), f32),
             pltpu.VMEM((4 * HEAD_DIM, width), f32),
             pltpu.VMEM((width, 4 * HEAD_DIM), f32),
+            held,
+            pltpu.SemaphoreType.DMA((9,)),
         ],
-        flops=24 * nodes * nodes * HEAD_DIM, exps=nodes * nodes, moved=8 << 20,
+        flops=24 * nodes * nodes * HEAD_DIM, exps=nodes * nodes, moved=8 << 20, far=chunks,
     )
     got = lax.ppermute(give, "c", [(0, 1), (1, 0)])
 
     part_out = ((N_XY, rows_here + rows_out * width // BLOCK, BLOCK), bf16)
     block_result_array, keep_out, give_out = call(
         result_kernel, "result", (low_shape, part_out, part_out), (place,),
-        chunks + (after(home, keep), w_out, out_grad, features, act),
-        [pltpu.VMEM((BLOCK, width), f32), pltpu.VMEM((width, BLOCK), f32), pltpu.VMEM((hd, width), f32)],
-        flops=6 * node_rows * width * width, moved=10 << 20,
+        (after(home, keep), w_out, out_grad, features, act),
+        [
+            pltpu.VMEM((BLOCK, width), f32), pltpu.VMEM((width, BLOCK), f32), pltpu.VMEM((hd, width), f32),
+            held, pltpu.SemaphoreType.DMA((9,)),
+        ],
+        flops=6 * node_rows * width * width, moved=10 << 20, far=chunks,
     )
     got_out = lax.ppermute(give_out, "c", [(0, 1), (1, 0)])
     all_rows = part_head[0][1] + part_out[0][1]
@@ -463,7 +478,7 @@
     pair, *stacks = lax.optimization_barrier((pair, *stacks))
     shares = exchange(pair, ("x", "y"))
     stacks = [stacks[0]] + [shift(stacks[j], -j) for j in range(1, N_SEQ)]
-    shares, *stacks = lax.optimization_barrier((shares, *stacks))
+    shares, *stacks[1:5] = lax.optimization_barrier((shares, *stacks[1:5]))
     (mine,) = call(
         share_kernel, "share_sum", (((N_SEQ, all_rows, BLOCK), bf16),), (), (shares,), moved=2 << 20,
     )
@@ -476,6 +491,7 @@
         flops=6 * node_rows * width * hd, moved=8 << 20,
     )
 
+    every, grad_input = lax.optimization_barrier((every, grad_input))
     first = ((lax.axis_index("x") * 4 + lax.axis_index("y")) * 2 + core) * rows_here
     w_rows = lax.dynamic_slice_in_dim(w_qkv, first, rows_here, 0)
     m_rows = lax.dynamic_slice_in_dim(w_msg, first, rows_here, 0)

time: 222 us -> 199 us (0.90)
  local copies, waits for them, and re-layouts: 63.6 us -> 9.52 us
  Pallas kernels: 48.2 us -> 67.8 us
  waiting for transfers between devices: 47.1 us -> 54.1 us
  starting transfers between devices: 58.4 us -> 64 us
    unnamed x176 -> x62, local copies, waits for them, and re-layouts: 62.6 us -> 4.3 us
    pallas_call x11, Pallas kernels: 45.1 us -> 64.8 us  [call(): pl.pallas_call(kernel, out_shape=tuple((jax.ShapeDtypeStruct(s, t) for s,...]
    ppermute x17, waiting for transfers between devices: 42.4 us -> 50.4 us  [shift(): lax.ppermute(array, 'z', [(i, (i + distance) % N_SEQ) for i in range(N_SE...]
    all_to_all x4, starting transfers between devices: 23.8 us -> 29.6 us  [exchange(): return lax.all_to_all(array, axis, split_axis=0, concat_axis=0, tiled=True)]
  transfers between devices with their start and end apart: 23 -> 23, of which waited for: 12 -> 14; matrix products, arithmetic and copies ran while one was open for 1% -> 3% of each run, Pallas kernels for 19% -> 27%
where the time goes in v2:
time: 199 us; the launch traced here: 198 us
  Pallas kernels  67.8 us (34%)
  starting transfers between devices  64 us (32%)
  waiting for transfers between devices  54.1 us (27%)
  local copies, waits for them, and re-layouts  9.52 us (5%)
    pallas_call x11, Pallas kernels, call(): pl.pallas_call(kernel, out_shape=tuple((jax.ShapeDtypeStruct(s, t) for s,...  64.8 us
    ppermute x17, waiting for transfers between devices, shift(): lax.ppermute(array, 'z', [(i, (i + distance) % N_SEQ) for i in range(N_SE...  50.4 us
    ppermute x17, starting transfers between devices, shift(): lax.ppermute(array, 'z', [(i, (i + distance) % N_SEQ) for i in range(N_SE...  33.8 us
    all_to_all x4, starting transfers between devices, exchange(): return lax.all_to_all(array, axis, split_axis=0, concat_axis=0, tiled=True)  29.6 us
    unnamed x62, local copies, waits for them, and re-layouts  4.3 us
  transfers between devices with their start and end apart: 23, of which 14 were waited for; matrix products, arithmetic and copies ran while one was open for 3% of the time, Pallas kernels for 27%

profile of v2, /device:TPU:6, one launch (start us, length us, event | category | flops | bytes accessed | tf_op | source)
XLA Modules:
  0.0 198.3 jit_solution(126335586504361515)
XLA Ops:
  4.6 3.9 %collective-permute-start.1 = (bf16[256,1024]{1,0:T(8,128)(2,1)}, bf16[256,1024]{1,0:T(8,128)(2,1)S(1)}, u32[]{:S(2)}, u32[]{:S(2)}) collective-permute-start(bf16[256,1024]{1,0:T(8,128)(2,1)} %normalize.1.refs_4_.refs_1_), channel_id=1, source_target_pairs={{0,7},{1,0},{2,1},{3,2},{4,3},{5,4},{6,5},{7,6},{8,15},{9,8},{10,9... | collective-permute-start | bytes 1572872 | tf_op jit(solution)/shard_map/ppermute | solution.py:364
  9.1 3.0 %pick_head.1.refs_11_ = bf16[192,1024]{1,0:T(8,128)(2,1)} custom-call(s32[2]{0:T(128)} %pad_add_fusion.place_ref.refs_0_, bf16[1024,1536]{1,0:T(8,128)(2,1)} %refs_9_.1, bf16[1024,1536]{1,0:T(8,128)(2,1)} %refs_9_.1, bf16[1024,1536]{1,0:T(8,128)(2,1)} %refs_9_.1), custom_call_target="tpu_custom_call" | custom-call | bytes 4194304 | tf_op jit(solution)/shard_map/pick_head/pallas_call | solution.py:85
  12.1 2.6 %d_out.1 = bf16[8,64,256]{2,1,0:T(8,128)(2,1)} custom-call(bf16[256,1024]{1,0:T(8,128)(2,1)} %refs_12_.3, bf16[512,1024]{1,0:T(8,128)(2,1)} %refs_11_.2), custom_call_target="tpu_custom_call" | custom-call | flops 268435456 | bytes 2097152 | tf_op jit(solution)/shard_map/d_out/pallas_call | solution.py:46
  14.7 6.0 %collective-permute-done.refs_3_.refs_2_ = bf16[256,1024]{1,0:T(8,128)(2,1)S(1)} collective-permute-done((bf16[256,1024]{1,0:T(8,128)(2,1)}, bf16[256,1024]{1,0:T(8,128)(2,1)S(1)}, u32[]{:S(2)}, u32[]{:S(2)}) %collective-permute-start) | collective-permute-done | bytes 524320 | tf_op jit(solution)/shard_map/ppermute | solution.py:364
  20.8 3.2 %collective-permute-start.3 = (bf16[256,1024]{1,0:T(8,128)(2,1)S(1)}, bf16[256,1024]{1,0:T(8,128)(2,1)S(1)}, u32[]{:S(2)}, u32[]{:S(2)}) collective-permute-start(bf16[256,1024]{1,0:T(8,128)(2,1)S(1)} %collective-permute-done.1.refs_5_.refs_9_), channel_id=1, source_target_pairs={{0,7},{1,0},{2,1},{3,2},{4,3},{5,4},{6,5},{7,6},{8,15},{9,8},{10,9... | collective-permute-start | bytes 1572872 | tf_op jit(solution)/shard_map/ppermute | solution.py:364
  24.0 7.1 %messages.1 = (f32[256,1024]{1,0:T(8,128)}, bf16[256,1024]{1,0:T(8,128)(2,1)}, f32[256,1024]{1,0:T(8,128)}, bf16[256,1024]{1,0:T(8,128)(2,1)}) custom-call(s32[2]{0:T(128)} %pad_add_fusion.place_ref.refs_0_, s32[2,4]{1,0:T(2,128)} %refs_1_.1, s32[2]{0:T(128)} %refs_2_.1, bf16[256,1024]{1,0:T(8,128)(2,1)} %copy-done.6, ...), custom_call_target="tpu_custom_call" | custom-call | flops 2147483648 | bytes 8388608 | tf_op jit(solution)/shard_map/messages/pallas_call | solution.py:46
  31.1 4.0 %collective-permute-done.2.refs_3_ = bf16[256,1024]{1,0:T(8,128)(2,1)S(1)} collective-permute-done((bf16[256,1024]{1,0:T(8,128)(2,1)S(1)}, bf16[256,1024]{1,0:T(8,128)(2,1)S(1)}, u32[]{:S(2)}, u32[]{:S(2)}) %collective-permute-start.2) | collective-permute-done | bytes 524320 | tf_op jit(solution)/shard_map/ppermute | solution.py:364
  40.4 10.8 %collective-permute-done.4.refs_4_ = bf16[256,1024]{1,0:T(8,128)(2,1)S(1)} collective-permute-done((bf16[256,1024]{1,0:T(8,128)(2,1)S(1)}, bf16[256,1024]{1,0:T(8,128)(2,1)S(1)}, u32[]{:S(2)}, u32[]{:S(2)}) %collective-permute-start.4) | collective-permute-done | bytes 524320 | tf_op jit(solution)/shard_map/ppermute | solution.py:364
  51.7 7.6 %collective-permute-done.6.refs_1_ = bf16[256,1024]{1,0:T(8,128)(2,1)S(1)} collective-permute-done((bf16[256,1024]{1,0:T(8,128)(2,1)}, bf16[256,1024]{1,0:T(8,128)(2,1)S(1)}, u32[]{:S(2)}, u32[]{:S(2)}) %collective-permute-start.6) | collective-permute-done | bytes 524320 | tf_op jit(solution)/shard_map/ppermute | solution.py:364
  63.9 4.1 %message_grad.1 = (bf16[8,128,256]{2,1,0:T(8,128)(2,1)}, f32[256,1024]{1,0:T(8,128)}) custom-call(f32[256,1024]{1,0:T(8,128)} %get-tuple-element.82.refs_0_, bf16[256,1024]{1,0:T(8,128)(2,1)} %copy-done.10, bf16[256,1024]{1,0:T(8,128)(2,1)} %copy-done.11, bf16[1024,1024]{1,0:T(8,128)(2,1)} %refs_3_.1), custom_call_target="tpu_custom_call" | custom-call | flops 536870912 | bytes 8388608 | tf_op jit(solution)/shard_map/message_grad/pallas_call | solution.py:46
  68.7 5.2 %all-to-all-start = ((bf16[8,64,256]{2,1,0:T(8,128)(2,1)}), bf16[8,64,256]{2,1,0:T(8,128)(2,1)S(1)}, u32[]{:S(2)}, u32[]{:S(2)}) async-start(bf16[8,64,256]{2,1,0:T(8,128)(2,1)} %d_out.1), calls=%async_computation | async-start | bytes 524288 | tf_op jit(solution)/shard_map/all_to_all | solution.py:360
  74.0 14.5 %attend_forward.1 = (bf16[8,192,256]{2,1,0:T(8,128)(2,1)}, bf16[8,256,128]{2,1,0:T(8,128)(2,1)}, bf16[8,64,256]{2,1,0:T(8,128)(2,1)}, bf16[8,64,256]{2,1,0:T(8,1...) custom-call(s32[2]{0:T(128)} %pad_add_fusion.place_ref.refs_0_, ...), custom_call_target="tpu_custom_call" | custom-call | flops 3221225472 | bytes 8388608 | tf_op jit(solution)/shard_map/attend_forward/pallas_call | solution.py:46
  88.5 7.2 %all-to-all-start.1 = ((bf16[8,192,256]{2,1,0:T(8,128)(2,1)}), bf16[8,192,256]{2,1,0:T(8,128)(2,1)S(1)}, u32[]{:S(2)}, u32[]{:S(2)}) async-start(bf16[8,192,256]{2,1,0:T(8,128)(2,1)} %get-tuple-element.94), calls=%async_computation.1 | async-start | bytes 1572864 | tf_op jit(solution)/shard_map/all_to_all | solution.py:360
  95.7 16.7 %attend_backward.1 = (bf16[192,256]{1,0:T(8,128)(2,1)}, bf16[192,256]{1,0:T(8,128)(2,1)}, bf16[192,256]{1,0:T(8,128)(2,1)}, bf16[192,256]{1,0:T(8,128)(2,1)}, bf...) custom-call(s32[2]{0:T(128)} %pad_add_fusion.place_ref.refs_0_, ...), custom_call_target="tpu_custom_call" | custom-call | flops 6442450944 | bytes 8388608 | tf_op jit(solution)/shard_map/attend_backward/pallas_call | solution.py:46
  115.1 6.2 %result.1 = (bf16[256,1024]{1,0:T(8,128)(2,1)}, bf16[16,160,128]{2,1,0:T(8,128)(2,1)}, bf16[16,160,128]{2,1,0:T(8,128)(2,1)}) custom-call(s32[2]{0:T(128)} %pad_add_fusion.place_ref.refs_0_, bf16[256,1024]{1,0:T(8,128)(2,1)} %normalize.1.refs_4_.refs_1_, bf16[256,1024]{1,0:T(8,128)(2,1)} %copy-done.6, bf16[256,1024]{1,0:T(8,128)(2,1)} %copy-done.8, ...), custom_call_target="tpu_custom_call" | custom-call | flops 1610612736 | bytes 10485760 | tf_op jit(solution)/shard_map/result/pallas_call | solution.py:46
  124.8 2.6 %pair_sum.1 = bf16[16,224,128]{2,1,0:T(8,128)(2,1)} custom-call(bf16[16,64,128]{2,1,0:T(8,128)(2,1)} %get-tuple-element.102.keep_a, bf16[16,64,128]{2,1,0:T(8,128)(2,1)} %copy-done.15, bf16[16,160,128]{2,1,0:T(8,128)(2,1)} %get-tuple-element.107.keep_b, bf16[16,160,128]{2,1,0:T(8,128)(2,1)} %copy-done.5), custom_call_target="tpu_custom_call" | custom-call | bytes 3145728 | tf_op jit(solution)/shard_map/pair_sum/pallas_call | solution.py:46
  127.5 7.4 %all-to-all-start.2 = ((bf16[16,224,128]{2,1,0:T(8,128)(2,1)}), bf16[16,224,128]{2,1,0:T(8,128)(2,1)S(1)}, u32[]{:S(2)}, u32[]{:S(2)}) async-start(bf16[16,224,128]{2,1,0:T(8,128)(2,1)} %pair_sum.1), calls=%async_computation.2 | async-start | bytes 1835008 | tf_op jit(solution)/shard_map/all_to_all | solution.py:360
  140.3 3.6 %collective-permute-start.15 = (bf16[192,256]{1,0:T(8,128)(2,1)S(1)}, bf16[192,256]{1,0:T(8,128)(2,1)S(1)}, u32[]{:S(2)}, u32[]{:S(2)}) collective-permute-start(bf16[192,256]{1,0:T(8,128)(2,1)S(1)} %copy-done.27), channel_id=1, source_target_pairs={{0,4},{1,5},{2,6},{3,7},{4,0},{5,1},{6,2},{7,3},{8,12},{9,13},{10,... | collective-permute-start | bytes 294920 | tf_op jit(solution)/shard_map/ppermute | solution.py:364
  145.9 4.4 %collective-permute-done.14.refs_4_ = bf16[192,256]{1,0:T(8,128)(2,1)S(1)} collective-permute-done((bf16[192,256]{1,0:T(8,128)(2,1)S(1)}, bf16[192,256]{1,0:T(8,128)(2,1)S(1)}, u32[]{:S(2)}, u32[]{:S(2)}) %collective-permute-start.14) | collective-permute-done | bytes 98336 | tf_op jit(solution)/shard_map/ppermute | solution.py:364
  153.4 9.8 %all-to-all-start.3 = ((bf16[8,224,128]{2,1,0:T(8,128)(2,1)}), bf16[8,224,128]{2,1,0:T(8,128)(2,1)S(1)}, u32[]{:S(2)}, u32[]{:S(2)}) async-start(bf16[8,224,128]{2,1,0:T(8,128)(2,1)} %share_sum.1), calls=%async_computation.3 | async-start | bytes 917504 | tf_op jit(solution)/shard_map/all_to_all | solution.py:360
  166.2 3.8 %collective-permute-start.16 = (bf16[192,256]{1,0:T(8,128)(2,1)S(1)}, bf16[192,256]{1,0:T(8,128)(2,1)S(1)}, u32[]{:S(2)}, u32[]{:S(2)}) collective-permute-start(bf16[192,256]{1,0:T(8,128)(2,1)S(1)} %copy-done.26), channel_id=1, source_target_pairs={{0,3},{1,4},{2,5},{3,6},{4,7},{5,0},{6,1},{7,2},{8,11},{9,12},{10,... | collective-permute-start | bytes 294920 | tf_op jit(solution)/shard_map/ppermute | solution.py:364
  170.0 2.7 %collective-permute-start.17 = (bf16[192,256]{1,0:T(8,128)(2,1)S(1)}, bf16[192,256]{1,0:T(8,128)(2,1)S(1)}, u32[]{:S(2)}, u32[]{:S(2)}) collective-permute-start(bf16[192,256]{1,0:T(8,128)(2,1)S(1)} %copy-done.25), channel_id=1, source_target_pairs={{0,2},{1,3},{2,4},{3,5},{4,6},{5,7},{6,0},{7,1},{8,10},{9,11},{10,... | collective-permute-start | bytes 294920 | tf_op jit(solution)/shard_map/ppermute | solution.py:364
  174.7 12.1 %collective-permute-done.16.refs_6_ = bf16[192,256]{1,0:T(8,128)(2,1)S(1)} collective-permute-done((bf16[192,256]{1,0:T(8,128)(2,1)S(1)}, bf16[192,256]{1,0:T(8,128)(2,1)S(1)}, u32[]{:S(2)}, u32[]{:S(2)}) %collective-permute-start.16) | collective-permute-done | bytes 98336 | tf_op jit(solution)/shard_map/ppermute | solution.py:364
  189.2 5.0 %input_grad.1 = bf16[256,1024]{1,0:T(8,128)(2,1)} custom-call(s32[2]{0:T(128)} %pad_add_fusion.place_ref.refs_0_, bf16[192,256]{1,0:T(8,128)(2,1)} %get-tuple-element.123.refs_1_, bf16[192,256]{1,0:T(8,128)(2,1)} %copy-done.16, bf16[192,256]{1,0:T(8,128)(2,1)} %copy-done.17, bf16[192,256]{1,0:T(8,128)(2,1)} %copy-done.18, bf16[192,256]{1,0:T(8,128)(2,1)} %copy-done.19, ...), custom_call_target="tpu_custom_call" | custom-call | flops 805306368 | bytes 8388608 | tf_op jit(solution)/shard_map/input_grad/pallas_call | solution.py:46
  (104 shorter events, 43.8 us)
Async XLA Ops:
  2.7 18.0 %collective-permute-start = (bf16[256,1024]{1,0:T(8,128)(2,1)}, bf16[256,1024]{1,0:T(8,128)(2,1)S(1)}, u32[]{:S(2)}, u32[]{:S(2)}) collective-permute-start(bf16[256,1024]{1,0:T(8,128)(2,1)} %normalize.1.refs_4_.refs_1_), channel_id=1, source_target_pairs={{0,1},{1,2},{2,3},{3,4},{4,5},{5,6},{6,7},{7,0},{8,9},{9,10},{10,1... | collective-permute-start | bytes 1572872 | tf_op jit(solution)/shard_map/ppermute | solution.py:364
  4.6 16.1 %collective-permute-start.1 = (bf16[256,1024]{1,0:T(8,128)(2,1)}, bf16[256,1024]{1,0:T(8,128)(2,1)S(1)}, u32[]{:S(2)}, u32[]{:S(2)}) collective-permute-start(bf16[256,1024]{1,0:T(8,128)(2,1)} %normalize.1.refs_4_.refs_1_), channel_id=1, source_target_pairs={{0,7},{1,0},{2,1},{3,2},{4,3},{5,4},{6,5},{7,6},{8,15},{9,8},{10,9... | collective-permute-start | bytes 1572872 | tf_op jit(solution)/shard_map/ppermute | solution.py:364
  20.7 14.4 %collective-permute-start.2 = (bf16[256,1024]{1,0:T(8,128)(2,1)S(1)}, bf16[256,1024]{1,0:T(8,128)(2,1)S(1)}, u32[]{:S(2)}, u32[]{:S(2)}) collective-permute-start(bf16[256,1024]{1,0:T(8,128)(2,1)S(1)} %collective-permute-done.refs_3_.refs_2_), channel_id=1, source_target_pairs={{0,1},{1,2},{2,3},{3,4},{4,5},{5,6},{6,7},{7,0},{8,9},{9,10},{10,1... | collective-permute-start | bytes 1572872 | tf_op jit(solution)/shard_map/ppermute | solution.py:364
  20.8 14.3 %collective-permute-start.3 = (bf16[256,1024]{1,0:T(8,128)(2,1)S(1)}, bf16[256,1024]{1,0:T(8,128)(2,1)S(1)}, u32[]{:S(2)}, u32[]{:S(2)}) collective-permute-start(bf16[256,1024]{1,0:T(8,128)(2,1)S(1)} %collective-permute-done.1.refs_5_.refs_9_), channel_id=1, source_target_pairs={{0,7},{1,0},{2,1},{3,2},{4,3},{5,4},{6,5},{7,6},{8,15},{9,8},{10,9... | collective-permute-start | bytes 1572872 | tf_op jit(solution)/shard_map/ppermute | solution.py:364
  35.1 16.1 %collective-permute-start.4 = (bf16[256,1024]{1,0:T(8,128)(2,1)S(1)}, bf16[256,1024]{1,0:T(8,128)(2,1)S(1)}, u32[]{:S(2)}, u32[]{:S(2)}) collective-permute-start(bf16[256,1024]{1,0:T(8,128)(2,1)S(1)} %collective-permute-done.2.refs_3_), channel_id=1, source_target_pairs={{0,1},{1,2},{2,3},{3,4},{4,5},{5,6},{6,7},{7,0},{8,9},{9,10},{10,1... | collective-permute-start | bytes 1572872 | tf_op jit(solution)/shard_map/ppermute | solution.py:364
  36.8 14.9 %collective-permute-start.5 = (bf16[256,1024]{1,0:T(8,128)(2,1)S(1)}, bf16[256,1024]{1,0:T(8,128)(2,1)S(1)}, u32[]{:S(2)}, u32[]{:S(2)}) collective-permute-start(bf16[256,1024]{1,0:T(8,128)(2,1)S(1)} %collective-permute-done.3.refs_8_), channel_id=1, source_target_pairs={{0,7},{1,0},{2,1},{3,2},{4,3},{5,4},{6,5},{7,6},{8,15},{9,8},{10,9... | collective-permute-start | bytes 1572872 | tf_op jit(solution)/shard_map/ppermute | solution.py:364
  38.4 20.9 %collective-permute-start.6 = (bf16[256,1024]{1,0:T(8,128)(2,1)}, bf16[256,1024]{1,0:T(8,128)(2,1)S(1)}, u32[]{:S(2)}, u32[]{:S(2)}) collective-permute-start(bf16[256,1024]{1,0:T(8,128)(2,1)} %get-tuple-element.78), channel_id=1, source_target_pairs={{0,7},{1,0},{2,1},{3,2},{4,3},{5,4},{6,5},{7,6},{8,15},{9,8},{10,9... | collective-permute-start | bytes 1572872 | tf_op jit(solution)/shard_map/ppermute | solution.py:364
  40.1 19.7 %collective-permute-start.7 = (bf16[256,1024]{1,0:T(8,128)(2,1)}, bf16[256,1024]{1,0:T(8,128)(2,1)S(1)}, u32[]{:S(2)}, u32[]{:S(2)}) collective-permute-start(bf16[256,1024]{1,0:T(8,128)(2,1)} %get-tuple-element.79), channel_id=1, source_target_pairs={{0,1},{1,2},{2,3},{3,4},{4,5},{5,6},{6,7},{7,0},{8,9},{9,10},{10,1... | collective-permute-start | bytes 1572872 | tf_op jit(solution)/shard_map/ppermute | solution.py:364
  59.8 8.2 %collective-permute-start.8 = (bf16[128,1024]{1,0:T(8,128)(2,1)S(1)}, bf16[128,1024]{1,0:T(8,128)(2,1)S(1)}, u32[]{:S(2)}, u32[]{:S(2)}) collective-permute-start(bf16[128,1024]{1,0:T(8,128)(2,1)S(1)} %slice.6), channel_id=1, source_target_pairs={{0,1},{1,2},{2,3},{3,4},{4,5},{5,6},{6,7},{7,0},{8,9},{9,10},{10,1... | collective-permute-start | bytes 786440 | tf_op jit(solution)/shard_map/ppermute | solution.py:364
  62.1 6.6 %collective-permute-start.9 = (bf16[128,1024]{1,0:T(8,128)(2,1)}, bf16[128,1024]{1,0:T(8,128)(2,1)S(1)}, u32[]{:S(2)}, u32[]{:S(2)}) collective-permute-start(bf16[128,1024]{1,0:T(8,128)(2,1)} %slice.7), channel_id=1, source_target_pairs={{0,7},{1,0},{2,1},{3,2},{4,3},{5,4},{6,5},{7,6},{8,15},{9,8},{10,9... | collective-permute-start | bytes 786440 | tf_op jit(solution)/shard_map/ppermute | solution.py:364
  68.7 19.8 %all-to-all-start = ((bf16[8,64,256]{2,1,0:T(8,128)(2,1)}), bf16[8,64,256]{2,1,0:T(8,128)(2,1)S(1)}, u32[]{:S(2)}, u32[]{:S(2)}) async-start(bf16[8,64,256]{2,1,0:T(8,128)(2,1)} %d_out.1), calls=%async_computation | async-start | bytes 524288 | tf_op jit(solution)/shard_map/all_to_all | solution.py:360
  88.5 25.7 %all-to-all-start.1 = ((bf16[8,192,256]{2,1,0:T(8,128)(2,1)}), bf16[8,192,256]{2,1,0:T(8,128)(2,1)S(1)}, u32[]{:S(2)}, u32[]{:S(2)}) async-start(bf16[8,192,256]{2,1,0:T(8,128)(2,1)} %get-tuple-element.94), calls=%async_computation.1 | async-start | bytes 1572864 | tf_op jit(solution)/shard_map/all_to_all | solution.py:360
  121.3 2.6 %collective-permute-start.11 = (bf16[16,160,128]{2,1,0:T(8,128)(2,1)}, bf16[16,160,128]{2,1,0:T(8,128)(2,1)S(1)}, u32[]{:S(2)}, u32[]{:S(2)}) collective-permute-start(bf16[16,160,128]{2,1,0:T(8,128)(2,1)} %get-tuple-element.108), channel_id=1, source_target_pairs={{0,8},{8,0},{1,9},{9,1},{2,10},{10,2},{3,11},{11,3},{4,12},{12,4},... | collective-permute-start | bytes 1966088 | tf_op jit(solution)/shard_map/ppermute | solution.py:472
  121.5 2.5 %collective-permute-start.10 = (bf16[16,64,128]{2,1,0:T(8,128)(2,1)S(1)}, bf16[16,64,128]{2,1,0:T(8,128)(2,1)S(1)}, u32[]{:S(2)}, u32[]{:S(2)}) collective-permute-start(bf16[16,64,128]{2,1,0:T(8,128)(2,1)S(1)} %copy-done.23), channel_id=1, source_target_pairs={{0,8},{8,0},{1,9},{9,1},{2,10},{10,2},{3,11},{11,3},{4,12},{12,4},... | collective-permute-start | bytes 786440 | tf_op jit(solution)/shard_map/ppermute | solution.py:460
  124.8 47.8 %copy-start.24 = (bf16[192,256]{1,0:T(8,128)(2,1)S(1)}, bf16[192,256]{1,0:T(8,128)(2,1)}, u32[]{:S(2)}) copy-start(bf16[192,256]{1,0:T(8,128)(2,1)} %get-tuple-element.130) | copy-start | bytes 294916
  127.5 22.9 %all-to-all-start.2 = ((bf16[16,224,128]{2,1,0:T(8,128)(2,1)}), bf16[16,224,128]{2,1,0:T(8,128)(2,1)S(1)}, u32[]{:S(2)}, u32[]{:S(2)}) async-start(bf16[16,224,128]{2,1,0:T(8,128)(2,1)} %pair_sum.1), calls=%async_computation.2 | async-start | bytes 1835008 | tf_op jit(solution)/shard_map/all_to_all | solution.py:360
  134.9 8.9 %collective-permute-start.12 = (bf16[192,256]{1,0:T(8,128)(2,1)S(1)}, bf16[192,256]{1,0:T(8,128)(2,1)S(1)}, u32[]{:S(2)}, u32[]{:S(2)}) collective-permute-start(bf16[192,256]{1,0:T(8,128)(2,1)S(1)} %copy-done.30), channel_id=1, source_target_pairs={{0,7},{1,0},{2,1},{3,2},{4,3},{5,4},{6,5},{7,6},{8,15},{9,8},{10,9... | collective-permute-start | bytes 294920 | tf_op jit(solution)/shard_map/ppermute | solution.py:364
  136.5 9.5 %collective-permute-start.13 = (bf16[192,256]{1,0:T(8,128)(2,1)S(1)}, bf16[192,256]{1,0:T(8,128)(2,1)S(1)}, u32[]{:S(2)}, u32[]{:S(2)}) collective-permute-start(bf16[192,256]{1,0:T(8,128)(2,1)S(1)} %copy-done.29), channel_id=1, source_target_pairs={{0,6},{1,7},{2,0},{3,1},{4,2},{5,3},{6,4},{7,5},{8,14},{9,15},{10,... | collective-permute-start | bytes 294920 | tf_op jit(solution)/shard_map/ppermute | solution.py:364
  138.8 11.5 %collective-permute-start.14 = (bf16[192,256]{1,0:T(8,128)(2,1)S(1)}, bf16[192,256]{1,0:T(8,128)(2,1)S(1)}, u32[]{:S(2)}, u32[]{:S(2)}) collective-permute-start(bf16[192,256]{1,0:T(8,128)(2,1)S(1)} %copy-done.28), channel_id=1, source_target_pairs={{0,5},{1,6},{2,7},{3,0},{4,1},{5,2},{6,3},{7,4},{8,13},{9,14},{10,... | collective-permute-start | bytes 294920 | tf_op jit(solution)/shard_map/ppermute | solution.py:364
  140.3 10.1 %collective-permute-start.15 = (bf16[192,256]{1,0:T(8,128)(2,1)S(1)}, bf16[192,256]{1,0:T(8,128)(2,1)S(1)}, u32[]{:S(2)}, u32[]{:S(2)}) collective-permute-start(bf16[192,256]{1,0:T(8,128)(2,1)S(1)} %copy-done.27), channel_id=1, source_target_pairs={{0,4},{1,5},{2,6},{3,7},{4,0},{5,1},{6,2},{7,3},{8,12},{9,13},{10,... | collective-permute-start | bytes 294920 | tf_op jit(solution)/shard_map/ppermute | solution.py:364
  153.4 40.8 %all-to-all-start.3 = ((bf16[8,224,128]{2,1,0:T(8,128)(2,1)}), bf16[8,224,128]{2,1,0:T(8,128)(2,1)S(1)}, u32[]{:S(2)}, u32[]{:S(2)}) async-start(bf16[8,224,128]{2,1,0:T(8,128)(2,1)} %share_sum.1), calls=%async_computation.3 | async-start | bytes 917504 | tf_op jit(solution)/shard_map/all_to_all | solution.py:360
  166.2 20.6 %collective-permute-start.16 = (bf16[192,256]{1,0:T(8,128)(2,1)S(1)}, bf16[192,256]{1,0:T(8,128)(2,1)S(1)}, u32[]{:S(2)}, u32[]{:S(2)}) collective-permute-start(bf16[192,256]{1,0:T(8,128)(2,1)S(1)} %copy-done.26), channel_id=1, source_target_pairs={{0,3},{1,4},{2,5},{3,6},{4,7},{5,0},{6,1},{7,2},{8,11},{9,12},{10,... | collective-permute-start | bytes 294920 | tf_op jit(solution)/shard_map/ppermute | solution.py:364
  170.0 17.7 %collective-permute-start.17 = (bf16[192,256]{1,0:T(8,128)(2,1)S(1)}, bf16[192,256]{1,0:T(8,128)(2,1)S(1)}, u32[]{:S(2)}, u32[]{:S(2)}) collective-permute-start(bf16[192,256]{1,0:T(8,128)(2,1)S(1)} %copy-done.25), channel_id=1, source_target_pairs={{0,2},{1,3},{2,4},{3,5},{4,6},{5,7},{6,0},{7,1},{8,10},{9,11},{10,... | collective-permute-start | bytes 294920 | tf_op jit(solution)/shard_map/ppermute | solution.py:364
  172.7 15.9 %collective-permute-start.18 = (bf16[192,256]{1,0:T(8,128)(2,1)S(1)}, bf16[192,256]{1,0:T(8,128)(2,1)S(1)}, u32[]{:S(2)}, u32[]{:S(2)}) collective-permute-start(bf16[192,256]{1,0:T(8,128)(2,1)S(1)} %copy-done.24), channel_id=1, source_target_pairs={{0,1},{1,2},{2,3},{3,4},{4,5},{5,6},{6,7},{7,0},{8,9},{9,10},{10,1... | collective-permute-start | bytes 294920 | tf_op jit(solution)/shard_map/ppermute | solution.py:364
  (30 other events, 485.8 us)

commit v3 on v2

--- a/solution.py
+++ b/solution.py
@@ -49,7 +49,7 @@
         in_specs=specs,
         out_specs=tuple(pl.BlockSpec(memory_space=pltpu.VMEM) for _ in out_shape),
         scratch_shapes=list(scratch),
-        compiler_params=pltpu.CompilerParams(vmem_limit_bytes=60 * 1024 * 1024),
+        compiler_params=pltpu.CompilerParams(vmem_limit_bytes=62 * 1024 * 1024),
         cost_estimate=pl.CostEstimate(flops=flops, bytes_accessed=moved, transcendentals=exps),
         name=name,
     )(*scalars, *far, *arrays)
@@ -212,13 +212,9 @@
 
 
 def backward_kernel(*refs):
-    place_ref = refs[0]
-    kv_ref, hq_ref, ku_ref, raw_ref, head_ref, stats_ref, d_ref = refs[10:17]
-    stacks = refs[17:25]
-    keep_ref, give_ref = refs[25:27]
-    sums, dqt, grad_t, grad, held, sems = refs[27:33]
-    wait = fetch_chunks(refs[1:10], held, sems)
-    z = place_ref[0]
+    z = refs[0][0]
+    kv_ref, hq_ref, ku_ref, raw_ref, head_ref, stats_ref, d_ref = refs[1:8]
+    stack_ref, sums, dqt = refs[8:]
     sums[...] = jnp.zeros_like(sums)
 
     def step(i, carry):
@@ -252,22 +248,13 @@
             mean = jnp.mean(d_unit * wide, axis=0, keepdims=True)
             pieces.append(factor * d_unit - factor * factor * factor * wide * mean)
         stacked = jnp.concatenate(pieces + [turned[HEAD_DIM:]], axis=0).astype(jnp.bfloat16)
-        stacks[j][...] = stacked
-        wait(j)
-        term = matmul(stacked, held[j])
-        if j == 0:
-            grad_t[: 3 * HEAD_DIM] = term
-        else:
-            grad_t[: 3 * HEAD_DIM] += term
-    grad_t[3 * HEAD_DIM :] = jnp.zeros((HEAD_DIM, grad_t.shape[1]), jnp.float32)
-    grad[...] = grad_t[...].T
-    split_rows(place_ref[1], grad, keep_ref, give_ref)
+        stack_ref[place_of(z, j)] = stacked
 
 
 def result_kernel(*refs):
     place_ref = refs[0]
-    home_ref, w_ref, grad_ref, x_ref, act_ref = refs[10:15]
-    out_ref, keep_ref, give_ref, grad_t, grad_msg, grad_out, held, sems = refs[15:]
+    home_ref, stack_ref, w_ref, grad_ref, x_ref, act_ref = refs[10:16]
+    out_ref, keep_ref, give_ref, grad_t, grad_node, grad_out, held, sems = refs[16:]
     wait = fetch_chunks(refs[1:10], held, sems)
     z = place_ref[0]
     every = jnp.concatenate([home_ref[h, :HEAD_DIM] for h in range(N_SEQ)], axis=0)
@@ -275,24 +262,20 @@
     for j in range(N_SEQ):
         folded = home_ref[place_of(z, j), HEAD_DIM:].astype(jnp.float32)
         columns = jnp.concatenate([folded[:, :BLOCK].T, folded[:, BLOCK:].T], axis=1)
+        d_head = stack_ref[place_of(z, j)]
+        pad = jnp.zeros((HEAD_DIM, CHUNK), jnp.bfloat16)
+        both = jnp.concatenate([d_head, pad, columns.astype(jnp.bfloat16)], axis=0)
         wait(j)
-        term = matmul(columns.astype(jnp.bfloat16), held[j])
+        term = matmul(both, held[j])
         if j == 0:
             grad_t[...] = term
         else:
             grad_t[...] += term
-    grad_msg[...] = grad_t[...].T
-    split_rows(place_ref[1], grad_msg, keep_ref, give_ref)
-    split_rows(place_ref[1], grad_out, keep_ref, give_ref, grad_msg.shape[0] // (2 * N_XY))
+    grad_node[...] = grad_t[...].T
+    split_rows(place_ref[1], grad_node, keep_ref, give_ref)
+    split_rows(place_ref[1], grad_out, keep_ref, give_ref, 3 * (grad_node.shape[0] // (2 * N_XY)))
     attn = contract_rows(every, w_ref[...])
     out_ref[...] = (x_ref[...].astype(jnp.float32) + attn + act_ref[...]).astype(jnp.bfloat16)
-
-
-def pair_kernel(keep_a, got_a, keep_b, got_b, out_ref):
-    cut = keep_a.shape[1]
-    for i in range(N_XY):
-        out_ref[i, :cut] = (keep_a[i].astype(jnp.float32) + got_a[i].astype(jnp.float32)).astype(jnp.bfloat16)
-        out_ref[i, cut:] = (keep_b[i].astype(jnp.float32) + got_b[i].astype(jnp.float32)).astype(jnp.bfloat16)
 
 
 def share_kernel(shares_ref, out_ref):
@@ -327,23 +310,15 @@
     half_rows = out_ref.shape[0]
     for t in range(N_SEQ):
         out_ref[:, t * BLOCK : (t + 1) * BLOCK] = total[t * half_rows : (t + 1) * half_rows] * (1.0 / nodes)
-    gain_out_ref[...] = jnp.sum(gain_sum, axis=1, keepdims=True) / gain_ref[...]
+    gain_out_ref[...] = jnp.sum(gain_sum.T, axis=0, keepdims=True) / gain_ref[...]
 
 
 def input_grad_kernel(*refs):
-    place_ref = refs[0]
-    stacks = refs[1:9]
-    w_ref, d_norm_ref, x_ref, grad_ref, gain_ref = refs[9:14]
-    out_ref, gathered = refs[14:]
-    z = place_ref[0]
-    hd = N_SEQ * HEAD_DIM
-    for j in range(N_SEQ):
-        head = lax.rem(z + j, N_SEQ)
-        for t in range(3):
-            gathered[pl.ds(t * hd + head * HEAD_DIM, HEAD_DIM), :] = stacks[j][
-                t * HEAD_DIM : (t + 1) * HEAD_DIM
-            ]
-    d_norm = matmul(w_ref[...], gathered[...]).T + d_norm_ref[...]
+    stack_ref, w_ref, d_norm_ref, x_ref, grad_ref, gain_ref, out_ref = refs
+    parts = [
+        stack_ref[h, t * HEAD_DIM : (t + 1) * HEAD_DIM] for t in range(3) for h in range(N_SEQ)
+    ]
+    d_norm = matmul(w_ref[...], jnp.concatenate(parts, axis=0)).T + d_norm_ref[...]
     wide = x_ref[...].astype(jnp.float32)
     inv_rms = unit_factor(wide, -1)
     x_hat = wide * inv_rms
@@ -442,52 +417,38 @@
 
     rows_here = width // (2 * N_XY)
     rows_out = hd // (2 * N_XY)
-    part_head = ((N_XY, 2 * rows_here, BLOCK), bf16)
-    *stacks, keep, give = call(
-        backward_kernel, "attend_backward",
-        (((3 * HEAD_DIM, CHUNK), bf16),) * N_SEQ + (part_head, part_head),
+    (stack,) = call(
+        backward_kernel, "attend_backward", (((N_SEQ, 3 * HEAD_DIM, CHUNK), bf16),),
         (place,), (*saved, d_heads),
+        [pltpu.VMEM((N_SEQ, CHUNK, 2 * HEAD_DIM), f32), pltpu.VMEM((N_SEQ, HEAD_DIM, CHUNK), f32)],
+        flops=24 * nodes * nodes * HEAD_DIM, exps=nodes * nodes, moved=4 << 20,
+    )
+    stack, home = lax.optimization_barrier((stack, home))
+    stack_home = exchange(stack, "z")
+
+    all_rows = 3 * rows_here + rows_out * width // BLOCK
+    part = ((N_XY, all_rows, BLOCK), bf16)
+    block_result_array, keep, give = call(
+        result_kernel, "result", (low_shape, part, part), (place,),
+        (home, stack, w_out, out_grad, features, act),
         [
-            pltpu.VMEM((N_SEQ, CHUNK, 2 * HEAD_DIM), f32),
-            pltpu.VMEM((N_SEQ, HEAD_DIM, CHUNK), f32),
-            pltpu.VMEM((4 * HEAD_DIM, width), f32),
-            pltpu.VMEM((width, 4 * HEAD_DIM), f32),
-            held,
-            pltpu.SemaphoreType.DMA((9,)),
+            pltpu.VMEM((3 * BLOCK, width), f32), pltpu.VMEM((width, 3 * BLOCK), f32),
+            pltpu.VMEM((hd, width), f32), held, pltpu.SemaphoreType.DMA((9,)),
         ],
-        flops=24 * nodes * nodes * HEAD_DIM, exps=nodes * nodes, moved=8 << 20, far=chunks,
+        flops=8 * node_rows * width * width, moved=10 << 20, far=chunks,
     )
     got = lax.ppermute(give, "c", [(0, 1), (1, 0)])
-
-    part_out = ((N_XY, rows_here + rows_out * width // BLOCK, BLOCK), bf16)
-    block_result_array, keep_out, give_out = call(
-        result_kernel, "result", (low_shape, part_out, part_out), (place,),
-        (after(home, keep), w_out, out_grad, features, act),
-        [
-            pltpu.VMEM((BLOCK, width), f32), pltpu.VMEM((width, BLOCK), f32), pltpu.VMEM((hd, width), f32),
-            held, pltpu.SemaphoreType.DMA((9,)),
-        ],
-        flops=6 * node_rows * width * width, moved=10 << 20, far=chunks,
-    )
-    got_out = lax.ppermute(give_out, "c", [(0, 1), (1, 0)])
-    all_rows = part_head[0][1] + part_out[0][1]
-    (pair,) = call(
-        pair_kernel, "pair_sum", (((N_XY, all_rows, BLOCK), bf16),), (), (keep, got, keep_out, got_out),
-        moved=3 << 20,
-    )
-    pair, *stacks = lax.optimization_barrier((pair, *stacks))
+    pair = (keep.astype(f32) + got.astype(f32)).astype(bf16)
+    pair, stack_home = lax.optimization_barrier((pair, stack_home))
     shares = exchange(pair, ("x", "y"))
-    stacks = [stacks[0]] + [shift(stacks[j], -j) for j in range(1, N_SEQ)]
-    shares, *stacks[1:5] = lax.optimization_barrier((shares, *stacks[1:5]))
     (mine,) = call(
         share_kernel, "share_sum", (((N_SEQ, all_rows, BLOCK), bf16),), (), (shares,), moved=2 << 20,
     )
     every = exchange(mine, "z")
 
     (grad_input,) = call(
-        input_grad_kernel, "input_grad", (low_shape,), (place,),
-        (*stacks, w_qkv, d_norm, features, out_grad, gain),
-        [pltpu.VMEM((3 * hd, node_rows), bf16)],
+        input_grad_kernel, "input_grad", (low_shape,), (),
+        (after(stack_home, mine), w_qkv, d_norm, features, out_grad, gain),
         flops=6 * node_rows * width * hd, moved=8 << 20,
     )
 
@@ -495,10 +456,10 @@
     first = ((lax.axis_index("x") * 4 + lax.axis_index("y")) * 2 + core) * rows_here
     w_rows = lax.dynamic_slice_in_dim(w_qkv, first, rows_here, 0)
     m_rows = lax.dynamic_slice_in_dim(w_msg, first, rows_here, 0)
-    gain_rows = lax.dynamic_slice_in_dim(norm_gain, first, rows_here, 0).reshape(rows_here, 1)
+    gain_rows = lax.dynamic_slice_in_dim(norm_gain, first, rows_here, 0).reshape(1, rows_here)
     grad_qkv, grad_out, grad_msg, grad_gain = call(
         finish_kernel, "finish",
-        (((rows_here, 3 * hd), f32), ((rows_out, width), f32), ((rows_here, width), f32), ((rows_here, 1), f32)),
+        (((rows_here, 3 * hd), f32), ((rows_out, width), f32), ((rows_here, width), f32), ((1, rows_here), f32)),
         (), (every, w_rows, m_rows, gain_rows), moved=2 << 20,
     )
     return block_result_array, grad_input, grad_gain.reshape(rows_here), grad_qkv, grad_out, grad_msg

time: 199 us -> 181 us (0.910)
  starting transfers between devices: 64 us -> 39.9 us
  blocking collectives: 0 us -> 17.4 us
  waiting for transfers between devices: 54.1 us -> 47.2 us
  Pallas kernels: 67.8 us -> 65 us
  local copies, waits for them, and re-layouts: 9.52 us -> 7.34 us
    ppermute x17 -> x10, waiting for transfers between devices: 50.4 us -> 29.9 us  [shift(): lax.ppermute(array, 'z', [(i, (i + distance) % N_SEQ) for i in range(N_SE...]
    all_to_all x0 -> x1, blocking collectives: none -> 17.4 us  [exchange(): return lax.all_to_all(array, axis, split_axis=0, concat_axis=0, tiled=True)]
    ppermute x17 -> x10, starting transfers between devices: 33.8 us -> 17.7 us  [shift(): lax.ppermute(array, 'z', [(i, (i + distance) % N_SEQ) for i in range(N_SE...]
    all_to_all x4, waiting for transfers between devices: 1.77 us -> 14.6 us  [exchange(): return lax.all_to_all(array, axis, split_axis=0, concat_axis=0, tiled=True)]
    all_to_all x4, starting transfers between devices: 29.6 us -> 22.1 us  [exchange(): return lax.all_to_all(array, axis, split_axis=0, concat_axis=0, tiled=True)]
    pallas_call x11 -> x10, Pallas kernels: 64.8 us -> 62 us  [call(): pl.pallas_call(kernel, out_shape=tuple((jax.ShapeDtypeStruct(s, t) for s,...]
    unnamed x62 -> x22, local copies, waits for them, and re-layouts: 4.3 us -> 1.6 us
  transfers between devices with their start and end apart: 23 -> 15, of which waited for: 14 -> 10; matrix products, arithmetic and copies ran while one was open for 3% -> 4% of each run, Pallas kernels for 27% -> 33%
where the time goes in v3:
time: 181 us; the launch traced here: 179 us
  Pallas kernels  65 us (36%)
  waiting for transfers between devices  47.2 us (26%)
  starting transfers between devices  39.9 us (22%)
  blocking collectives  17.4 us (10%)
  local copies, waits for them, and re-layouts  7.34 us (4%)
  other arithmetic  2 us (1%)
    pallas_call x10, Pallas kernels, call(): pl.pallas_call(kernel, out_shape=tuple((jax.ShapeDtypeStruct(s, t) for s,...  62 us
    ppermute x10, waiting for transfers between devices, shift(): lax.ppermute(array, 'z', [(i, (i + distance) % N_SEQ) for i in range(N_SE...  29.9 us
    all_to_all x4, starting transfers between devices, exchange(): return lax.all_to_all(array, axis, split_axis=0, concat_axis=0, tiled=True)  22.1 us
    ppermute x10, starting transfers between devices, shift(): lax.ppermute(array, 'z', [(i, (i + distance) % N_SEQ) for i in range(N_SE...  17.7 us
    all_to_all x1, blocking collectives, exchange(): return lax.all_to_all(array, axis, split_axis=0, concat_axis=0, tiled=True)  17.4 us
    all_to_all x4, waiting for transfers between devices, exchange(): return lax.all_to_all(array, axis, split_axis=0, concat_axis=0, tiled=True)  14.6 us
  transfers between devices with their start and end apart: 15, of which 10 were waited for; matrix products, arithmetic and copies ran while one was open for 4% of the time, Pallas kernels for 33%

profile of v3, /device:TPU:6, one launch (start us, length us, event | category | flops | bytes accessed | tf_op | source)
XLA Modules:
  0.0 179.5 jit_solution(7165449071182355453)
XLA Ops:
  4.6 3.9 %collective-permute-start.1 = (bf16[256,1024]{1,0:T(8,128)(2,1)}, bf16[256,1024]{1,0:T(8,128)(2,1)S(1)}, u32[]{:S(2)}, u32[]{:S(2)}) collective-permute-start(bf16[256,1024]{1,0:T(8,128)(2,1)} %normalize.1.refs_4_.refs_1_), channel_id=1, source_target_pairs={{0,7},{1,0},{2,1},{3,2},{4,3},{5,4},{6,5},{7,6},{8,15},{9,8},{10,9... | collective-permute-start | bytes 1572872 | tf_op jit(solution)/shard_map/ppermute | solution.py:339
  9.1 3.0 %pick_head.1.refs_11_ = bf16[192,1024]{1,0:T(8,128)(2,1)} custom-call(s32[2]{0:T(128)} %pad_add_fusion.place_ref.refs_0_, bf16[1024,1536]{1,0:T(8,128)(2,1)} %refs_1_.3, bf16[1024,1536]{1,0:T(8,128)(2,1)} %refs_1_.3, bf16[1024,1536]{1,0:T(8,128)(2,1)} %refs_1_.3), custom_call_target="tpu_custom_call" | custom-call | bytes 4194304 | tf_op jit(solution)/shard_map/pick_head/pallas_call | solution.py:85
  12.1 2.6 %d_out.1 = bf16[8,64,256]{2,1,0:T(8,128)(2,1)} custom-call(bf16[256,1024]{1,0:T(8,128)(2,1)} %refs_4_.1, bf16[512,1024]{1,0:T(8,128)(2,1)} %refs_12_.1), custom_call_target="tpu_custom_call" | custom-call | flops 268435456 | bytes 2097152 | tf_op jit(solution)/shard_map/d_out/pallas_call | solution.py:46
  14.7 6.0 %collective-permute-done.refs_3_.refs_2_ = bf16[256,1024]{1,0:T(8,128)(2,1)S(1)} collective-permute-done((bf16[256,1024]{1,0:T(8,128)(2,1)}, bf16[256,1024]{1,0:T(8,128)(2,1)S(1)}, u32[]{:S(2)}, u32[]{:S(2)}) %collective-permute-start) | collective-permute-done | bytes 524320 | tf_op jit(solution)/shard_map/ppermute | solution.py:339
  20.8 3.2 %collective-permute-start.3 = (bf16[256,1024]{1,0:T(8,128)(2,1)S(1)}, bf16[256,1024]{1,0:T(8,128)(2,1)}, u32[]{:S(2)}, u32[]{:S(2)}) collective-permute-start(bf16[256,1024]{1,0:T(8,128)(2,1)S(1)} %collective-permute-done.1.refs_5_.refs_9_), channel_id=1, source_target_pairs={{0,7},{1,0},{2,1},{3,2},{4,3},{5,4},{6,5},{7,6},{8,15},{9,8},{10,9... | collective-permute-start | bytes 1572872 | tf_op jit(solution)/shard_map/ppermute | solution.py:339
  24.0 7.1 %messages.1 = (f32[256,1024]{1,0:T(8,128)}, bf16[256,1024]{1,0:T(8,128)(2,1)}, f32[256,1024]{1,0:T(8,128)}, bf16[256,1024]{1,0:T(8,128)(2,1)}) custom-call(s32[2]{0:T(128)} %pad_add_fusion.place_ref.refs_0_, s32[2,4]{1,0:T(2,128)} %refs_1_.2, s32[2]{0:T(128)} %refs_2_.1, bf16[256,1024]{1,0:T(8,128)(2,1)} %copy-done.5, ...), custom_call_target="tpu_custom_call" | custom-call | flops 2147483648 | bytes 8388608 | tf_op jit(solution)/shard_map/messages/pallas_call | solution.py:46
  31.1 4.0 %collective-permute-done.2.refs_3_ = bf16[256,1024]{1,0:T(8,128)(2,1)S(1)} collective-permute-done((bf16[256,1024]{1,0:T(8,128)(2,1)S(1)}, bf16[256,1024]{1,0:T(8,128)(2,1)S(1)}, u32[]{:S(2)}, u32[]{:S(2)}) %collective-permute-start.2) | collective-permute-done | bytes 524320 | tf_op jit(solution)/shard_map/ppermute | solution.py:339
  41.1 11.0 %collective-permute-done.4.refs_4_ = bf16[256,1024]{1,0:T(8,128)(2,1)S(1)} collective-permute-done((bf16[256,1024]{1,0:T(8,128)(2,1)}, bf16[256,1024]{1,0:T(8,128)(2,1)S(1)}, u32[]{:S(2)}, u32[]{:S(2)}) %collective-permute-start.4) | collective-permute-done | bytes 524320 | tf_op jit(solution)/shard_map/ppermute | solution.py:339
  52.2 7.9 %collective-permute-done.6.refs_1_ = bf16[256,1024]{1,0:T(8,128)(2,1)S(1)} collective-permute-done((bf16[256,1024]{1,0:T(8,128)(2,1)}, bf16[256,1024]{1,0:T(8,128)(2,1)S(1)}, u32[]{:S(2)}, u32[]{:S(2)}) %collective-permute-start.6) | collective-permute-done | bytes 524320 | tf_op jit(solution)/shard_map/ppermute | solution.py:339
  63.1 2.4 %collective-permute-start.9 = (bf16[128,1024]{1,0:T(8,128)(2,1)}, bf16[128,1024]{1,0:T(8,128)(2,1)}, u32[]{:S(2)}, u32[]{:S(2)}) collective-permute-start(bf16[128,1024]{1,0:T(8,128)(2,1)} %slice.7), channel_id=1, source_target_pairs={{0,7},{1,0},{2,1},{3,2},{4,3},{5,4},{6,5},{7,6},{8,15},{9,8},{10,9... | collective-permute-start | bytes 786440 | tf_op jit(solution)/shard_map/ppermute | solution.py:339
  65.5 4.0 %message_grad.1 = (bf16[8,128,256]{2,1,0:T(8,128)(2,1)}, f32[256,1024]{1,0:T(8,128)}) custom-call(f32[256,1024]{1,0:T(8,128)} %get-tuple-element.62.refs_0_, bf16[256,1024]{1,0:T(8,128)(2,1)} %copy-done.8, bf16[256,1024]{1,0:T(8,128)(2,1)} %collective-permute-done.7.refs_2_, bf16[1024,1024]{1,0:T(8,128)(2,1)} %refs_3_.2), custom_call_target="tpu_custom_call" | custom-call | flops 536870912 | bytes 8388608 | tf_op jit(solution)/shard_map/message_grad/pallas_call | solution.py:46
  69.8 5.9 %all-to-all-start = ((bf16[8,64,256]{2,1,0:T(8,128)(2,1)}), bf16[8,64,256]{2,1,0:T(8,128)(2,1)S(1)}, u32[]{:S(2)}, u32[]{:S(2)}) async-start(bf16[8,64,256]{2,1,0:T(8,128)(2,1)} %d_out.1), calls=%async_computation | async-start | bytes 524288 | tf_op jit(solution)/shard_map/all_to_all | solution.py:335
  75.7 14.5 %attend_forward.1 = (bf16[8,192,256]{2,1,0:T(8,128)(2,1)}, bf16[8,256,128]{2,1,0:T(8,128)(2,1)}, bf16[8,64,256]{2,1,0:T(8,128)(2,1)}, bf16[8,64,256]{2,1,0:T(8,1...) custom-call(s32[2]{0:T(128)} %pad_add_fusion.place_ref.refs_0_, ...), custom_call_target="tpu_custom_call" | custom-call | flops 3221225472 | bytes 8388608 | tf_op jit(solution)/shard_map/attend_forward/pallas_call | solution.py:46
  90.2 7.2 %all-to-all-start.1 = ((bf16[8,192,256]{2,1,0:T(8,128)(2,1)}), bf16[8,192,256]{2,1,0:T(8,128)(2,1)S(1)}, u32[]{:S(2)}, u32[]{:S(2)}) async-start(bf16[8,192,256]{2,1,0:T(8,128)(2,1)} %get-tuple-element.81), calls=%async_computation.1 | async-start | bytes 1572864 | tf_op jit(solution)/shard_map/all_to_all | solution.py:335
  97.4 15.4 %attend_backward.1.refs_11_ = bf16[8,192,256]{2,1,0:T(8,128)(2,1)} custom-call(s32[2]{0:T(128)} %pad_add_fusion.place_ref.refs_0_, bf16[8,256,128]{2,1,0:T(8,128)(2,1)} %get-tuple-element.72.refs_1_, bf16[8,64,256]{2,1,0:T(8,128)(2,1)} %get-tuple-element.73.refs_2_, bf16[8,64,256]{2,1,0:T(8,128)(2,1)} %get-tuple-element.74.refs_3_, ...), custom_call_target="tpu_custom_call" | custom-call | flops 6442450944 | bytes 4194304 | tf_op jit(solution)/shard_map/attend_backward/pallas_call | solution.py:46
  112.8 3.1 %all-to-all-done.1.refs_10_ = bf16[8,192,256]{2,1,0:T(8,128)(2,1)S(1)} async-done(((bf16[8,192,256]{2,1,0:T(8,128)(2,1)}), bf16[8,192,256]{2,1,0:T(8,128)(2,1)S(1)}, u32[]{:S(2)}, u32[]{:S(2)}) %all-to-all-start.1) | async-done | bytes 786464 | tf_op jit(solution)/shard_map/all_to_all | solution.py:335
  115.9 4.1 %all-to-all-start.2 = ((bf16[8,192,256]{2,1,0:T(8,128)(2,1)}), bf16[8,192,256]{2,1,0:T(8,128)(2,1)S(1)}, u32[]{:S(2)}, u32[]{:S(2)}) async-start(bf16[8,192,256]{2,1,0:T(8,128)(2,1)} %attend_backward.1.refs_11_), calls=%async_computation.2 | async-start | bytes 1572864 | tf_op jit(solution)/shard_map/all_to_all | solution.py:335
  120.0 7.5 %result.1 = (bf16[256,1024]{1,0:T(8,128)(2,1)}, bf16[16,224,128]{2,1,0:T(8,128)(2,1)}, bf16[16,224,128]{2,1,0:T(8,128)(2,1)}) custom-call(s32[2]{0:T(128)} %pad_add_fusion.place_ref.refs_0_, bf16[256,1024]{1,0:T(8,128)(2,1)} %normalize.1.refs_4_.refs_1_, bf16[256,1024]{1,0:T(8,128)(2,1)} %copy-done.5, bf16[256,1024]{1,0:T(8,128)(2,1)} %copy-done.7, ...), custom_call_target="tpu_custom_call" | custom-call | flops 2147483648 | bytes 10485760 | tf_op jit(solution)/shard_map/result/pallas_call | solution.py:46
  127.7 2.7 %collective-permute-done.10 = bf16[16,224,128]{2,1,0:T(8,128)(2,1)S(1)} collective-permute-done((bf16[16,224,128]{2,1,0:T(8,128)(2,1)}, bf16[16,224,128]{2,1,0:T(8,128)(2,1)S(1)}, u32[]{:S(2)}, u32[]{:S(2)}) %collective-permute-start.10) | collective-permute-done | bytes 917536 | tf_op jit(solution)/shard_map/ppermute | solution.py:440
  131.7 6.1 %all-to-all-done.2.refs_0_ = bf16[8,192,256]{2,1,0:T(8,128)(2,1)S(1)} async-done(((bf16[8,192,256]{2,1,0:T(8,128)(2,1)}), bf16[8,192,256]{2,1,0:T(8,128)(2,1)S(1)}, u32[]{:S(2)}, u32[]{:S(2)}) %all-to-all-start.2) | async-done | bytes 786464 | tf_op jit(solution)/shard_map/all_to_all | solution.py:335
  137.9 17.4 %all_to_all.25.shares_ref = bf16[16,224,128]{2,1,0:T(8,128)(2,1)} all-to-all(bf16[16,224,128]{2,1,0:T(8,128)(2,1)S(1)} %add_convert_fusion), channel_id=1, replica_groups=mesh['x'=4,'y'=4,'c'=2,'z'=8] {'x','y'}, dimensions={0} | all-to-all | bytes 1835008 | tf_op jit(solution)/shard_map/all_to_all | solution.py:335
  157.4 4.9 %all-to-all-start.4 = ((bf16[8,224,128]{2,1,0:T(8,128)(2,1)}), bf16[8,224,128]{2,1,0:T(8,128)(2,1)S(1)}, u32[]{:S(2)}, u32[]{:S(2)}) async-start(bf16[8,224,128]{2,1,0:T(8,128)(2,1)} %share_sum.1), calls=%async_computation.4 | async-start | bytes 917504 | tf_op jit(solution)/shard_map/all_to_all | solution.py:335
  166.5 4.8 %input_grad.1 = bf16[256,1024]{1,0:T(8,128)(2,1)} custom-call(bf16[8,192,256]{2,1,0:T(8,128)(2,1)} %copy-done.1, bf16[1024,1536]{1,0:T(8,128)(2,1)} %refs_1_.3, f32[256,1024]{1,0:T(8,128)} %get-tuple-element.91.refs_2_, bf16[256,1024]{1,0:T(8,128)(2,1)} %refs_3_.3, bf16[256,1024]{1,0:T(8,128)(2,1)} %refs_4_.1, f32[1,1024]{1,0:T(1,128)} %bitcast.7), custom_call_target="tpu_custom_call" | custom-call | flops 805306368 | bytes 8388608 | tf_op jit(solution)/shard_map/input_grad/pallas_call | solution.py:46
  171.4 5.4 %all-to-all-done.4.every_ref = bf16[8,224,128]{2,1,0:T(8,128)(2,1)S(1)} async-done(((bf16[8,224,128]{2,1,0:T(8,128)(2,1)}), bf16[8,224,128]{2,1,0:T(8,128)(2,1)S(1)}, u32[]{:S(2)}, u32[]{:S(2)}) %all-to-all-start.4) | async-done | bytes 458784 | tf_op jit(solution)/shard_map/all_to_all | solution.py:335
  (47 shorter events, 24.5 us)
Async XLA Ops:
  2.7 18.0 %collective-permute-start = (bf16[256,1024]{1,0:T(8,128)(2,1)}, bf16[256,1024]{1,0:T(8,128)(2,1)S(1)}, u32[]{:S(2)}, u32[]{:S(2)}) collective-permute-start(bf16[256,1024]{1,0:T(8,128)(2,1)} %normalize.1.refs_4_.refs_1_), channel_id=1, source_target_pairs={{0,1},{1,2},{2,3},{3,4},{4,5},{5,6},{6,7},{7,0},{8,9},{9,10},{10,1... | collective-permute-start | bytes 1572872 | tf_op jit(solution)/shard_map/ppermute | solution.py:339
  4.6 16.1 %collective-permute-start.1 = (bf16[256,1024]{1,0:T(8,128)(2,1)}, bf16[256,1024]{1,0:T(8,128)(2,1)S(1)}, u32[]{:S(2)}, u32[]{:S(2)}) collective-permute-start(bf16[256,1024]{1,0:T(8,128)(2,1)} %normalize.1.refs_4_.refs_1_), channel_id=1, source_target_pairs={{0,7},{1,0},{2,1},{3,2},{4,3},{5,4},{6,5},{7,6},{8,15},{9,8},{10,9... | collective-permute-start | bytes 1572872 | tf_op jit(solution)/shard_map/ppermute | solution.py:339
  20.7 3.3 %copy-start.5 = (bf16[256,1024]{1,0:T(8,128)(2,1)}, bf16[256,1024]{1,0:T(8,128)(2,1)S(1)}, u32[]{:S(2)}) copy-start(bf16[256,1024]{1,0:T(8,128)(2,1)S(1)} %collective-permute-done.refs_3_.refs_2_) | copy-start | bytes 1572868
  20.7 3.3 %copy-start.6 = (bf16[256,1024]{1,0:T(8,128)(2,1)}, bf16[256,1024]{1,0:T(8,128)(2,1)S(1)}, u32[]{:S(2)}) copy-start(bf16[256,1024]{1,0:T(8,128)(2,1)S(1)} %collective-permute-done.1.refs_5_.refs_9_) | copy-start | bytes 1572868
  20.7 14.4 %collective-permute-start.2 = (bf16[256,1024]{1,0:T(8,128)(2,1)S(1)}, bf16[256,1024]{1,0:T(8,128)(2,1)S(1)}, u32[]{:S(2)}, u32[]{:S(2)}) collective-permute-start(bf16[256,1024]{1,0:T(8,128)(2,1)S(1)} %collective-permute-done.refs_3_.refs_2_), channel_id=1, source_target_pairs={{0,1},{1,2},{2,3},{3,4},{4,5},{5,6},{6,7},{7,0},{8,9},{9,10},{10,1... | collective-permute-start | bytes 1572872 | tf_op jit(solution)/shard_map/ppermute | solution.py:339
  20.8 14.3 %collective-permute-start.3 = (bf16[256,1024]{1,0:T(8,128)(2,1)S(1)}, bf16[256,1024]{1,0:T(8,128)(2,1)}, u32[]{:S(2)}, u32[]{:S(2)}) collective-permute-start(bf16[256,1024]{1,0:T(8,128)(2,1)S(1)} %collective-permute-done.1.refs_5_.refs_9_), channel_id=1, source_target_pairs={{0,7},{1,0},{2,1},{3,2},{4,3},{5,4},{6,5},{7,6},{8,15},{9,8},{10,9... | collective-permute-start | bytes 1572872 | tf_op jit(solution)/shard_map/ppermute | solution.py:339
  35.9 16.3 %collective-permute-start.4 = (bf16[256,1024]{1,0:T(8,128)(2,1)}, bf16[256,1024]{1,0:T(8,128)(2,1)S(1)}, u32[]{:S(2)}, u32[]{:S(2)}) collective-permute-start(bf16[256,1024]{1,0:T(8,128)(2,1)} %copy-done.7), channel_id=1, source_target_pairs={{0,1},{1,2},{2,3},{3,4},{4,5},{5,6},{6,7},{7,0},{8,9},{9,10},{10,1... | collective-permute-start | bytes 1572872 | tf_op jit(solution)/shard_map/ppermute | solution.py:339
  36.9 15.2 %collective-permute-start.5 = (bf16[256,1024]{1,0:T(8,128)(2,1)}, bf16[256,1024]{1,0:T(8,128)(2,1)S(1)}, u32[]{:S(2)}, u32[]{:S(2)}) collective-permute-start(bf16[256,1024]{1,0:T(8,128)(2,1)} %collective-permute-done.3.refs_8_), channel_id=1, source_target_pairs={{0,7},{1,0},{2,1},{3,2},{4,3},{5,4},{6,5},{7,6},{8,15},{9,8},{10,9... | collective-permute-start | bytes 1572872 | tf_op jit(solution)/shard_map/ppermute | solution.py:339
  39.1 21.0 %collective-permute-start.6 = (bf16[256,1024]{1,0:T(8,128)(2,1)}, bf16[256,1024]{1,0:T(8,128)(2,1)S(1)}, u32[]{:S(2)}, u32[]{:S(2)}) collective-permute-start(bf16[256,1024]{1,0:T(8,128)(2,1)} %get-tuple-element.58), channel_id=1, source_target_pairs={{0,7},{1,0},{2,1},{3,2},{4,3},{5,4},{6,5},{7,6},{8,15},{9,8},{10,9... | collective-permute-start | bytes 1572872 | tf_op jit(solution)/shard_map/ppermute | solution.py:339
  40.2 20.6 %collective-permute-start.7 = (bf16[256,1024]{1,0:T(8,128)(2,1)}, bf16[256,1024]{1,0:T(8,128)(2,1)}, u32[]{:S(2)}, u32[]{:S(2)}) collective-permute-start(bf16[256,1024]{1,0:T(8,128)(2,1)} %get-tuple-element.59), channel_id=1, source_target_pairs={{0,1},{1,2},{2,3},{3,4},{4,5},{5,6},{6,7},{7,0},{8,9},{9,10},{10,1... | collective-permute-start | bytes 1572872 | tf_op jit(solution)/shard_map/ppermute | solution.py:339
  52.1 17.4 %copy-start.3 = (bf16[256,1024]{1,0:T(8,128)(2,1)}, bf16[256,1024]{1,0:T(8,128)(2,1)S(1)}, u32[]{:S(2)}) copy-start(bf16[256,1024]{1,0:T(8,128)(2,1)S(1)} %collective-permute-done.4.refs_4_) | copy-start | bytes 1572868
  52.1 17.4 %copy-start.4 = (bf16[256,1024]{1,0:T(8,128)(2,1)}, bf16[256,1024]{1,0:T(8,128)(2,1)S(1)}, u32[]{:S(2)}) copy-start(bf16[256,1024]{1,0:T(8,128)(2,1)S(1)} %collective-permute-done.5.refs_7_) | copy-start | bytes 1572868
  60.1 5.4 %copy-start.8 = (bf16[256,1024]{1,0:T(8,128)(2,1)}, bf16[256,1024]{1,0:T(8,128)(2,1)S(1)}, u32[]{:S(2)}) copy-start(bf16[256,1024]{1,0:T(8,128)(2,1)S(1)} %collective-permute-done.6.refs_1_) | copy-start | bytes 1572868
  61.5 8.0 %collective-permute-start.8 = (bf16[128,1024]{1,0:T(8,128)(2,1)}, bf16[128,1024]{1,0:T(8,128)(2,1)S(1)}, u32[]{:S(2)}, u32[]{:S(2)}) collective-permute-start(bf16[128,1024]{1,0:T(8,128)(2,1)} %slice.6), channel_id=1, source_target_pairs={{0,1},{1,2},{2,3},{3,4},{4,5},{5,6},{6,7},{7,0},{8,9},{9,10},{10,1... | collective-permute-start | bytes 786440 | tf_op jit(solution)/shard_map/ppermute | solution.py:339
  63.1 6.7 %collective-permute-start.9 = (bf16[128,1024]{1,0:T(8,128)(2,1)}, bf16[128,1024]{1,0:T(8,128)(2,1)}, u32[]{:S(2)}, u32[]{:S(2)}) collective-permute-start(bf16[128,1024]{1,0:T(8,128)(2,1)} %slice.7), channel_id=1, source_target_pairs={{0,7},{1,0},{2,1},{3,2},{4,3},{5,4},{6,5},{7,6},{8,15},{9,8},{10,9... | collective-permute-start | bytes 786440 | tf_op jit(solution)/shard_map/ppermute | solution.py:339
  69.6 6.1 %copy-start.9 = (bf16[128,1024]{1,0:T(8,128)(2,1)}, bf16[128,1024]{1,0:T(8,128)(2,1)S(1)}, u32[]{:S(2)}) copy-start(bf16[128,1024]{1,0:T(8,128)(2,1)S(1)} %collective-permute-done.8.refs_5_) | copy-start | bytes 786436
  69.8 20.4 %all-to-all-start = ((bf16[8,64,256]{2,1,0:T(8,128)(2,1)}), bf16[8,64,256]{2,1,0:T(8,128)(2,1)S(1)}, u32[]{:S(2)}, u32[]{:S(2)}) async-start(bf16[8,64,256]{2,1,0:T(8,128)(2,1)} %d_out.1), calls=%async_computation | async-start | bytes 524288 | tf_op jit(solution)/shard_map/all_to_all | solution.py:335
  90.2 7.2 %copy-start.10 = (bf16[8,64,256]{2,1,0:T(8,128)(2,1)}, bf16[8,64,256]{2,1,0:T(8,128)(2,1)S(1)}, u32[]{:S(2)}) copy-start(bf16[8,64,256]{2,1,0:T(8,128)(2,1)S(1)} %all-to-all-done.refs_7_) | copy-start | bytes 786436
  90.2 25.7 %all-to-all-start.1 = ((bf16[8,192,256]{2,1,0:T(8,128)(2,1)}), bf16[8,192,256]{2,1,0:T(8,128)(2,1)S(1)}, u32[]{:S(2)}, u32[]{:S(2)}) async-start(bf16[8,192,256]{2,1,0:T(8,128)(2,1)} %get-tuple-element.81), calls=%async_computation.1 | async-start | bytes 1572864 | tf_op jit(solution)/shard_map/all_to_all | solution.py:335
  115.9 4.1 %copy-start = (bf16[8,192,256]{2,1,0:T(8,128)(2,1)}, bf16[8,192,256]{2,1,0:T(8,128)(2,1)S(1)}, u32[]{:S(2)}) copy-start(bf16[8,192,256]{2,1,0:T(8,128)(2,1)S(1)} %all-to-all-done.1.refs_10_) | copy-start | bytes 2359300
  115.9 22.0 %all-to-all-start.2 = ((bf16[8,192,256]{2,1,0:T(8,128)(2,1)}), bf16[8,192,256]{2,1,0:T(8,128)(2,1)S(1)}, u32[]{:S(2)}, u32[]{:S(2)}) async-start(bf16[8,192,256]{2,1,0:T(8,128)(2,1)} %attend_backward.1.refs_11_), calls=%async_computation.2 | async-start | bytes 1572864 | tf_op jit(solution)/shard_map/all_to_all | solution.py:335
  127.6 2.8 %collective-permute-start.10 = (bf16[16,224,128]{2,1,0:T(8,128)(2,1)}, bf16[16,224,128]{2,1,0:T(8,128)(2,1)S(1)}, u32[]{:S(2)}, u32[]{:S(2)}) collective-permute-start(bf16[16,224,128]{2,1,0:T(8,128)(2,1)} %get-tuple-element.87), channel_id=1, source_target_pairs={{0,8},{8,0},{1,9},{9,1},{2,10},{10,2},{3,11},{11,3},{4,12},{12,4},... | collective-permute-start | bytes 2752520 | tf_op jit(solution)/shard_map/ppermute | solution.py:440
  137.9 27.1 %copy-start.1 = (bf16[8,192,256]{2,1,0:T(8,128)(2,1)}, bf16[8,192,256]{2,1,0:T(8,128)(2,1)S(1)}, u32[]{:S(2)}) copy-start(bf16[8,192,256]{2,1,0:T(8,128)(2,1)S(1)} %all-to-all-done.2.refs_0_) | copy-start | bytes 2359300
  157.4 19.4 %all-to-all-start.4 = ((bf16[8,224,128]{2,1,0:T(8,128)(2,1)}), bf16[8,224,128]{2,1,0:T(8,128)(2,1)S(1)}, u32[]{:S(2)}, u32[]{:S(2)}) async-start(bf16[8,224,128]{2,1,0:T(8,128)(2,1)} %share_sum.1), calls=%async_computation.4 | async-start | bytes 917504 | tf_op jit(solution)/shard_map/all_to_all | solution.py:335
  (2 other events, 1.6 us)

commit v4 on v3

--- a/solution.py
+++ b/solution.py
@@ -60,6 +60,22 @@
     out_ref[...] = (wide * unit_factor(wide, -1) * gain_ref[...]).astype(jnp.bfloat16)
 
 
+def normalize_half(features, gain, half):
+    width = features.shape[1]
+    return pl.pallas_call(
+        normalize_kernel,
+        grid=(1,),
+        in_specs=[
+            pl.BlockSpec((BLOCK, width), lambda i: (half, 0)),
+            pl.BlockSpec((1, width), lambda i: (0, 0)),
+        ],
+        out_specs=pl.BlockSpec((BLOCK, width), lambda i: (0, 0)),
+        out_shape=jax.ShapeDtypeStruct((BLOCK, width), jnp.bfloat16),
+        cost_estimate=pl.CostEstimate(flops=0, bytes_accessed=1 << 19, transcendentals=0),
+        name="normalize",
+    )(features, gain)
+
+
 def d_out_kernel(grad_ref, w_ref, out_ref):
     turned = contract_cols(w_ref[...], grad_ref[...]).astype(jnp.bfloat16)
     for h in range(N_SEQ):
@@ -98,11 +114,14 @@
 
 
 def message_kernel(*refs):
-    place_ref, ids_ref, counts_ref, low_ref, own_ref, high_ref, w_ref, tiles_ref, grad_ref = refs[:9]
-    act_ref, to_low_ref, mid_ref, to_high_ref, msg, landed = refs[9:]
+    place_ref, ids_ref, counts_ref = refs[:3]
+    blocks = refs[3:9]
+    w_ref, tiles_ref, grad_ref = refs[9:12]
+    act_ref, to_low_ref, mid_ref, to_high_ref, msg, landed = refs[12:]
     z = place_ref[0]
-    for t, ref in enumerate((low_ref, own_ref, high_ref)):
-        rows = matmul(ref[...], w_ref[...]).astype(jnp.bfloat16)
+    for t in range(3):
+        both = jnp.concatenate([blocks[2 * t][...], blocks[2 * t + 1][...]], axis=0)
+        rows = matmul(both, w_ref[...]).astype(jnp.bfloat16)
         msg[2 * t] = rows[:BLOCK]
         msg[2 * t + 1] = rows[BLOCK:]
     landed[...] = jnp.zeros_like(landed)
@@ -141,15 +160,14 @@
             )
 
 
-def message_grad_kernel(*refs):
-    mid_ref, above_ref, below_ref, w_ref = refs[:4]
-    cut_ref, d_norm_ref = refs[4:]
+def merge_kernel(heads_ref, mid_ref, above_ref, below_ref, send_ref, d_msg_ref):
     total = mid_ref[...] + above_ref[...].astype(jnp.float32) + below_ref[...].astype(jnp.float32)
     d_msg = total.astype(jnp.bfloat16)
+    d_msg_ref[...] = d_msg
     for t in range(N_SEQ):
         columns = d_msg[:, t * BLOCK : (t + 1) * BLOCK]
-        cut_ref[t] = jnp.concatenate([columns[:BLOCK], columns[BLOCK:]], axis=1)
-    d_norm_ref[...] = contract_cols(d_msg, w_ref[...])
+        send_ref[t, :HEAD_DIM] = heads_ref[t]
+        send_ref[t, HEAD_DIM:] = jnp.concatenate([columns[:BLOCK], columns[BLOCK:]], axis=1)
 
 
 def place_of(z, j):
@@ -157,29 +175,26 @@
 
 
 def fetch_chunks(refs, held, sems):
-    half = CHUNK // 2
-    targets = [held.at[j] for j in range(4)]
-    targets += [held.at[4, pl.ds(0, half)], held.at[4, pl.ds(half, half)]]
-    targets += [held.at[j] for j in range(5, N_SEQ)]
-    copies = [pltpu.make_async_copy(ref, to, sems.at[i]) for i, (ref, to) in enumerate(zip(refs, targets))]
+    copies = [
+        pltpu.make_async_copy(ref, held.at[i // 2, pl.ds(i % 2 * BLOCK, BLOCK)], sems.at[i])
+        for i, ref in enumerate(refs)
+    ]
     for copy in copies:
         copy.start()
 
     def wait(j):
-        for copy in copies[j + (j > 4) : j + 1 + (j >= 4)]:
-            copy.wait()
+        copies[2 * j].wait()
+        copies[2 * j + 1].wait()
 
     return wait
 
 
 def forward_kernel(*refs):
     z = refs[0][0]
-    cut_ref, w_ref = refs[10:12]
-    send_ref, kv_ref, hq_ref, ku_ref, raw_ref, out_ref, stats_ref = refs[12:19]
-    v_ext, held, sems = refs[19:22]
-    wait = fetch_chunks(refs[1:10], held, sems)
-    pass_on = pltpu.make_async_copy(cut_ref, send_ref.at[:, pl.ds(HEAD_DIM, BLOCK)], sems.at[9])
-    pass_on.start()
+    w_ref = refs[17]
+    out_ref, kv_ref, hq_ref, ku_ref, raw_ref, stats_ref = refs[18:24]
+    v_ext, held, sems = refs[24:]
+    wait = fetch_chunks(refs[1:17], held, sems)
     for j in range(N_SEQ):
         wait(j)
         proj = contract_cols(w_ref[...], held[j]).astype(jnp.bfloat16)
@@ -203,17 +218,15 @@
         inverse = 1.0 / out[HEAD_DIM : HEAD_DIM + 1]
         stats_ref[i, 0:1] = inverse
         head_out = (out[:HEAD_DIM] * inverse).astype(jnp.bfloat16)
-        out_ref[i] = head_out
-        send_ref[place_of(z, i), :HEAD_DIM] = head_out
+        out_ref[place_of(z, i)] = head_out
         return carry
 
     lax.fori_loop(0, N_SEQ, step, 0)
-    pass_on.wait()
 
 
 def backward_kernel(*refs):
     z = refs[0][0]
-    kv_ref, hq_ref, ku_ref, raw_ref, head_ref, stats_ref, d_ref = refs[1:8]
+    head_ref, kv_ref, hq_ref, ku_ref, raw_ref, stats_ref, d_ref = refs[1:8]
     stack_ref, sums, dqt = refs[8:]
     sums[...] = jnp.zeros_like(sums)
 
@@ -228,7 +241,7 @@
         rhs = jnp.concatenate([jnp.where(left, 0.0, rows), jnp.where(left, rows, 0.0)], axis=0)
         rhs = rhs.astype(jnp.bfloat16)
         inverse = stats_ref[i, 0:1]
-        row_dot = jnp.sum(head_ref[i].astype(jnp.float32) * d_wide, axis=0, keepdims=True)
+        row_dot = jnp.sum(head_ref[place_of(z, i)].astype(jnp.float32) * d_wide, axis=0, keepdims=True)
         keys = kv_ref[...].reshape(N_SEQ * CHUNK, 2 * HEAD_DIM)
         prob = jnp.exp(matmul(keys, query)) * inverse
         d_scores = (prob * (matmul(keys, d_head) - row_dot)).astype(jnp.bfloat16)
@@ -253,9 +266,9 @@
 
 def result_kernel(*refs):
     place_ref = refs[0]
-    home_ref, stack_ref, w_ref, grad_ref, x_ref, act_ref = refs[10:16]
-    out_ref, keep_ref, give_ref, grad_t, grad_node, grad_out, held, sems = refs[16:]
-    wait = fetch_chunks(refs[1:10], held, sems)
+    home_ref, stack_ref, w_ref, grad_ref, x_ref, act_ref = refs[17:23]
+    out_ref, keep_ref, give_ref, grad_t, grad_node, grad_out, held, sems = refs[23:]
+    wait = fetch_chunks(refs[1:17], held, sems)
     z = place_ref[0]
     every = jnp.concatenate([home_ref[h, :HEAD_DIM] for h in range(N_SEQ)], axis=0)
     grad_out[...] = matmul(every, grad_ref[...])
@@ -314,11 +327,12 @@
 
 
 def input_grad_kernel(*refs):
-    stack_ref, w_ref, d_norm_ref, x_ref, grad_ref, gain_ref, out_ref = refs
+    stack_ref, w_ref, d_msg_ref, w_msg_ref, x_ref, grad_ref, gain_ref, out_ref = refs
     parts = [
         stack_ref[h, t * HEAD_DIM : (t + 1) * HEAD_DIM] for t in range(3) for h in range(N_SEQ)
     ]
-    d_norm = matmul(w_ref[...], jnp.concatenate(parts, axis=0)).T + d_norm_ref[...]
+    d_norm = matmul(w_ref[...], jnp.concatenate(parts, axis=0)).T
+    d_norm += contract_cols(d_msg_ref[...], w_msg_ref[...])
     wide = x_ref[...].astype(jnp.float32)
     inv_rms = unit_factor(wide, -1)
     x_hat = wide * inv_rms
@@ -370,47 +384,51 @@
     wide_shape = ((node_rows, width), f32)
     low_shape = ((node_rows, width), bf16)
 
-    (normed,) = call(normalize_kernel, "normalize", (low_shape,), (), (features, gain), moved=1 << 20)
-
-    a1, b1 = up(normed), down(normed)
+    n_a = normalize_half(features, gain, 0)
+    a_up, a_down = [n_a, up(n_a)], [n_a, down(n_a)]
+    n_b = normalize_half(features, gain, 1)
+    b_up, b_down = [n_b, up(n_b)], [n_b, down(n_b)]
+    w_head = pick_head(place, w_qkv)
     (d_out,) = call(
         d_out_kernel, "d_out", (((N_SEQ, HEAD_DIM, node_rows), bf16),), (), (out_grad, w_out),
         flops=2 * node_rows * width * hd, moved=2 << 20,
     )
-    w_head = pick_head(place, w_qkv)
-    a1, b1, d_out, w_head = lax.optimization_barrier((a1, b1, d_out, w_head))
-    a2, b2 = up(a1), down(b1)
-
+    a_up[1], a_down[1], d_out, w_head = lax.optimization_barrier((a_up[1], a_down[1], d_out, w_head))
+    a_up.append(up(a_up[1]))
+    a_down.append(down(a_down[1]))
+    b_up.append(up(b_up[1]))
+    b_down.append(down(b_down[1]))
+    a_up.append(up(a_up[2]))
+    a_down.append(down(a_down[2]))
     act, to_low, mid, to_high = call(
         message_kernel, "messages", (wide_shape, low_shape, wide_shape, low_shape),
-        (place, block_ids, block_counts), (a1, normed, b1, w_msg, edge_tiles, out_grad),
+        (place, block_ids, block_counts),
+        (after(a_up[1], a_up[3], a_down[3]), b_up[1], n_a, n_b, a_down[1], b_down[1], w_msg, edge_tiles, out_grad),
         [pltpu.VMEM((6, BLOCK, width), bf16), pltpu.VMEM((6, BLOCK, width), f32)],
         flops=8 * node_rows * width * width, exps=node_rows * width, moved=8 << 20,
     )
-    a2, b2, to_low, to_high = lax.optimization_barrier((a2, b2, to_low, to_high))
-    a3, b3 = up(a2), down(b2)
+    b_up.append(up(b_up[2]))
+    b_down.append(down(b_down[2]))
+    c4 = [up(a_up[3]), down(b_down[3])]
+    *c4, to_low, to_high, d_out = lax.optimization_barrier((*c4, to_low, to_high, d_out))
     above, below = down(to_low), up(to_high)
-    a3, b3, above, below = lax.optimization_barrier((a3, b3, above, below))
-    half = node_rows // 2
-    c4 = (up(a3[:half]), down(b3[half:]))
-    d_msg_cut, d_norm = call(
-        message_grad_kernel, "message_grad", (((N_SEQ, BLOCK, CHUNK), bf16), wide_shape),
-        (), (mid, above, below, w_msg), flops=2 * node_rows * width * width, moved=8 << 20,
-    )
-    *c4, d_msg_cut, d_norm, d_out = lax.optimization_barrier((*c4, d_msg_cut, d_norm, d_out))
-    chunks = (normed, a1, a2, a3, *c4, b3, b2, b1)
+    pairs = list(zip(a_up, b_up)) + [c4] + list(zip(a_down, b_down))[:0:-1]
+    chunks = tuple(half for pair in pairs for half in pair)
     d_heads = exchange(d_out, "z")
 
     held = pltpu.VMEM((N_SEQ, CHUNK, width), bf16)
     lanes_in = ((N_SEQ, CHUNK, 2 * HEAD_DIM), bf16)
     turned = ((N_SEQ, HEAD_DIM, CHUNK), bf16)
-    send, *saved = call(
+    heads, *saved = call(
         forward_kernel, "attend_forward",
-        (((N_SEQ, HEAD_DIM + BLOCK, CHUNK), bf16), lanes_in, turned, turned,
-         ((N_SEQ, 2 * HEAD_DIM, CHUNK), bf16), turned, ((N_SEQ, 8, CHUNK), f32)),
+        (turned, lanes_in, turned, turned, ((N_SEQ, 2 * HEAD_DIM, CHUNK), bf16), ((N_SEQ, 8, CHUNK), f32)),
         (place,), (w_head,),
-        [pltpu.VMEM((N_SEQ, HEAD_DIM + ONES, CHUNK), bf16), held, pltpu.SemaphoreType.DMA((10,))],
-        flops=12 * nodes * nodes * HEAD_DIM, exps=nodes * nodes, moved=8 << 20, far=chunks + (d_msg_cut,),
+        [pltpu.VMEM((N_SEQ, HEAD_DIM + ONES, CHUNK), bf16), held, pltpu.SemaphoreType.DMA((16,))],
+        flops=12 * nodes * nodes * HEAD_DIM, exps=nodes * nodes, moved=8 << 20, far=chunks,
+    )
+    send, d_msg = call(
+        merge_kernel, "merge", (((N_SEQ, HEAD_DIM + BLOCK, CHUNK), bf16), low_shape), (),
+        (heads, mid, above, below), moved=4 << 20,
     )
     send, d_heads = lax.optimization_barrier((send, d_heads))
     home = exchange(send, "z")
@@ -419,7 +437,7 @@
     rows_out = hd // (2 * N_XY)
     (stack,) = call(
         backward_kernel, "attend_backward", (((N_SEQ, 3 * HEAD_DIM, CHUNK), bf16),),
-        (place,), (*saved, d_heads),
+        (place,), (heads, *saved, d_heads),
         [pltpu.VMEM((N_SEQ, CHUNK, 2 * HEAD_DIM), f32), pltpu.VMEM((N_SEQ, HEAD_DIM, CHUNK), f32)],
         flops=24 * nodes * nodes * HEAD_DIM, exps=nodes * nodes, moved=4 << 20,
     )
@@ -433,7 +451,7 @@
         (home, stack, w_out, out_grad, features, act),
         [
             pltpu.VMEM((3 * BLOCK, width), f32), pltpu.VMEM((width, 3 * BLOCK), f32),
-            pltpu.VMEM((hd, width), f32), held, pltpu.SemaphoreType.DMA((9,)),
+            pltpu.VMEM((hd, width), f32), held, pltpu.SemaphoreType.DMA((16,)),
         ],
         flops=8 * node_rows * width * width, moved=10 << 20, far=chunks,
     )
@@ -448,7 +466,7 @@
 
     (grad_input,) = call(
         input_grad_kernel, "input_grad", (low_shape,), (),
-        (after(stack_home, mine), w_qkv, d_norm, features, out_grad, gain),
+        (after(stack_home, mine), w_qkv, d_msg, w_msg, features, out_grad, gain),
         flops=6 * node_rows * width * hd, moved=8 << 20,
     )
 

time: 181 us -> 173 us (0.956)
  waiting for transfers between devices: 47.2 us -> 25.2 us
  starting transfers between devices: 39.9 us -> 54.4 us
    ppermute x10 -> x16, waiting for transfers between devices: 29.9 us -> 10.2 us  [shift(): lax.ppermute(array, 'z', [(i, (i + distance) % N_SEQ) for i in range(N_SE...]
    ppermute x10 -> x16, starting transfers between devices: 17.7 us -> 30.1 us  [shift(): lax.ppermute(array, 'z', [(i, (i + distance) % N_SEQ) for i in range(N_SE...]
    pallas_call x0 -> x2, Pallas kernels: none -> 3.65 us  [normalize_half(): pl.pallas_call(normalize_kernel, grid=(1,), in_specs=[pl.BlockSpec((BLOCK...]
    pallas_call x10 -> x9, Pallas kernels: 62 us -> 59 us  [call(): pl.pallas_call(kernel, out_shape=tuple((jax.ShapeDtypeStruct(s, t) for s,...]
    all_to_all x4, waiting for transfers between devices: 14.6 us -> 12.3 us  [exchange(): return lax.all_to_all(array, axis, split_axis=0, concat_axis=0, tiled=True)]
    all_to_all x4, starting transfers between devices: 22.1 us -> 24.2 us  [exchange(): return lax.all_to_all(array, axis, split_axis=0, concat_axis=0, tiled=True)]
  transfers between devices with their start and end apart: 15 -> 21, of which waited for: 10 -> 11; matrix products, arithmetic and copies ran while one was open for 4% -> 4% of each run, Pallas kernels for 33% -> 35%
where the time goes in v4:
time: 173 us; the launch traced here: 172 us
  Pallas kernels  65.7 us (38%)
  starting transfers between devices  54.4 us (31%)
  waiting for transfers between devices  25.2 us (15%)
  blocking collectives  17.4 us (10%)
  local copies, waits for them, and re-layouts  6.71 us (4%)
  other arithmetic  2 us (1%)
    pallas_call x9, Pallas kernels, call(): pl.pallas_call(kernel, out_shape=tuple((jax.ShapeDtypeStruct(s, t) for s,...  59 us
    ppermute x16, starting transfers between devices, shift(): lax.ppermute(array, 'z', [(i, (i + distance) % N_SEQ) for i in range(N_SE...  30.1 us
    all_to_all x4, starting transfers between devices, exchange(): return lax.all_to_all(array, axis, split_axis=0, concat_axis=0, tiled=True)  24.2 us
    all_to_all x1, blocking collectives, exchange(): return lax.all_to_all(array, axis, split_axis=0, concat_axis=0, tiled=True)  17.4 us
    all_to_all x4, waiting for transfers between devices, exchange(): return lax.all_to_all(array, axis, split_axis=0, concat_axis=0, tiled=True)  12.3 us
    ppermute x16, waiting for transfers between devices, shift(): lax.ppermute(array, 'z', [(i, (i + distance) % N_SEQ) for i in range(N_SE...  10.2 us
    pallas_call x2, Pallas kernels, normalize_half(): pl.pallas_call(normalize_kernel, grid=(1,), in_specs=[pl.BlockSpec((BLOCK...  3.65 us
  transfers between devices with their start and end apart: 21, of which 11 were waited for; matrix products, arithmetic and copies ran while one was open for 4% of the time, Pallas kernels for 35%

profile of v4, /device:TPU:6, one launch (start us, length us, event | category | flops | bytes accessed | tf_op | source)
XLA Modules:
  0.0 172.2 jit_solution(17097994517640926074)
XLA Ops:
  4.4 3.9 %collective-permute-start.1 = (bf16[128,1024]{1,0:T(8,128)(2,1)}, bf16[128,1024]{1,0:T(8,128)(2,1)S(1)}, u32[]{:S(2)}, u32[]{:S(2)}) collective-permute-start(bf16[128,1024]{1,0:T(8,128)(2,1)} %normalize.2.refs_5_.refs_1_), channel_id=1, source_target_pairs={{0,7},{1,0},{2,1},{3,2},{4,3},{5,4},{6,5},{7,6},{8,15},{9,8},{10,9... | collective-permute-start | bytes 786440 | tf_op jit(solution)/shard_map/ppermute | solution.py:353
  12.7 3.1 %pick_head.1.refs_17_ = bf16[192,1024]{1,0:T(8,128)(2,1)} custom-call(s32[2]{0:T(128)} %pad_add_fusion.place_ref.refs_0_, bf16[1024,1536]{1,0:T(8,128)(2,1)} %refs_1_.3, bf16[1024,1536]{1,0:T(8,128)(2,1)} %refs_1_.3, bf16[1024,1536]{1,0:T(8,128)(2,1)} %refs_1_.3), custom_call_target="tpu_custom_call" | custom-call | bytes 4194304 | tf_op jit(solution)/shard_map/pick_head/pallas_call | solution.py:101
  15.8 2.6 %d_out.1 = bf16[8,64,256]{2,1,0:T(8,128)(2,1)} custom-call(bf16[256,1024]{1,0:T(8,128)(2,1)} %refs_5_.1, bf16[512,1024]{1,0:T(8,128)(2,1)} %refs_19_.1), custom_call_target="tpu_custom_call" | custom-call | flops 268435456 | bytes 2097152 | tf_op jit(solution)/shard_map/d_out/pallas_call | solution.py:46
  19.8 3.6 %collective-permute-start.9 = (bf16[128,1024]{1,0:T(8,128)(2,1)S(1)}, bf16[128,1024]{1,0:T(8,128)(2,1)S(1)}, u32[]{:S(2)}, u32[]{:S(2)}) collective-permute-start(bf16[128,1024]{1,0:T(8,128)(2,1)S(1)} %collective-permute-done.8.refs_8_.refs_16_), channel_id=1, source_target_pairs={{0,7},{1,0},{2,1},{3,2},{4,3},{5,4},{6,5},{7,6},{8,15},{9,8},{10,9... | collective-permute-start | bytes 786440 | tf_op jit(solution)/shard_map/ppermute | solution.py:353
  23.4 3.2 %collective-permute-start.12 = (bf16[128,1024]{1,0:T(8,128)(2,1)S(1)}, bf16[128,1024]{1,0:T(8,128)(2,1)S(1)}, u32[]{:S(2)}, u32[]{:S(2)}) collective-permute-start(bf16[128,1024]{1,0:T(8,128)(2,1)S(1)} %collective-permute-done.1.refs_7_.refs_15_), channel_id=1, source_target_pairs={{0,7},{1,0},{2,1},{3,2},{4,3},{5,4},{6,5},{7,6},{8,15},{9,8},{10,9... | collective-permute-start | bytes 786440 | tf_op jit(solution)/shard_map/ppermute | solution.py:353
  27.9 2.3 %collective-permute-done.9.refs_14_ = bf16[128,1024]{1,0:T(8,128)(2,1)S(1)} collective-permute-done((bf16[128,1024]{1,0:T(8,128)(2,1)S(1)}, bf16[128,1024]{1,0:T(8,128)(2,1)S(1)}, u32[]{:S(2)}, u32[]{:S(2)}) %collective-permute-start.9) | collective-permute-done | bytes 262176 | tf_op jit(solution)/shard_map/ppermute | solution.py:353
  30.2 3.7 %collective-permute-start.10 = (bf16[128,1024]{1,0:T(8,128)(2,1)S(1)}, bf16[128,1024]{1,0:T(8,128)(2,1)}, u32[]{:S(2)}, u32[]{:S(2)}) collective-permute-start(bf16[128,1024]{1,0:T(8,128)(2,1)S(1)} %collective-permute-done.9.refs_14_), channel_id=1, source_target_pairs={{0,7},{1,0},{2,1},{3,2},{4,3},{5,4},{6,5},{7,6},{8,15},{9,8},{10,9... | collective-permute-start | bytes 786440 | tf_op jit(solution)/shard_map/ppermute | solution.py:353
  35.8 3.7 %collective-permute-start.13 = (bf16[128,1024]{1,0:T(8,128)(2,1)S(1)}, bf16[128,1024]{1,0:T(8,128)(2,1)}, u32[]{:S(2)}, u32[]{:S(2)}) collective-permute-start(bf16[128,1024]{1,0:T(8,128)(2,1)S(1)} %collective-permute-done.12.refs_13_), channel_id=1, source_target_pairs={{0,7},{1,0},{2,1},{3,2},{4,3},{5,4},{6,5},{7,6},{8,15},{9,8},{10,9... | collective-permute-start | bytes 786440 | tf_op jit(solution)/shard_map/ppermute | solution.py:353
  41.4 3.8 %collective-permute-start.11 = (bf16[128,1024]{1,0:T(8,128)(2,1)}, bf16[128,1024]{1,0:T(8,128)(2,1)}, u32[]{:S(2)}, u32[]{:S(2)}) collective-permute-start(bf16[128,1024]{1,0:T(8,128)(2,1)} %collective-permute-done.10.refs_12_), channel_id=1, source_target_pairs={{0,7},{1,0},{2,1},{3,2},{4,3},{5,4},{6,5},{7,6},{8,15},{9,8},{10,9... | collective-permute-start | bytes 786440 | tf_op jit(solution)/shard_map/ppermute | solution.py:353
  47.0 7.1 %messages.1 = (f32[256,1024]{1,0:T(8,128)}, bf16[256,1024]{1,0:T(8,128)(2,1)}, f32[256,1024]{1,0:T(8,128)}, bf16[256,1024]{1,0:T(8,128)(2,1)}) custom-call(s32[2]{0:T(128)} %pad_add_fusion.place_ref.refs_0_, s32[2,4]{1,0:T(2,128)} %refs_1_.2, s32[2]{0:T(128)} %refs_2_.1, bf16[128,1024]{1,0:T(8,128)(2,1)} %copy-done.6, bf16[128,1024]{1,0:T(8,128)(2,1)} %copy-done.11, ...), custom_call_target="tpu_custom_call" | custom-call | flops 2147483648 | bytes 8388608 | tf_op jit(solution)/shard_map/messages/pallas_call | solution.py:46
  54.2 3.9 %collective-permute-start.14 = (bf16[256,1024]{1,0:T(8,128)(2,1)}, bf16[256,1024]{1,0:T(8,128)(2,1)S(1)}, u32[]{:S(2)}, u32[]{:S(2)}) collective-permute-start(bf16[256,1024]{1,0:T(8,128)(2,1)} %get-tuple-element.60), channel_id=1, source_target_pairs={{0,7},{1,0},{2,1},{3,2},{4,3},{5,4},{6,5},{7,6},{8,15},{9,8},{10,9... | collective-permute-start | bytes 1572872 | tf_op jit(solution)/shard_map/ppermute | solution.py:353
  58.1 6.1 %all-to-all-start = ((bf16[8,64,256]{2,1,0:T(8,128)(2,1)}), bf16[8,64,256]{2,1,0:T(8,128)(2,1)S(1)}, u32[]{:S(2)}, u32[]{:S(2)}) async-start(bf16[8,64,256]{2,1,0:T(8,128)(2,1)} %d_out.1), calls=%async_computation | async-start | bytes 524288 | tf_op jit(solution)/shard_map/all_to_all | solution.py:349
  64.2 13.6 %attend_forward.1 = (bf16[8,64,256]{2,1,0:T(8,128)(2,1)}, bf16[8,256,128]{2,1,0:T(8,128)(2,1)}, bf16[8,64,256]{2,1,0:T(8,128)(2,1)}, bf16[8,64,256]{2,1,0:T(8,12...) custom-call(s32[2]{0:T(128)} %pad_add_fusion.place_ref.refs_0_, bf16[128,1024]{1,0:T(8,128)(2,1)} %normalize.2.refs_5_.refs_1_, ...), custom_call_target="tpu_custom_call" | custom-call | flops 3221225472 | bytes 8388608 | tf_op jit(solution)/shard_map/attend_forward/pallas_call | solution.py:46
  78.8 2.9 %merge.1 = (bf16[8,192,256]{2,1,0:T(8,128)(2,1)}, bf16[256,1024]{1,0:T(8,128)(2,1)}) custom-call(bf16[8,64,256]{2,1,0:T(8,128)(2,1)} %get-tuple-element.53.heads_ref.refs_1_, f32[256,1024]{1,0:T(8,128)} %get-tuple-element.59.mid_ref, bf16[256,1024]{1,0:T(8,128)(2,1)} %copy-done.4, bf16[256,1024]{1,0:T(8,128)(2,1)} %copy-done.5), custom_call_target="tpu_custom_call" | custom-call | bytes 4194304 | tf_op jit(solution)/shard_map/merge/pallas_call | solution.py:46
  82.4 7.2 %all-to-all-start.1 = ((bf16[8,192,256]{2,1,0:T(8,128)(2,1)}), bf16[8,192,256]{2,1,0:T(8,128)(2,1)S(1)}, u32[]{:S(2)}, u32[]{:S(2)}) async-start(bf16[8,192,256]{2,1,0:T(8,128)(2,1)} %get-tuple-element.65), calls=%async_computation.1 | async-start | bytes 1572864 | tf_op jit(solution)/shard_map/all_to_all | solution.py:349
  89.6 15.3 %attend_backward.1.refs_18_ = bf16[8,192,256]{2,1,0:T(8,128)(2,1)} custom-call(s32[2]{0:T(128)} %pad_add_fusion.place_ref.refs_0_, bf16[8,64,256]{2,1,0:T(8,128)(2,1)} %get-tuple-element.53.heads_ref.refs_1_, bf16[8,256,128]{2,1,0:T(8,128)(2,1)} %get-tuple-element.54.refs_2_, bf16[8,64,256]{2,1,0:T(8,128)(2,1)} %get-tuple-element.55.refs_3_, ...), custom_call_target="tpu_custom_call" | custom-call | flops 6442450944 | bytes 4194304 | tf_op jit(solution)/shard_map/attend_backward/pallas_call | solution.py:46
  107.1 5.0 %all-to-all-start.2 = ((bf16[8,192,256]{2,1,0:T(8,128)(2,1)}), bf16[8,192,256]{2,1,0:T(8,128)(2,1)S(1)}, u32[]{:S(2)}, u32[]{:S(2)}) async-start(bf16[8,192,256]{2,1,0:T(8,128)(2,1)} %attend_backward.1.refs_18_), calls=%async_computation.2 | async-start | bytes 1572864 | tf_op jit(solution)/shard_map/all_to_all | solution.py:349
  112.1 7.6 %result.1 = (bf16[256,1024]{1,0:T(8,128)(2,1)}, bf16[16,224,128]{2,1,0:T(8,128)(2,1)}, bf16[16,224,128]{2,1,0:T(8,128)(2,1)}) custom-call(s32[2]{0:T(128)} %pad_add_fusion.place_ref.refs_0_, bf16[128,1024]{1,0:T(8,128)(2,1)} %normalize.2.refs_5_.refs_1_, bf16[128,1024]{1,0:T(8,128)(2,1)} %normalize.3.refs_6_.refs_2_, bf16[128,1024]{1,0:T(8,128)(2,1)} %copy-done.6, ...), custom_call_target="tpu_custom_call" | custom-call | flops 2147483648 | bytes 10485760 | tf_op jit(solution)/shard_map/result/pallas_call | solution.py:46
  119.8 2.7 %collective-permute-done.16 = bf16[16,224,128]{2,1,0:T(8,128)(2,1)S(1)} collective-permute-done((bf16[16,224,128]{2,1,0:T(8,128)(2,1)}, bf16[16,224,128]{2,1,0:T(8,128)(2,1)S(1)}, u32[]{:S(2)}, u32[]{:S(2)}) %collective-permute-start.16) | collective-permute-done | bytes 917536 | tf_op jit(solution)/shard_map/ppermute | solution.py:458
  123.9 5.2 %all-to-all-done.2.refs_0_ = bf16[8,192,256]{2,1,0:T(8,128)(2,1)S(1)} async-done(((bf16[8,192,256]{2,1,0:T(8,128)(2,1)}), bf16[8,192,256]{2,1,0:T(8,128)(2,1)S(1)}, u32[]{:S(2)}, u32[]{:S(2)}) %all-to-all-start.2) | async-done | bytes 786464 | tf_op jit(solution)/shard_map/all_to_all | solution.py:349
  129.2 17.4 %all_to_all.25.shares_ref = bf16[16,224,128]{2,1,0:T(8,128)(2,1)} all-to-all(bf16[16,224,128]{2,1,0:T(8,128)(2,1)S(1)} %add_convert_fusion), channel_id=1, replica_groups=mesh['x'=4,'y'=4,'c'=2,'z'=8] {'x','y'}, dimensions={0} | all-to-all | bytes 1835008 | tf_op jit(solution)/shard_map/all_to_all | solution.py:349
  148.7 5.8 %all-to-all-start.4 = ((bf16[8,224,128]{2,1,0:T(8,128)(2,1)}), bf16[8,224,128]{2,1,0:T(8,128)(2,1)S(1)}, u32[]{:S(2)}, u32[]{:S(2)}) async-start(bf16[8,224,128]{2,1,0:T(8,128)(2,1)} %share_sum.1), calls=%async_computation.4 | async-start | bytes 917504 | tf_op jit(solution)/shard_map/all_to_all | solution.py:349
  158.8 5.8 %input_grad.1 = bf16[256,1024]{1,0:T(8,128)(2,1)} custom-call(bf16[8,192,256]{2,1,0:T(8,128)(2,1)} %copy-done, bf16[1024,1536]{1,0:T(8,128)(2,1)} %refs_1_.3, bf16[256,1024]{1,0:T(8,128)(2,1)} %get-tuple-element.75.refs_2_, bf16[1024,1024]{1,0:T(8,128)(2,1)} %refs_3_.1, bf16[256,1024]{1,0:T(8,128)(2,1)} %refs_4_.1, bf16[256,1024]{1,0:T(8,128)(2,1)} %refs_5_.1, ...), custom_call_target="tpu_custom_call" | custom-call | flops 805306368 | bytes 8388608 | tf_op jit(solution)/shard_map/input_grad/pallas_call | solution.py:46
  164.6 4.8 %all-to-all-done.4.every_ref = bf16[8,224,128]{2,1,0:T(8,128)(2,1)S(1)} async-done(((bf16[8,224,128]{2,1,0:T(8,128)(2,1)}), bf16[8,224,128]{2,1,0:T(8,128)(2,1)S(1)}, u32[]{:S(2)}, u32[]{:S(2)}) %all-to-all-start.4) | async-done | bytes 458784 | tf_op jit(solution)/shard_map/all_to_all | solution.py:349
  (66 shorter events, 30.9 us)
Async XLA Ops:
  2.5 15.9 %collective-permute-start = (bf16[128,1024]{1,0:T(8,128)(2,1)}, bf16[128,1024]{1,0:T(8,128)(2,1)S(1)}, u32[]{:S(2)}, u32[]{:S(2)}) collective-permute-start(bf16[128,1024]{1,0:T(8,128)(2,1)} %normalize.2.refs_5_.refs_1_), channel_id=1, source_target_pairs={{0,1},{1,2},{2,3},{3,4},{4,5},{5,6},{6,7},{7,0},{8,9},{9,10},{10,1... | collective-permute-start | bytes 786440 | tf_op jit(solution)/shard_map/ppermute | solution.py:353
  4.4 14.0 %collective-permute-start.1 = (bf16[128,1024]{1,0:T(8,128)(2,1)}, bf16[128,1024]{1,0:T(8,128)(2,1)S(1)}, u32[]{:S(2)}, u32[]{:S(2)}) collective-permute-start(bf16[128,1024]{1,0:T(8,128)(2,1)} %normalize.2.refs_5_.refs_1_), channel_id=1, source_target_pairs={{0,7},{1,0},{2,1},{3,2},{4,3},{5,4},{6,5},{7,6},{8,15},{9,8},{10,9... | collective-permute-start | bytes 786440 | tf_op jit(solution)/shard_map/ppermute | solution.py:353
  10.1 9.7 %collective-permute-start.8 = (bf16[128,1024]{1,0:T(8,128)(2,1)}, bf16[128,1024]{1,0:T(8,128)(2,1)S(1)}, u32[]{:S(2)}, u32[]{:S(2)}) collective-permute-start(bf16[128,1024]{1,0:T(8,128)(2,1)} %normalize.3.refs_6_.refs_2_), channel_id=1, source_target_pairs={{0,7},{1,0},{2,1},{3,2},{4,3},{5,4},{6,5},{7,6},{8,15},{9,8},{10,9... | collective-permute-start | bytes 786440 | tf_op jit(solution)/shard_map/ppermute | solution.py:353
  18.4 28.6 %copy-start.6 = (bf16[128,1024]{1,0:T(8,128)(2,1)}, bf16[128,1024]{1,0:T(8,128)(2,1)S(1)}, u32[]{:S(2)}) copy-start(bf16[128,1024]{1,0:T(8,128)(2,1)S(1)} %collective-permute-done.refs_3_) | copy-start | bytes 786436
  18.4 28.6 %copy-start.7 = (bf16[128,1024]{1,0:T(8,128)(2,1)}, bf16[128,1024]{1,0:T(8,128)(2,1)S(1)}, u32[]{:S(2)}) copy-start(bf16[128,1024]{1,0:T(8,128)(2,1)S(1)} %collective-permute-done.1.refs_7_.refs_15_) | copy-start | bytes 786436
  18.4 9.4 %collective-permute-start.3 = (bf16[128,1024]{1,0:T(8,128)(2,1)S(1)}, bf16[128,1024]{1,0:T(8,128)(2,1)S(1)}, u32[]{:S(2)}, u32[]{:S(2)}) collective-permute-start(bf16[128,1024]{1,0:T(8,128)(2,1)S(1)} %collective-permute-done.refs_3_), channel_id=1, source_target_pairs={{0,1},{1,2},{2,3},{3,4},{4,5},{5,6},{6,7},{7,0},{8,9},{9,10},{10,1... | collective-permute-start | bytes 786440 | tf_op jit(solution)/shard_map/ppermute | solution.py:353
  19.8 10.3 %collective-permute-start.9 = (bf16[128,1024]{1,0:T(8,128)(2,1)S(1)}, bf16[128,1024]{1,0:T(8,128)(2,1)S(1)}, u32[]{:S(2)}, u32[]{:S(2)}) collective-permute-start(bf16[128,1024]{1,0:T(8,128)(2,1)S(1)} %collective-permute-done.8.refs_8_.refs_16_), channel_id=1, source_target_pairs={{0,7},{1,0},{2,1},{3,2},{4,3},{5,4},{6,5},{7,6},{8,15},{9,8},{10,9... | collective-permute-start | bytes 786440 | tf_op jit(solution)/shard_map/ppermute | solution.py:353
  23.4 10.5 %collective-permute-start.2 = (bf16[128,1024]{1,0:T(8,128)(2,1)S(1)}, bf16[128,1024]{1,0:T(8,128)(2,1)S(1)}, u32[]{:S(2)}, u32[]{:S(2)}) collective-permute-start(bf16[128,1024]{1,0:T(8,128)(2,1)S(1)} %copy-done.3), channel_id=1, source_target_pairs={{0,1},{1,2},{2,3},{3,4},{4,5},{5,6},{6,7},{7,0},{8,9},{9,10},{10,1... | collective-permute-start | bytes 786440 | tf_op jit(solution)/shard_map/ppermute | solution.py:353
  23.4 12.4 %collective-permute-start.12 = (bf16[128,1024]{1,0:T(8,128)(2,1)S(1)}, bf16[128,1024]{1,0:T(8,128)(2,1)S(1)}, u32[]{:S(2)}, u32[]{:S(2)}) collective-permute-start(bf16[128,1024]{1,0:T(8,128)(2,1)S(1)} %collective-permute-done.1.refs_7_.refs_15_), channel_id=1, source_target_pairs={{0,7},{1,0},{2,1},{3,2},{4,3},{5,4},{6,5},{7,6},{8,15},{9,8},{10,9... | collective-permute-start | bytes 786440 | tf_op jit(solution)/shard_map/ppermute | solution.py:353
  27.8 11.7 %collective-permute-start.5 = (bf16[128,1024]{1,0:T(8,128)(2,1)S(1)}, bf16[128,1024]{1,0:T(8,128)(2,1)}, u32[]{:S(2)}, u32[]{:S(2)}) collective-permute-start(bf16[128,1024]{1,0:T(8,128)(2,1)S(1)} %collective-permute-done.3.refs_5_), channel_id=1, source_target_pairs={{0,1},{1,2},{2,3},{3,4},{4,5},{5,6},{6,7},{7,0},{8,9},{9,10},{10,1... | collective-permute-start | bytes 786440 | tf_op jit(solution)/shard_map/ppermute | solution.py:353
  30.2 11.2 %collective-permute-start.10 = (bf16[128,1024]{1,0:T(8,128)(2,1)S(1)}, bf16[128,1024]{1,0:T(8,128)(2,1)}, u32[]{:S(2)}, u32[]{:S(2)}) collective-permute-start(bf16[128,1024]{1,0:T(8,128)(2,1)S(1)} %collective-permute-done.9.refs_14_), channel_id=1, source_target_pairs={{0,7},{1,0},{2,1},{3,2},{4,3},{5,4},{6,5},{7,6},{8,15},{9,8},{10,9... | collective-permute-start | bytes 786440 | tf_op jit(solution)/shard_map/ppermute | solution.py:353
  33.9 11.3 %collective-permute-start.4 = (bf16[128,1024]{1,0:T(8,128)(2,1)S(1)}, bf16[128,1024]{1,0:T(8,128)(2,1)S(1)}, u32[]{:S(2)}, u32[]{:S(2)}) collective-permute-start(bf16[128,1024]{1,0:T(8,128)(2,1)S(1)} %collective-permute-done.2.refs_4_), channel_id=1, source_target_pairs={{0,1},{1,2},{2,3},{3,4},{4,5},{5,6},{6,7},{7,0},{8,9},{9,10},{10,1... | collective-permute-start | bytes 786440 | tf_op jit(solution)/shard_map/ppermute | solution.py:353
  35.8 11.2 %collective-permute-start.13 = (bf16[128,1024]{1,0:T(8,128)(2,1)S(1)}, bf16[128,1024]{1,0:T(8,128)(2,1)}, u32[]{:S(2)}, u32[]{:S(2)}) collective-permute-start(bf16[128,1024]{1,0:T(8,128)(2,1)S(1)} %collective-permute-done.12.refs_13_), channel_id=1, source_target_pairs={{0,7},{1,0},{2,1},{3,2},{4,3},{5,4},{6,5},{7,6},{8,15},{9,8},{10,9... | collective-permute-start | bytes 786440 | tf_op jit(solution)/shard_map/ppermute | solution.py:353
  39.6 14.6 %collective-permute-start.7 = (bf16[128,1024]{1,0:T(8,128)(2,1)}, bf16[128,1024]{1,0:T(8,128)(2,1)}, u32[]{:S(2)}, u32[]{:S(2)}) collective-permute-start(bf16[128,1024]{1,0:T(8,128)(2,1)} %collective-permute-done.5.refs_7_), channel_id=1, source_target_pairs={{0,1},{1,2},{2,3},{3,4},{4,5},{5,6},{6,7},{7,0},{8,9},{9,10},{10,1... | collective-permute-start | bytes 786440 | tf_op jit(solution)/shard_map/ppermute | solution.py:353
  41.4 12.8 %collective-permute-start.11 = (bf16[128,1024]{1,0:T(8,128)(2,1)}, bf16[128,1024]{1,0:T(8,128)(2,1)}, u32[]{:S(2)}, u32[]{:S(2)}) collective-permute-start(bf16[128,1024]{1,0:T(8,128)(2,1)} %collective-permute-done.10.refs_12_), channel_id=1, source_target_pairs={{0,7},{1,0},{2,1},{3,2},{4,3},{5,4},{6,5},{7,6},{8,15},{9,8},{10,9... | collective-permute-start | bytes 786440 | tf_op jit(solution)/shard_map/ppermute | solution.py:353
  45.2 19.0 %collective-permute-start.6 = (bf16[128,1024]{1,0:T(8,128)(2,1)S(1)}, bf16[128,1024]{1,0:T(8,128)(2,1)}, u32[]{:S(2)}, u32[]{:S(2)}) collective-permute-start(bf16[128,1024]{1,0:T(8,128)(2,1)S(1)} %collective-permute-done.4.refs_6_), channel_id=1, source_target_pairs={{0,1},{1,2},{2,3},{3,4},{4,5},{5,6},{6,7},{7,0},{8,9},{9,10},{10,1... | collective-permute-start | bytes 786440 | tf_op jit(solution)/shard_map/ppermute | solution.py:353
  54.2 23.6 %collective-permute-start.14 = (bf16[256,1024]{1,0:T(8,128)(2,1)}, bf16[256,1024]{1,0:T(8,128)(2,1)S(1)}, u32[]{:S(2)}, u32[]{:S(2)}) collective-permute-start(bf16[256,1024]{1,0:T(8,128)(2,1)} %get-tuple-element.60), channel_id=1, source_target_pairs={{0,7},{1,0},{2,1},{3,2},{4,3},{5,4},{6,5},{7,6},{8,15},{9,8},{10,9... | collective-permute-start | bytes 1572872 | tf_op jit(solution)/shard_map/ppermute | solution.py:353
  58.1 19.8 %collective-permute-start.15 = (bf16[256,1024]{1,0:T(8,128)(2,1)}, bf16[256,1024]{1,0:T(8,128)(2,1)S(1)}, u32[]{:S(2)}, u32[]{:S(2)}) collective-permute-start(bf16[256,1024]{1,0:T(8,128)(2,1)} %get-tuple-element.61), channel_id=1, source_target_pairs={{0,1},{1,2},{2,3},{3,4},{4,5},{5,6},{6,7},{7,0},{8,9},{9,10},{10,1... | collective-permute-start | bytes 1572872 | tf_op jit(solution)/shard_map/ppermute | solution.py:353
  58.1 23.6 %all-to-all-start = ((bf16[8,64,256]{2,1,0:T(8,128)(2,1)}), bf16[8,64,256]{2,1,0:T(8,128)(2,1)S(1)}, u32[]{:S(2)}, u32[]{:S(2)}) async-start(bf16[8,64,256]{2,1,0:T(8,128)(2,1)} %d_out.1), calls=%async_computation | async-start | bytes 524288 | tf_op jit(solution)/shard_map/all_to_all | solution.py:349
  82.4 24.8 %all-to-all-start.1 = ((bf16[8,192,256]{2,1,0:T(8,128)(2,1)}), bf16[8,192,256]{2,1,0:T(8,128)(2,1)S(1)}, u32[]{:S(2)}, u32[]{:S(2)}) async-start(bf16[8,192,256]{2,1,0:T(8,128)(2,1)} %get-tuple-element.65), calls=%async_computation.1 | async-start | bytes 1572864 | tf_op jit(solution)/shard_map/all_to_all | solution.py:349
  107.1 22.1 %all-to-all-start.2 = ((bf16[8,192,256]{2,1,0:T(8,128)(2,1)}), bf16[8,192,256]{2,1,0:T(8,128)(2,1)S(1)}, u32[]{:S(2)}, u32[]{:S(2)}) async-start(bf16[8,192,256]{2,1,0:T(8,128)(2,1)} %attend_backward.1.refs_18_), calls=%async_computation.2 | async-start | bytes 1572864 | tf_op jit(solution)/shard_map/all_to_all | solution.py:349
  119.8 2.8 %collective-permute-start.16 = (bf16[16,224,128]{2,1,0:T(8,128)(2,1)}, bf16[16,224,128]{2,1,0:T(8,128)(2,1)S(1)}, u32[]{:S(2)}, u32[]{:S(2)}) collective-permute-start(bf16[16,224,128]{2,1,0:T(8,128)(2,1)} %get-tuple-element.71), channel_id=1, source_target_pairs={{0,8},{8,0},{1,9},{9,1},{2,10},{10,2},{3,11},{11,3},{4,12},{12,4},... | collective-permute-start | bytes 2752520 | tf_op jit(solution)/shard_map/ppermute | solution.py:458
  129.2 28.1 %copy-start = (bf16[8,192,256]{2,1,0:T(8,128)(2,1)}, bf16[8,192,256]{2,1,0:T(8,128)(2,1)S(1)}, u32[]{:S(2)}) copy-start(bf16[8,192,256]{2,1,0:T(8,128)(2,1)S(1)} %all-to-all-done.2.refs_0_) | copy-start | bytes 2359300
  148.7 20.8 %all-to-all-start.4 = ((bf16[8,224,128]{2,1,0:T(8,128)(2,1)}), bf16[8,224,128]{2,1,0:T(8,128)(2,1)S(1)}, u32[]{:S(2)}, u32[]{:S(2)}) async-start(bf16[8,224,128]{2,1,0:T(8,128)(2,1)} %share_sum.1), calls=%async_computation.4 | async-start | bytes 917504 | tf_op jit(solution)/shard_map/all_to_all | solution.py:349
  (12 other events, 127.9 us)

commit v5 on v4

--- a/solution.py
+++ b/solution.py
@@ -82,13 +82,20 @@
         out_ref[h] = turned[h * HEAD_DIM : (h + 1) * HEAD_DIM]
 
 
-def pick_kernel(place_ref, q_ref, k_ref, v_ref, out_ref, turned):
-    odd = lax.rem(place_ref[0], 2)
-    for t, ref in enumerate((q_ref, k_ref, v_ref)):
-        turned[...] = ref[...].astype(jnp.float32).T
-        out_ref[t * HEAD_DIM : (t + 1) * HEAD_DIM] = turned[
-            pl.ds(odd * HEAD_DIM, HEAD_DIM), :
-        ].astype(jnp.bfloat16)
+def pick_kernel(place_ref, q_ref, k_ref, v_ref, out_ref):
+    odd = lax.rem(place_ref[0], 2) == 1
+
+    def halves(ref):
+        wide = ref[...].astype(jnp.float32)
+        swapped = jnp.concatenate([wide[:, HEAD_DIM:], wide[:, :HEAD_DIM]], axis=1)
+        return jnp.where(odd, swapped, wide), jnp.where(odd, wide, swapped)
+
+    left = lax.broadcasted_iota(jnp.int32, q_ref.shape, 1) < HEAD_DIM
+    query, _ = halves(q_ref)
+    _, keyrow = halves(k_ref)
+    val, _ = halves(v_ref)
+    out_ref[:, : 2 * HEAD_DIM] = jnp.where(left, query, keyrow).astype(jnp.bfloat16)
+    out_ref[:, 2 * HEAD_DIM :] = jnp.where(left, val, 0.0).astype(jnp.bfloat16)
 
 
 def pick_head(place, w_qkv):
@@ -104,10 +111,9 @@
             num_scalar_prefetch=1,
             grid=(1,),
             in_specs=[block(0), block(1), block(2)],
-            out_specs=pl.BlockSpec((3 * HEAD_DIM, width), lambda i, place: (0, 0)),
-            scratch_shapes=[pltpu.VMEM((2 * HEAD_DIM, width), jnp.float32)],
+            out_specs=pl.BlockSpec((width, 4 * HEAD_DIM), lambda i, place: (0, 0)),
         ),
-        out_shape=jax.ShapeDtypeStruct((3 * HEAD_DIM, width), jnp.bfloat16),
+        out_shape=jax.ShapeDtypeStruct((width, 4 * HEAD_DIM), jnp.bfloat16),
         cost_estimate=pl.CostEstimate(flops=0, bytes_accessed=4 << 20, transcendentals=0),
         name="pick_head",
     )(place, w_qkv, w_qkv, w_qkv)
@@ -197,11 +203,11 @@
     wait = fetch_chunks(refs[1:17], held, sems)
     for j in range(N_SEQ):
         wait(j)
-        proj = contract_cols(w_ref[...], held[j]).astype(jnp.bfloat16)
+        proj = matmul(held[j], w_ref[...]).T.astype(jnp.bfloat16)
         raw_ref[j] = proj[: 2 * HEAD_DIM]
         query = proj[:HEAD_DIM].astype(jnp.float32)
         keyrow = proj[HEAD_DIM : 2 * HEAD_DIM].astype(jnp.float32)
-        val = proj[2 * HEAD_DIM :]
+        val = proj[2 * HEAD_DIM : 3 * HEAD_DIM]
         q_unit = (query * unit_factor(query, 0)).astype(jnp.bfloat16).astype(jnp.float32) * SCALE
         k_unit = keyrow * unit_factor(keyrow, 0)
         hq_ref[j] = q_unit.astype(jnp.bfloat16)
@@ -403,18 +409,18 @@
     act, to_low, mid, to_high = call(
         message_kernel, "messages", (wide_shape, low_shape, wide_shape, low_shape),
         (place, block_ids, block_counts),
-        (after(a_up[1], a_up[3], a_down[3]), b_up[1], n_a, n_b, a_down[1], b_down[1], w_msg, edge_tiles, out_grad),
+        (after(a_up[1], a_up[2], a_down[2]), b_up[1], n_a, n_b, a_down[1], b_down[1], w_msg, edge_tiles, out_grad),
         [pltpu.VMEM((6, BLOCK, width), bf16), pltpu.VMEM((6, BLOCK, width), f32)],
         flops=8 * node_rows * width * width, exps=node_rows * width, moved=8 << 20,
     )
+    d_heads = exchange(after(d_out, a_up[3], a_down[3]), "z")
     b_up.append(up(b_up[2]))
     b_down.append(down(b_down[2]))
     c4 = [up(a_up[3]), down(b_down[3])]
-    *c4, to_low, to_high, d_out = lax.optimization_barrier((*c4, to_low, to_high, d_out))
+    *c4, to_low, to_high = lax.optimization_barrier((*c4, to_low, to_high))
     above, below = down(to_low), up(to_high)
     pairs = list(zip(a_up, b_up)) + [c4] + list(zip(a_down, b_down))[:0:-1]
     chunks = tuple(half for pair in pairs for half in pair)
-    d_heads = exchange(d_out, "z")
 
     held = pltpu.VMEM((N_SEQ, CHUNK, width), bf16)
     lanes_in = ((N_SEQ, CHUNK, 2 * HEAD_DIM), bf16)

time: 173 us -> 173 us (level)
    ppermute x16, starting transfers between devices: 30.1 us -> 24.8 us  [shift(): lax.ppermute(array, 'z', [(i, (i + distance) % N_SEQ) for i in range(N_SE...]
    all_to_all x4, starting transfers between devices: 24.2 us -> 27.8 us  [exchange(): return lax.all_to_all(array, axis, split_axis=0, concat_axis=0, tiled=True)]
    ppermute x16, waiting for transfers between devices: 10.2 us -> 13.8 us  [shift(): lax.ppermute(array, 'z', [(i, (i + distance) % N_SEQ) for i in range(N_SE...]
    all_to_all x4, waiting for transfers between devices: 12.3 us -> 9.79 us  [exchange(): return lax.all_to_all(array, axis, split_axis=0, concat_axis=0, tiled=True)]
  transfers between devices with their start and end apart: 21 -> 21, of which waited for: 11 -> 9; matrix products, arithmetic and copies ran while one was open for 4% -> 4% of each run, Pallas kernels for 35% -> 35%
where the time goes in v5:
time: 173 us; the launch traced here: 172 us
  Pallas kernels  66.3 us (38%)
  starting transfers between devices  52.7 us (30%)
  waiting for transfers between devices  26.3 us (15%)
  blocking collectives  17.4 us (10%)
  local copies, waits for them, and re-layouts  6.78 us (4%)
  other arithmetic  2 us (1%)
    pallas_call x9, Pallas kernels, call(): pl.pallas_call(kernel, out_shape=tuple((jax.ShapeDtypeStruct(s, t) for s,...  59.6 us
    all_to_all x4, starting transfers between devices, exchange(): return lax.all_to_all(array, axis, split_axis=0, concat_axis=0, tiled=True)  27.8 us
    ppermute x16, starting transfers between devices, shift(): lax.ppermute(array, 'z', [(i, (i + distance) % N_SEQ) for i in range(N_SE...  24.8 us
    all_to_all x1, blocking collectives, exchange(): return lax.all_to_all(array, axis, split_axis=0, concat_axis=0, tiled=True)  17.4 us
    ppermute x16, waiting for transfers between devices, shift(): lax.ppermute(array, 'z', [(i, (i + distance) % N_SEQ) for i in range(N_SE...  13.8 us
    all_to_all x4, waiting for transfers between devices, exchange(): return lax.all_to_all(array, axis, split_axis=0, concat_axis=0, tiled=True)  9.79 us
    pallas_call x2, Pallas kernels, normalize_half(): pl.pallas_call(normalize_kernel, grid=(1,), in_specs=[pl.BlockSpec((BLOCK...  3.63 us
  transfers between devices with their start and end apart: 21, of which 9 were waited for; matrix products, arithmetic and copies ran while one was open for 4% of the time, Pallas kernels for 35%

profile of v5, /device:TPU:6, one launch (start us, length us, event | category | flops | bytes accessed | tf_op | source)
XLA Modules:
  0.0 172.3 jit_solution(5763568534262462111)
XLA Ops:
  4.4 3.9 %collective-permute-start.1 = (bf16[128,1024]{1,0:T(8,128)(2,1)}, bf16[128,1024]{1,0:T(8,128)(2,1)S(1)}, u32[]{:S(2)}, u32[]{:S(2)}) collective-permute-start(bf16[128,1024]{1,0:T(8,128)(2,1)} %normalize.2.refs_5_.refs_1_), channel_id=1, source_target_pairs={{0,7},{1,0},{2,1},{3,2},{4,3},{5,4},{6,5},{7,6},{8,15},{9,8},{10,9... | collective-permute-start | bytes 786440 | tf_op jit(solution)/shard_map/ppermute | solution.py:359
  12.7 3.1 %pick_head.1.refs_17_ = bf16[1024,256]{1,0:T(8,128)(2,1)} custom-call(s32[2]{0:T(128)} %pad_add_fusion.place_ref.refs_0_, bf16[1024,1536]{1,0:T(8,128)(2,1)} %refs_1_.3, bf16[1024,1536]{1,0:T(8,128)(2,1)} %refs_1_.3, bf16[1024,1536]{1,0:T(8,128)(2,1)} %refs_1_.3), custom_call_target="tpu_custom_call" | custom-call | bytes 4194304 | tf_op jit(solution)/shard_map/pick_head/pallas_call | solution.py:108
  15.8 2.6 %d_out.1 = bf16[8,64,256]{2,1,0:T(8,128)(2,1)} custom-call(bf16[256,1024]{1,0:T(8,128)(2,1)} %refs_5_.1, bf16[512,1024]{1,0:T(8,128)(2,1)} %refs_19_.1), custom_call_target="tpu_custom_call" | custom-call | flops 268435456 | bytes 2097152 | tf_op jit(solution)/shard_map/d_out/pallas_call | solution.py:46
  19.8 3.6 %collective-permute-start.9 = (bf16[128,1024]{1,0:T(8,128)(2,1)S(1)}, bf16[128,1024]{1,0:T(8,128)(2,1)S(1)}, u32[]{:S(2)}, u32[]{:S(2)}) collective-permute-start(bf16[128,1024]{1,0:T(8,128)(2,1)S(1)} %collective-permute-done.8.refs_8_.refs_16_), channel_id=1, source_target_pairs={{0,7},{1,0},{2,1},{3,2},{4,3},{5,4},{6,5},{7,6},{8,15},{9,8},{10,9... | collective-permute-start | bytes 786440 | tf_op jit(solution)/shard_map/ppermute | solution.py:359
  23.4 4.4 %collective-permute-done.3.refs_5_ = bf16[128,1024]{1,0:T(8,128)(2,1)S(1)} collective-permute-done((bf16[128,1024]{1,0:T(8,128)(2,1)S(1)}, bf16[128,1024]{1,0:T(8,128)(2,1)S(1)}, u32[]{:S(2)}, u32[]{:S(2)}) %collective-permute-start.3) | collective-permute-done | bytes 262176 | tf_op jit(solution)/shard_map/ppermute | solution.py:359
  28.1 3.7 %collective-permute-start.10 = (bf16[128,1024]{1,0:T(8,128)(2,1)S(1)}, bf16[128,1024]{1,0:T(8,128)(2,1)}, u32[]{:S(2)}, u32[]{:S(2)}) collective-permute-start(bf16[128,1024]{1,0:T(8,128)(2,1)S(1)} %collective-permute-done.9.refs_14_), channel_id=1, source_target_pairs={{0,7},{1,0},{2,1},{3,2},{4,3},{5,4},{6,5},{7,6},{8,15},{9,8},{10,9... | collective-permute-start | bytes 786440 | tf_op jit(solution)/shard_map/ppermute | solution.py:359
  33.9 5.7 %collective-permute-done.5.refs_7_ = bf16[128,1024]{1,0:T(8,128)(2,1)} collective-permute-done((bf16[128,1024]{1,0:T(8,128)(2,1)S(1)}, bf16[128,1024]{1,0:T(8,128)(2,1)}, u32[]{:S(2)}, u32[]{:S(2)}) %collective-permute-start.5) | collective-permute-done | bytes 262176 | tf_op jit(solution)/shard_map/ppermute | solution.py:359
  39.6 3.2 %collective-permute-start.11 = (bf16[128,1024]{1,0:T(8,128)(2,1)}, bf16[128,1024]{1,0:T(8,128)(2,1)}, u32[]{:S(2)}, u32[]{:S(2)}) collective-permute-start(bf16[128,1024]{1,0:T(8,128)(2,1)} %collective-permute-done.10.refs_12_), channel_id=1, source_target_pairs={{0,7},{1,0},{2,1},{3,2},{4,3},{5,4},{6,5},{7,6},{8,15},{9,8},{10,9... | collective-permute-start | bytes 786440 | tf_op jit(solution)/shard_map/ppermute | solution.py:359
  42.8 3.0 %collective-permute-start.13 = (bf16[128,1024]{1,0:T(8,128)(2,1)}, bf16[128,1024]{1,0:T(8,128)(2,1)}, u32[]{:S(2)}, u32[]{:S(2)}) collective-permute-start(bf16[128,1024]{1,0:T(8,128)(2,1)} %collective-permute-done.12.refs_13_), channel_id=1, source_target_pairs={{0,7},{1,0},{2,1},{3,2},{4,3},{5,4},{6,5},{7,6},{8,15},{9,8},{10,9... | collective-permute-start | bytes 786440 | tf_op jit(solution)/shard_map/ppermute | solution.py:359
  45.9 7.1 %messages.1 = (f32[256,1024]{1,0:T(8,128)}, bf16[256,1024]{1,0:T(8,128)(2,1)}, f32[256,1024]{1,0:T(8,128)}, bf16[256,1024]{1,0:T(8,128)(2,1)}) custom-call(s32[2]{0:T(128)} %pad_add_fusion.place_ref.refs_0_, s32[2,4]{1,0:T(2,128)} %refs_1_.2, s32[2]{0:T(128)} %refs_2_.1, bf16[128,1024]{1,0:T(8,128)(2,1)} %copy-done.6, bf16[128,1024]{1,0:T(8,128)(2,1)} %copy-done.11, ...), custom_call_target="tpu_custom_call" | custom-call | flops 2147483648 | bytes 8388608 | tf_op jit(solution)/shard_map/messages/pallas_call | solution.py:46
  53.1 3.3 %collective-permute-start.14 = (bf16[256,1024]{1,0:T(8,128)(2,1)}, bf16[256,1024]{1,0:T(8,128)(2,1)S(1)}, u32[]{:S(2)}, u32[]{:S(2)}) collective-permute-start(bf16[256,1024]{1,0:T(8,128)(2,1)} %get-tuple-element.59), channel_id=1, source_target_pairs={{0,7},{1,0},{2,1},{3,2},{4,3},{5,4},{6,5},{7,6},{8,15},{9,8},{10,9... | collective-permute-start | bytes 1572872 | tf_op jit(solution)/shard_map/ppermute | solution.py:359
  56.3 7.5 %all-to-all-start = ((bf16[8,64,256]{2,1,0:T(8,128)(2,1)}), bf16[8,64,256]{2,1,0:T(8,128)(2,1)S(1)}, u32[]{:S(2)}, u32[]{:S(2)}) async-start(bf16[8,64,256]{2,1,0:T(8,128)(2,1)} %d_out.1), calls=%async_computation | async-start | bytes 524288 | tf_op jit(solution)/shard_map/all_to_all | solution.py:355
  63.8 14.2 %attend_forward.1 = (bf16[8,64,256]{2,1,0:T(8,128)(2,1)}, bf16[8,256,128]{2,1,0:T(8,128)(2,1)}, bf16[8,64,256]{2,1,0:T(8,128)(2,1)}, bf16[8,64,256]{2,1,0:T(8,12...) custom-call(s32[2]{0:T(128)} %pad_add_fusion.place_ref.refs_0_, bf16[128,1024]{1,0:T(8,128)(2,1)} %normalize.2.refs_5_.refs_1_, ...), custom_call_target="tpu_custom_call" | custom-call | flops 3221225472 | bytes 8388608 | tf_op jit(solution)/shard_map/attend_forward/pallas_call | solution.py:46
  79.0 2.9 %merge.1 = (bf16[8,192,256]{2,1,0:T(8,128)(2,1)}, bf16[256,1024]{1,0:T(8,128)(2,1)}) custom-call(bf16[8,64,256]{2,1,0:T(8,128)(2,1)} %get-tuple-element.52.heads_ref.refs_1_, f32[256,1024]{1,0:T(8,128)} %get-tuple-element.58.mid_ref, bf16[256,1024]{1,0:T(8,128)(2,1)} %copy-done.4, bf16[256,1024]{1,0:T(8,128)(2,1)} %copy-done.5), custom_call_target="tpu_custom_call" | custom-call | bytes 4194304 | tf_op jit(solution)/shard_map/merge/pallas_call | solution.py:46
  82.5 7.2 %all-to-all-start.1 = ((bf16[8,192,256]{2,1,0:T(8,128)(2,1)}), bf16[8,192,256]{2,1,0:T(8,128)(2,1)S(1)}, u32[]{:S(2)}, u32[]{:S(2)}) async-start(bf16[8,192,256]{2,1,0:T(8,128)(2,1)} %get-tuple-element.65), calls=%async_computation.1 | async-start | bytes 1572864 | tf_op jit(solution)/shard_map/all_to_all | solution.py:355
  89.7 15.4 %attend_backward.1.refs_18_ = bf16[8,192,256]{2,1,0:T(8,128)(2,1)} custom-call(s32[2]{0:T(128)} %pad_add_fusion.place_ref.refs_0_, bf16[8,64,256]{2,1,0:T(8,128)(2,1)} %get-tuple-element.52.heads_ref.refs_1_, bf16[8,256,128]{2,1,0:T(8,128)(2,1)} %get-tuple-element.53.refs_2_, bf16[8,64,256]{2,1,0:T(8,128)(2,1)} %get-tuple-element.54.refs_3_, ...), custom_call_target="tpu_custom_call" | custom-call | flops 6442450944 | bytes 4194304 | tf_op jit(solution)/shard_map/attend_backward/pallas_call | solution.py:46
  105.9 6.5 %all-to-all-start.2 = ((bf16[8,192,256]{2,1,0:T(8,128)(2,1)}), bf16[8,192,256]{2,1,0:T(8,128)(2,1)S(1)}, u32[]{:S(2)}, u32[]{:S(2)}) async-start(bf16[8,192,256]{2,1,0:T(8,128)(2,1)} %attend_backward.1.refs_18_), calls=%async_computation.2 | async-start | bytes 1572864 | tf_op jit(solution)/shard_map/all_to_all | solution.py:355
  112.3 7.6 %result.1 = (bf16[256,1024]{1,0:T(8,128)(2,1)}, bf16[16,224,128]{2,1,0:T(8,128)(2,1)}, bf16[16,224,128]{2,1,0:T(8,128)(2,1)}) custom-call(s32[2]{0:T(128)} %pad_add_fusion.place_ref.refs_0_, bf16[128,1024]{1,0:T(8,128)(2,1)} %normalize.2.refs_5_.refs_1_, bf16[128,1024]{1,0:T(8,128)(2,1)} %normalize.3.refs_6_.refs_2_, bf16[128,1024]{1,0:T(8,128)(2,1)} %copy-done.6, ...), custom_call_target="tpu_custom_call" | custom-call | flops 2147483648 | bytes 10485760 | tf_op jit(solution)/shard_map/result/pallas_call | solution.py:46
  120.1 2.7 %collective-permute-done.16 = bf16[16,224,128]{2,1,0:T(8,128)(2,1)S(1)} collective-permute-done((bf16[16,224,128]{2,1,0:T(8,128)(2,1)}, bf16[16,224,128]{2,1,0:T(8,128)(2,1)S(1)}, u32[]{:S(2)}, u32[]{:S(2)}) %collective-permute-start.16) | collective-permute-done | bytes 917536 | tf_op jit(solution)/shard_map/ppermute | solution.py:464
  124.2 4.3 %all-to-all-done.2.refs_0_ = bf16[8,192,256]{2,1,0:T(8,128)(2,1)S(1)} async-done(((bf16[8,192,256]{2,1,0:T(8,128)(2,1)}), bf16[8,192,256]{2,1,0:T(8,128)(2,1)S(1)}, u32[]{:S(2)}, u32[]{:S(2)}) %all-to-all-start.2) | async-done | bytes 786464 | tf_op jit(solution)/shard_map/all_to_all | solution.py:355
  128.4 17.4 %all_to_all.25.shares_ref = bf16[16,224,128]{2,1,0:T(8,128)(2,1)} all-to-all(bf16[16,224,128]{2,1,0:T(8,128)(2,1)S(1)} %add_convert_fusion), channel_id=1, replica_groups=mesh['x'=4,'y'=4,'c'=2,'z'=8] {'x','y'}, dimensions={0} | all-to-all | bytes 1835008 | tf_op jit(solution)/shard_map/all_to_all | solution.py:355
  147.9 6.7 %all-to-all-start.4 = ((bf16[8,224,128]{2,1,0:T(8,128)(2,1)}), bf16[8,224,128]{2,1,0:T(8,128)(2,1)S(1)}, u32[]{:S(2)}, u32[]{:S(2)}) async-start(bf16[8,224,128]{2,1,0:T(8,128)(2,1)} %share_sum.1), calls=%async_computation.4 | async-start | bytes 917504 | tf_op jit(solution)/shard_map/all_to_all | solution.py:355
  159.0 5.8 %input_grad.1 = bf16[256,1024]{1,0:T(8,128)(2,1)} custom-call(bf16[8,192,256]{2,1,0:T(8,128)(2,1)} %copy-done, bf16[1024,1536]{1,0:T(8,128)(2,1)} %refs_1_.3, bf16[256,1024]{1,0:T(8,128)(2,1)} %get-tuple-element.75.refs_2_, bf16[1024,1024]{1,0:T(8,128)(2,1)} %refs_3_.1, bf16[256,1024]{1,0:T(8,128)(2,1)} %refs_4_.1, bf16[256,1024]{1,0:T(8,128)(2,1)} %refs_5_.1, ...), custom_call_target="tpu_custom_call" | custom-call | flops 805306368 | bytes 8388608 | tf_op jit(solution)/shard_map/input_grad/pallas_call | solution.py:46
  164.9 4.8 %all-to-all-done.4.every_ref = bf16[8,224,128]{2,1,0:T(8,128)(2,1)S(1)} async-done(((bf16[8,224,128]{2,1,0:T(8,128)(2,1)}), bf16[8,224,128]{2,1,0:T(8,128)(2,1)S(1)}, u32[]{:S(2)}, u32[]{:S(2)}) %all-to-all-start.4) | async-done | bytes 458784 | tf_op jit(solution)/shard_map/all_to_all | solution.py:355
  (64 shorter events, 25.0 us)
Async XLA Ops:
  2.4 15.9 %collective-permute-start = (bf16[128,1024]{1,0:T(8,128)(2,1)}, bf16[128,1024]{1,0:T(8,128)(2,1)S(1)}, u32[]{:S(2)}, u32[]{:S(2)}) collective-permute-start(bf16[128,1024]{1,0:T(8,128)(2,1)} %normalize.2.refs_5_.refs_1_), channel_id=1, source_target_pairs={{0,1},{1,2},{2,3},{3,4},{4,5},{5,6},{6,7},{7,0},{8,9},{9,10},{10,1... | collective-permute-start | bytes 786440 | tf_op jit(solution)/shard_map/ppermute | solution.py:359
  4.4 14.0 %collective-permute-start.1 = (bf16[128,1024]{1,0:T(8,128)(2,1)}, bf16[128,1024]{1,0:T(8,128)(2,1)S(1)}, u32[]{:S(2)}, u32[]{:S(2)}) collective-permute-start(bf16[128,1024]{1,0:T(8,128)(2,1)} %normalize.2.refs_5_.refs_1_), channel_id=1, source_target_pairs={{0,7},{1,0},{2,1},{3,2},{4,3},{5,4},{6,5},{7,6},{8,15},{9,8},{10,9... | collective-permute-start | bytes 786440 | tf_op jit(solution)/shard_map/ppermute | solution.py:359
  10.1 9.7 %collective-permute-start.8 = (bf16[128,1024]{1,0:T(8,128)(2,1)}, bf16[128,1024]{1,0:T(8,128)(2,1)S(1)}, u32[]{:S(2)}, u32[]{:S(2)}) collective-permute-start(bf16[128,1024]{1,0:T(8,128)(2,1)} %normalize.3.refs_6_.refs_2_), channel_id=1, source_target_pairs={{0,7},{1,0},{2,1},{3,2},{4,3},{5,4},{6,5},{7,6},{8,15},{9,8},{10,9... | collective-permute-start | bytes 786440 | tf_op jit(solution)/shard_map/ppermute | solution.py:359
  18.4 27.5 %copy-start.6 = (bf16[128,1024]{1,0:T(8,128)(2,1)}, bf16[128,1024]{1,0:T(8,128)(2,1)S(1)}, u32[]{:S(2)}) copy-start(bf16[128,1024]{1,0:T(8,128)(2,1)S(1)} %collective-permute-done.refs_3_) | copy-start | bytes 786436
  18.4 27.5 %copy-start.7 = (bf16[128,1024]{1,0:T(8,128)(2,1)}, bf16[128,1024]{1,0:T(8,128)(2,1)S(1)}, u32[]{:S(2)}) copy-start(bf16[128,1024]{1,0:T(8,128)(2,1)S(1)} %collective-permute-done.1.refs_7_.refs_15_) | copy-start | bytes 786436
  18.4 9.4 %collective-permute-start.3 = (bf16[128,1024]{1,0:T(8,128)(2,1)S(1)}, bf16[128,1024]{1,0:T(8,128)(2,1)S(1)}, u32[]{:S(2)}, u32[]{:S(2)}) collective-permute-start(bf16[128,1024]{1,0:T(8,128)(2,1)S(1)} %collective-permute-done.refs_3_), channel_id=1, source_target_pairs={{0,1},{1,2},{2,3},{3,4},{4,5},{5,6},{6,7},{7,0},{8,9},{9,10},{10,1... | collective-permute-start | bytes 786440 | tf_op jit(solution)/shard_map/ppermute | solution.py:359
  19.8 8.3 %collective-permute-start.9 = (bf16[128,1024]{1,0:T(8,128)(2,1)S(1)}, bf16[128,1024]{1,0:T(8,128)(2,1)S(1)}, u32[]{:S(2)}, u32[]{:S(2)}) collective-permute-start(bf16[128,1024]{1,0:T(8,128)(2,1)S(1)} %collective-permute-done.8.refs_8_.refs_16_), channel_id=1, source_target_pairs={{0,7},{1,0},{2,1},{3,2},{4,3},{5,4},{6,5},{7,6},{8,15},{9,8},{10,9... | collective-permute-start | bytes 786440 | tf_op jit(solution)/shard_map/ppermute | solution.py:359
  23.4 10.5 %collective-permute-start.2 = (bf16[128,1024]{1,0:T(8,128)(2,1)S(1)}, bf16[128,1024]{1,0:T(8,128)(2,1)S(1)}, u32[]{:S(2)}, u32[]{:S(2)}) collective-permute-start(bf16[128,1024]{1,0:T(8,128)(2,1)S(1)} %copy-done.3), channel_id=1, source_target_pairs={{0,1},{1,2},{2,3},{3,4},{4,5},{5,6},{6,7},{7,0},{8,9},{9,10},{10,1... | collective-permute-start | bytes 786440 | tf_op jit(solution)/shard_map/ppermute | solution.py:359
  27.8 11.8 %collective-permute-start.5 = (bf16[128,1024]{1,0:T(8,128)(2,1)S(1)}, bf16[128,1024]{1,0:T(8,128)(2,1)}, u32[]{:S(2)}, u32[]{:S(2)}) collective-permute-start(bf16[128,1024]{1,0:T(8,128)(2,1)S(1)} %collective-permute-done.3.refs_5_), channel_id=1, source_target_pairs={{0,1},{1,2},{2,3},{3,4},{4,5},{5,6},{6,7},{7,0},{8,9},{9,10},{10,1... | collective-permute-start | bytes 786440 | tf_op jit(solution)/shard_map/ppermute | solution.py:359
  28.1 11.5 %collective-permute-start.10 = (bf16[128,1024]{1,0:T(8,128)(2,1)S(1)}, bf16[128,1024]{1,0:T(8,128)(2,1)}, u32[]{:S(2)}, u32[]{:S(2)}) collective-permute-start(bf16[128,1024]{1,0:T(8,128)(2,1)S(1)} %collective-permute-done.9.refs_14_), channel_id=1, source_target_pairs={{0,7},{1,0},{2,1},{3,2},{4,3},{5,4},{6,5},{7,6},{8,15},{9,8},{10,9... | collective-permute-start | bytes 786440 | tf_op jit(solution)/shard_map/ppermute | solution.py:359
  31.8 11.0 %collective-permute-start.12 = (bf16[128,1024]{1,0:T(8,128)(2,1)S(1)}, bf16[128,1024]{1,0:T(8,128)(2,1)}, u32[]{:S(2)}, u32[]{:S(2)}) collective-permute-start(bf16[128,1024]{1,0:T(8,128)(2,1)S(1)} %collective-permute-done.1.refs_7_.refs_15_), channel_id=1, source_target_pairs={{0,7},{1,0},{2,1},{3,2},{4,3},{5,4},{6,5},{7,6},{8,15},{9,8},{10,9... | collective-permute-start | bytes 786440 | tf_op jit(solution)/shard_map/ppermute | solution.py:359
  33.9 12.0 %collective-permute-start.4 = (bf16[128,1024]{1,0:T(8,128)(2,1)S(1)}, bf16[128,1024]{1,0:T(8,128)(2,1)S(1)}, u32[]{:S(2)}, u32[]{:S(2)}) collective-permute-start(bf16[128,1024]{1,0:T(8,128)(2,1)S(1)} %collective-permute-done.2.refs_4_), channel_id=1, source_target_pairs={{0,1},{1,2},{2,3},{3,4},{4,5},{5,6},{6,7},{7,0},{8,9},{9,10},{10,1... | collective-permute-start | bytes 786440 | tf_op jit(solution)/shard_map/ppermute | solution.py:359
  39.6 13.5 %collective-permute-start.7 = (bf16[128,1024]{1,0:T(8,128)(2,1)}, bf16[128,1024]{1,0:T(8,128)(2,1)}, u32[]{:S(2)}, u32[]{:S(2)}) collective-permute-start(bf16[128,1024]{1,0:T(8,128)(2,1)} %collective-permute-done.5.refs_7_), channel_id=1, source_target_pairs={{0,1},{1,2},{2,3},{3,4},{4,5},{5,6},{6,7},{7,0},{8,9},{9,10},{10,1... | collective-permute-start | bytes 786440 | tf_op jit(solution)/shard_map/ppermute | solution.py:359
  39.6 13.5 %collective-permute-start.11 = (bf16[128,1024]{1,0:T(8,128)(2,1)}, bf16[128,1024]{1,0:T(8,128)(2,1)}, u32[]{:S(2)}, u32[]{:S(2)}) collective-permute-start(bf16[128,1024]{1,0:T(8,128)(2,1)} %collective-permute-done.10.refs_12_), channel_id=1, source_target_pairs={{0,7},{1,0},{2,1},{3,2},{4,3},{5,4},{6,5},{7,6},{8,15},{9,8},{10,9... | collective-permute-start | bytes 786440 | tf_op jit(solution)/shard_map/ppermute | solution.py:359
  42.8 13.5 %collective-permute-start.13 = (bf16[128,1024]{1,0:T(8,128)(2,1)}, bf16[128,1024]{1,0:T(8,128)(2,1)}, u32[]{:S(2)}, u32[]{:S(2)}) collective-permute-start(bf16[128,1024]{1,0:T(8,128)(2,1)} %collective-permute-done.12.refs_13_), channel_id=1, source_target_pairs={{0,7},{1,0},{2,1},{3,2},{4,3},{5,4},{6,5},{7,6},{8,15},{9,8},{10,9... | collective-permute-start | bytes 786440 | tf_op jit(solution)/shard_map/ppermute | solution.py:359
  45.8 17.9 %collective-permute-start.6 = (bf16[128,1024]{1,0:T(8,128)(2,1)S(1)}, bf16[128,1024]{1,0:T(8,128)(2,1)}, u32[]{:S(2)}, u32[]{:S(2)}) collective-permute-start(bf16[128,1024]{1,0:T(8,128)(2,1)S(1)} %collective-permute-done.4.refs_6_), channel_id=1, source_target_pairs={{0,1},{1,2},{2,3},{3,4},{4,5},{5,6},{6,7},{7,0},{8,9},{9,10},{10,1... | collective-permute-start | bytes 786440 | tf_op jit(solution)/shard_map/ppermute | solution.py:359
  53.1 24.9 %collective-permute-start.14 = (bf16[256,1024]{1,0:T(8,128)(2,1)}, bf16[256,1024]{1,0:T(8,128)(2,1)S(1)}, u32[]{:S(2)}, u32[]{:S(2)}) collective-permute-start(bf16[256,1024]{1,0:T(8,128)(2,1)} %get-tuple-element.59), channel_id=1, source_target_pairs={{0,7},{1,0},{2,1},{3,2},{4,3},{5,4},{6,5},{7,6},{8,15},{9,8},{10,9... | collective-permute-start | bytes 1572872 | tf_op jit(solution)/shard_map/ppermute | solution.py:359
  56.3 21.7 %collective-permute-start.15 = (bf16[256,1024]{1,0:T(8,128)(2,1)}, bf16[256,1024]{1,0:T(8,128)(2,1)S(1)}, u32[]{:S(2)}, u32[]{:S(2)}) collective-permute-start(bf16[256,1024]{1,0:T(8,128)(2,1)} %get-tuple-element.60), channel_id=1, source_target_pairs={{0,1},{1,2},{2,3},{3,4},{4,5},{5,6},{6,7},{7,0},{8,9},{9,10},{10,1... | collective-permute-start | bytes 1572872 | tf_op jit(solution)/shard_map/ppermute | solution.py:359
  56.3 25.5 %all-to-all-start = ((bf16[8,64,256]{2,1,0:T(8,128)(2,1)}), bf16[8,64,256]{2,1,0:T(8,128)(2,1)S(1)}, u32[]{:S(2)}, u32[]{:S(2)}) async-start(bf16[8,64,256]{2,1,0:T(8,128)(2,1)} %d_out.1), calls=%async_computation | async-start | bytes 524288 | tf_op jit(solution)/shard_map/all_to_all | solution.py:355
  82.5 23.3 %all-to-all-start.1 = ((bf16[8,192,256]{2,1,0:T(8,128)(2,1)}), bf16[8,192,256]{2,1,0:T(8,128)(2,1)S(1)}, u32[]{:S(2)}, u32[]{:S(2)}) async-start(bf16[8,192,256]{2,1,0:T(8,128)(2,1)} %get-tuple-element.65), calls=%async_computation.1 | async-start | bytes 1572864 | tf_op jit(solution)/shard_map/all_to_all | solution.py:355
  105.9 22.6 %all-to-all-start.2 = ((bf16[8,192,256]{2,1,0:T(8,128)(2,1)}), bf16[8,192,256]{2,1,0:T(8,128)(2,1)S(1)}, u32[]{:S(2)}, u32[]{:S(2)}) async-start(bf16[8,192,256]{2,1,0:T(8,128)(2,1)} %attend_backward.1.refs_18_), calls=%async_computation.2 | async-start | bytes 1572864 | tf_op jit(solution)/shard_map/all_to_all | solution.py:355
  120.0 2.8 %collective-permute-start.16 = (bf16[16,224,128]{2,1,0:T(8,128)(2,1)}, bf16[16,224,128]{2,1,0:T(8,128)(2,1)S(1)}, u32[]{:S(2)}, u32[]{:S(2)}) collective-permute-start(bf16[16,224,128]{2,1,0:T(8,128)(2,1)} %get-tuple-element.71), channel_id=1, source_target_pairs={{0,8},{8,0},{1,9},{9,1},{2,10},{10,2},{3,11},{11,3},{4,12},{12,4},... | collective-permute-start | bytes 2752520 | tf_op jit(solution)/shard_map/ppermute | solution.py:464
  128.4 29.1 %copy-start = (bf16[8,192,256]{2,1,0:T(8,128)(2,1)}, bf16[8,192,256]{2,1,0:T(8,128)(2,1)S(1)}, u32[]{:S(2)}) copy-start(bf16[8,192,256]{2,1,0:T(8,128)(2,1)S(1)} %all-to-all-done.2.refs_0_) | copy-start | bytes 2359300
  147.9 21.7 %all-to-all-start.4 = ((bf16[8,224,128]{2,1,0:T(8,128)(2,1)}), bf16[8,224,128]{2,1,0:T(8,128)(2,1)S(1)}, u32[]{:S(2)}, u32[]{:S(2)}) async-start(bf16[8,224,128]{2,1,0:T(8,128)(2,1)} %share_sum.1), calls=%async_computation.4 | async-start | bytes 917504 | tf_op jit(solution)/shard_map/all_to_all | solution.py:355
  (11 other events, 115.8 us)

commit v6 on v5

--- a/solution.py
+++ b/solution.py
@@ -49,7 +49,7 @@
         in_specs=specs,
         out_specs=tuple(pl.BlockSpec(memory_space=pltpu.VMEM) for _ in out_shape),
         scratch_shapes=list(scratch),
-        compiler_params=pltpu.CompilerParams(vmem_limit_bytes=62 * 1024 * 1024),
+        compiler_params=pltpu.CompilerParams(vmem_limit_bytes=63 * 1024 * 1024),
         cost_estimate=pl.CostEstimate(flops=flops, bytes_accessed=moved, transcendentals=exps),
         name=name,
     )(*scalars, *far, *arrays)
@@ -416,8 +416,8 @@
     d_heads = exchange(after(d_out, a_up[3], a_down[3]), "z")
     b_up.append(up(b_up[2]))
     b_down.append(down(b_down[2]))
+    a_up[3], b_down[3], to_low, to_high = lax.optimization_barrier((a_up[3], b_down[3], to_low, to_high))
     c4 = [up(a_up[3]), down(b_down[3])]
-    *c4, to_low, to_high = lax.optimization_barrier((*c4, to_low, to_high))
     above, below = down(to_low), up(to_high)
     pairs = list(zip(a_up, b_up)) + [c4] + list(zip(a_down, b_down))[:0:-1]
     chunks = tuple(half for pair in pairs for half in pair)

time: 173 us -> 168 us (0.971)
  waiting for transfers between devices: 26.3 us -> 21.3 us
    ppermute x16, waiting for transfers between devices: 13.8 us -> 8.02 us  [shift(): lax.ppermute(array, 'z', [(i, (i + distance) % N_SEQ) for i in range(N_SE...]
    all_to_all x4, starting transfers between devices: 27.8 us -> 25.8 us  [exchange(): return lax.all_to_all(array, axis, split_axis=0, concat_axis=0, tiled=True)]
    ppermute x16, starting transfers between devices: 24.8 us -> 26.6 us  [shift(): lax.ppermute(array, 'z', [(i, (i + distance) % N_SEQ) for i in range(N_SE...]
  transfers between devices with their start and end apart: 21 -> 21, of which waited for: 9 -> 8; matrix products, arithmetic and copies ran while one was open for 4% -> 4% of each run, Pallas kernels for 35% -> 36%
where the time goes in v6:
time: 168 us; the launch traced here: 167 us
  Pallas kernels  66 us (39%)
  starting transfers between devices  52.5 us (31%)
  waiting for transfers between devices  21.3 us (13%)
  blocking collectives  17.4 us (10%)
  local copies, waits for them, and re-layouts  6.65 us (4%)
  other arithmetic  2 us (1%)
    pallas_call x9, Pallas kernels, call(): pl.pallas_call(kernel, out_shape=tuple((jax.ShapeDtypeStruct(s, t) for s,...  59.4 us
    ppermute x16, starting transfers between devices, shift(): lax.ppermute(array, 'z', [(i, (i + distance) % N_SEQ) for i in range(N_SE...  26.6 us
    all_to_all x4, starting transfers between devices, exchange(): return lax.all_to_all(array, axis, split_axis=0, concat_axis=0, tiled=True)  25.8 us
    all_to_all x1, blocking collectives, exchange(): return lax.all_to_all(array, axis, split_axis=0, concat_axis=0, tiled=True)  17.4 us
    all_to_all x4, waiting for transfers between devices, exchange(): return lax.all_to_all(array, axis, split_axis=0, concat_axis=0, tiled=True)  10.6 us
    ppermute x16, waiting for transfers between devices, shift(): lax.ppermute(array, 'z', [(i, (i + distance) % N_SEQ) for i in range(N_SE...  8.02 us
    pallas_call x2, Pallas kernels, normalize_half(): pl.pallas_call(normalize_kernel, grid=(1,), in_specs=[pl.BlockSpec((BLOCK...  3.62 us
  transfers between devices with their start and end apart: 21, of which 8 were waited for; matrix products, arithmetic and copies ran while one was open for 4% of the time, Pallas kernels for 36%

profile of v6, /device:TPU:6, one launch (start us, length us, event | category | flops | bytes accessed | tf_op | source)
XLA Modules:
  0.0 166.6 jit_solution(17537506831023477022)
XLA Ops:
  4.4 3.9 %collective-permute-start.1 = (bf16[128,1024]{1,0:T(8,128)(2,1)}, bf16[128,1024]{1,0:T(8,128)(2,1)S(1)}, u32[]{:S(2)}, u32[]{:S(2)}) collective-permute-start(bf16[128,1024]{1,0:T(8,128)(2,1)} %normalize.2.refs_5_.refs_1_), channel_id=1, source_target_pairs={{0,7},{1,0},{2,1},{3,2},{4,3},{5,4},{6,5},{7,6},{8,15},{9,8},{10,9... | collective-permute-start | bytes 786440 | tf_op jit(solution)/shard_map/ppermute | solution.py:359
  10.1 2.0 %collective-permute-start.6 = (bf16[128,1024]{1,0:T(8,128)(2,1)}, bf16[128,1024]{1,0:T(8,128)(2,1)S(1)}, u32[]{:S(2)}, u32[]{:S(2)}) collective-permute-start(bf16[128,1024]{1,0:T(8,128)(2,1)} %normalize.3.refs_6_.refs_2_), channel_id=1, source_target_pairs={{0,7},{1,0},{2,1},{3,2},{4,3},{5,4},{6,5},{7,6},{8,15},{9,8},{10,9... | collective-permute-start | bytes 786440 | tf_op jit(solution)/shard_map/ppermute | solution.py:359
  12.7 2.9 %pick_head.1.refs_17_ = bf16[1024,256]{1,0:T(8,128)(2,1)} custom-call(s32[2]{0:T(128)} %pad_add_fusion.place_ref.refs_0_, bf16[1024,1536]{1,0:T(8,128)(2,1)} %refs_1_.3, bf16[1024,1536]{1,0:T(8,128)(2,1)} %refs_1_.3, bf16[1024,1536]{1,0:T(8,128)(2,1)} %refs_1_.3), custom_call_target="tpu_custom_call" | custom-call | bytes 4194304 | tf_op jit(solution)/shard_map/pick_head/pallas_call | solution.py:108
  15.7 2.6 %d_out.1 = bf16[8,64,256]{2,1,0:T(8,128)(2,1)} custom-call(bf16[256,1024]{1,0:T(8,128)(2,1)} %refs_5_.1, bf16[512,1024]{1,0:T(8,128)(2,1)} %refs_19_.1), custom_call_target="tpu_custom_call" | custom-call | flops 268435456 | bytes 2097152 | tf_op jit(solution)/shard_map/d_out/pallas_call | solution.py:46
  19.8 3.6 %collective-permute-start.7 = (bf16[128,1024]{1,0:T(8,128)(2,1)S(1)}, bf16[128,1024]{1,0:T(8,128)(2,1)}, u32[]{:S(2)}, u32[]{:S(2)}) collective-permute-start(bf16[128,1024]{1,0:T(8,128)(2,1)S(1)} %collective-permute-done.6.refs_8_.refs_16_), channel_id=1, source_target_pairs={{0,7},{1,0},{2,1},{3,2},{4,3},{5,4},{6,5},{7,6},{8,15},{9,8},{10,9... | collective-permute-start | bytes 786440 | tf_op jit(solution)/shard_map/ppermute | solution.py:359
  27.4 2.7 %collective-permute-done.7.refs_14_ = bf16[128,1024]{1,0:T(8,128)(2,1)} collective-permute-done((bf16[128,1024]{1,0:T(8,128)(2,1)S(1)}, bf16[128,1024]{1,0:T(8,128)(2,1)}, u32[]{:S(2)}, u32[]{:S(2)}) %collective-permute-start.7) | collective-permute-done | bytes 262176 | tf_op jit(solution)/shard_map/ppermute | solution.py:359
  30.2 3.8 %collective-permute-start.8 = (bf16[128,1024]{1,0:T(8,128)(2,1)}, bf16[128,1024]{1,0:T(8,128)(2,1)}, u32[]{:S(2)}, u32[]{:S(2)}) collective-permute-start(bf16[128,1024]{1,0:T(8,128)(2,1)} %collective-permute-done.7.refs_14_), channel_id=1, source_target_pairs={{0,7},{1,0},{2,1},{3,2},{4,3},{5,4},{6,5},{7,6},{8,15},{9,8},{10,9... | collective-permute-start | bytes 786440 | tf_op jit(solution)/shard_map/ppermute | solution.py:359
  35.8 3.8 %collective-permute-start.13 = (bf16[128,1024]{1,0:T(8,128)(2,1)}, bf16[128,1024]{1,0:T(8,128)(2,1)}, u32[]{:S(2)}, u32[]{:S(2)}) collective-permute-start(bf16[128,1024]{1,0:T(8,128)(2,1)} %collective-permute-done.9.refs_13_), channel_id=1, source_target_pairs={{0,7},{1,0},{2,1},{3,2},{4,3},{5,4},{6,5},{7,6},{8,15},{9,8},{10,9... | collective-permute-start | bytes 786440 | tf_op jit(solution)/shard_map/ppermute | solution.py:359
  39.6 7.1 %messages.1 = (f32[256,1024]{1,0:T(8,128)}, bf16[256,1024]{1,0:T(8,128)(2,1)}, f32[256,1024]{1,0:T(8,128)}, bf16[256,1024]{1,0:T(8,128)(2,1)}) custom-call(s32[2]{0:T(128)} %pad_add_fusion.place_ref.refs_0_, s32[2,4]{1,0:T(2,128)} %refs_1_.2, s32[2]{0:T(128)} %refs_2_.1, bf16[128,1024]{1,0:T(8,128)(2,1)} %copy-done.3, ...), custom_call_target="tpu_custom_call" | custom-call | flops 2147483648 | bytes 8388608 | tf_op jit(solution)/shard_map/messages/pallas_call | solution.py:46
  46.8 3.3 %collective-permute-start.12 = (bf16[128,1024]{1,0:T(8,128)(2,1)}, bf16[128,1024]{1,0:T(8,128)(2,1)}, u32[]{:S(2)}, u32[]{:S(2)}) collective-permute-start(bf16[128,1024]{1,0:T(8,128)(2,1)} %collective-permute-done.8.refs_12_), channel_id=1, source_target_pairs={{0,7},{1,0},{2,1},{3,2},{4,3},{5,4},{6,5},{7,6},{8,15},{9,8},{10,9... | collective-permute-start | bytes 786440 | tf_op jit(solution)/shard_map/ppermute | solution.py:359
  52.1 6.1 %all-to-all-start = ((bf16[8,64,256]{2,1,0:T(8,128)(2,1)}), bf16[8,64,256]{2,1,0:T(8,128)(2,1)}, u32[]{:S(2)}, u32[]{:S(2)}) async-start(bf16[8,64,256]{2,1,0:T(8,128)(2,1)} %d_out.1), calls=%async_computation | async-start | bytes 524288 | tf_op jit(solution)/shard_map/all_to_all | solution.py:355
  58.8 14.1 %attend_forward.1 = (bf16[8,64,256]{2,1,0:T(8,128)(2,1)}, bf16[8,256,128]{2,1,0:T(8,128)(2,1)}, bf16[8,64,256]{2,1,0:T(8,128)(2,1)}, bf16[8,64,256]{2,1,0:T(8,12...) custom-call(s32[2]{0:T(128)} %pad_add_fusion.place_ref.refs_0_, bf16[128,1024]{1,0:T(8,128)(2,1)} %normalize.2.refs_5_.refs_1_, ...), custom_call_target="tpu_custom_call" | custom-call | flops 3221225472 | bytes 8388608 | tf_op jit(solution)/shard_map/attend_forward/pallas_call | solution.py:46
  73.8 2.9 %merge.1 = (bf16[8,192,256]{2,1,0:T(8,128)(2,1)}, bf16[256,1024]{1,0:T(8,128)(2,1)}) custom-call(bf16[8,64,256]{2,1,0:T(8,128)(2,1)} %get-tuple-element.52.heads_ref.refs_1_, f32[256,1024]{1,0:T(8,128)} %get-tuple-element.58.mid_ref, bf16[256,1024]{1,0:T(8,128)(2,1)} %copy-done.2, bf16[256,1024]{1,0:T(8,128)(2,1)} %collective-permute-done.15.below_ref), custom_call_target="tpu_custom_call" | custom-call | bytes 4194304 | tf_op jit(solution)/shard_map/merge/pallas_call | solution.py:46
  76.7 7.2 %all-to-all-start.1 = ((bf16[8,192,256]{2,1,0:T(8,128)(2,1)}), bf16[8,192,256]{2,1,0:T(8,128)(2,1)S(1)}, u32[]{:S(2)}, u32[]{:S(2)}) async-start(bf16[8,192,256]{2,1,0:T(8,128)(2,1)} %get-tuple-element.65), calls=%async_computation.1 | async-start | bytes 1572864 | tf_op jit(solution)/shard_map/all_to_all | solution.py:355
  83.9 15.4 %attend_backward.1.refs_18_ = bf16[8,192,256]{2,1,0:T(8,128)(2,1)} custom-call(s32[2]{0:T(128)} %pad_add_fusion.place_ref.refs_0_, bf16[8,64,256]{2,1,0:T(8,128)(2,1)} %get-tuple-element.52.heads_ref.refs_1_, bf16[8,256,128]{2,1,0:T(8,128)(2,1)} %get-tuple-element.53.refs_2_, bf16[8,64,256]{2,1,0:T(8,128)(2,1)} %get-tuple-element.54.refs_3_, ...), custom_call_target="tpu_custom_call" | custom-call | flops 6442450944 | bytes 4194304 | tf_op jit(solution)/shard_map/attend_backward/pallas_call | solution.py:46
  101.4 5.9 %all-to-all-start.2 = ((bf16[8,192,256]{2,1,0:T(8,128)(2,1)}), bf16[8,192,256]{2,1,0:T(8,128)(2,1)S(1)}, u32[]{:S(2)}, u32[]{:S(2)}) async-start(bf16[8,192,256]{2,1,0:T(8,128)(2,1)} %attend_backward.1.refs_18_), calls=%async_computation.2 | async-start | bytes 1572864 | tf_op jit(solution)/shard_map/all_to_all | solution.py:355
  107.3 7.6 %result.1 = (bf16[256,1024]{1,0:T(8,128)(2,1)}, bf16[16,224,128]{2,1,0:T(8,128)(2,1)}, bf16[16,224,128]{2,1,0:T(8,128)(2,1)}) custom-call(s32[2]{0:T(128)} %pad_add_fusion.place_ref.refs_0_, bf16[128,1024]{1,0:T(8,128)(2,1)} %normalize.2.refs_5_.refs_1_, bf16[128,1024]{1,0:T(8,128)(2,1)} %normalize.3.refs_6_.refs_2_, bf16[128,1024]{1,0:T(8,128)(2,1)} %copy-done.3, ...), custom_call_target="tpu_custom_call" | custom-call | flops 2147483648 | bytes 10485760 | tf_op jit(solution)/shard_map/result/pallas_call | solution.py:46
  115.0 2.7 %collective-permute-done.16 = bf16[16,224,128]{2,1,0:T(8,128)(2,1)S(1)} collective-permute-done((bf16[16,224,128]{2,1,0:T(8,128)(2,1)}, bf16[16,224,128]{2,1,0:T(8,128)(2,1)S(1)}, u32[]{:S(2)}, u32[]{:S(2)}) %collective-permute-start.16) | collective-permute-done | bytes 917536 | tf_op jit(solution)/shard_map/ppermute | solution.py:464
  119.1 4.4 %all-to-all-done.2.refs_0_ = bf16[8,192,256]{2,1,0:T(8,128)(2,1)S(1)} async-done(((bf16[8,192,256]{2,1,0:T(8,128)(2,1)}), bf16[8,192,256]{2,1,0:T(8,128)(2,1)S(1)}, u32[]{:S(2)}, u32[]{:S(2)}) %all-to-all-start.2) | async-done | bytes 786464 | tf_op jit(solution)/shard_map/all_to_all | solution.py:355
  123.5 17.4 %all_to_all.25.shares_ref = bf16[16,224,128]{2,1,0:T(8,128)(2,1)} all-to-all(bf16[16,224,128]{2,1,0:T(8,128)(2,1)S(1)} %add_convert_fusion), channel_id=1, replica_groups=mesh['x'=4,'y'=4,'c'=2,'z'=8] {'x','y'}, dimensions={0} | all-to-all | bytes 1835008 | tf_op jit(solution)/shard_map/all_to_all | solution.py:355
  140.9 2.1 %share_sum.1 = bf16[8,224,128]{2,1,0:T(8,128)(2,1)} custom-call(bf16[16,224,128]{2,1,0:T(8,128)(2,1)} %all_to_all.25.shares_ref), custom_call_target="tpu_custom_call" | custom-call | bytes 2097152 | tf_op jit(solution)/shard_map/share_sum/pallas_call | solution.py:46
  143.0 6.7 %all-to-all-start.4 = ((bf16[8,224,128]{2,1,0:T(8,128)(2,1)}), bf16[8,224,128]{2,1,0:T(8,128)(2,1)}, u32[]{:S(2)}, u32[]{:S(2)}) async-start(bf16[8,224,128]{2,1,0:T(8,128)(2,1)} %share_sum.1), calls=%async_computation.4 | async-start | bytes 917504 | tf_op jit(solution)/shard_map/all_to_all | solution.py:355
  153.9 5.8 %input_grad.1 = bf16[256,1024]{1,0:T(8,128)(2,1)} custom-call(bf16[8,192,256]{2,1,0:T(8,128)(2,1)} %copy-done, bf16[1024,1536]{1,0:T(8,128)(2,1)} %refs_1_.3, bf16[256,1024]{1,0:T(8,128)(2,1)} %get-tuple-element.75.refs_2_, bf16[1024,1024]{1,0:T(8,128)(2,1)} %refs_3_.1, bf16[256,1024]{1,0:T(8,128)(2,1)} %refs_4_.1, bf16[256,1024]{1,0:T(8,128)(2,1)} %refs_5_.1, ...), custom_call_target="tpu_custom_call" | custom-call | flops 805306368 | bytes 8388608 | tf_op jit(solution)/shard_map/input_grad/pallas_call | solution.py:46
  159.8 4.9 %all-to-all-done.4.every_ref = bf16[8,224,128]{2,1,0:T(8,128)(2,1)} async-done(((bf16[8,224,128]{2,1,0:T(8,128)(2,1)}), bf16[8,224,128]{2,1,0:T(8,128)(2,1)}, u32[]{:S(2)}, u32[]{:S(2)}) %all-to-all-start.4) | async-done | bytes 458784 | tf_op jit(solution)/shard_map/all_to_all | solution.py:355
  (50 shorter events, 27.1 us)
Async XLA Ops:
  2.4 15.8 %collective-permute-start = (bf16[128,1024]{1,0:T(8,128)(2,1)}, bf16[128,1024]{1,0:T(8,128)(2,1)S(1)}, u32[]{:S(2)}, u32[]{:S(2)}) collective-permute-start(bf16[128,1024]{1,0:T(8,128)(2,1)} %normalize.2.refs_5_.refs_1_), channel_id=1, source_target_pairs={{0,1},{1,2},{2,3},{3,4},{4,5},{5,6},{6,7},{7,0},{8,9},{9,10},{10,1... | collective-permute-start | bytes 786440 | tf_op jit(solution)/shard_map/ppermute | solution.py:359
  4.4 13.9 %collective-permute-start.1 = (bf16[128,1024]{1,0:T(8,128)(2,1)}, bf16[128,1024]{1,0:T(8,128)(2,1)S(1)}, u32[]{:S(2)}, u32[]{:S(2)}) collective-permute-start(bf16[128,1024]{1,0:T(8,128)(2,1)} %normalize.2.refs_5_.refs_1_), channel_id=1, source_target_pairs={{0,7},{1,0},{2,1},{3,2},{4,3},{5,4},{6,5},{7,6},{8,15},{9,8},{10,9... | collective-permute-start | bytes 786440 | tf_op jit(solution)/shard_map/ppermute | solution.py:359
  10.1 9.7 %collective-permute-start.6 = (bf16[128,1024]{1,0:T(8,128)(2,1)}, bf16[128,1024]{1,0:T(8,128)(2,1)S(1)}, u32[]{:S(2)}, u32[]{:S(2)}) collective-permute-start(bf16[128,1024]{1,0:T(8,128)(2,1)} %normalize.3.refs_6_.refs_2_), channel_id=1, source_target_pairs={{0,7},{1,0},{2,1},{3,2},{4,3},{5,4},{6,5},{7,6},{8,15},{9,8},{10,9... | collective-permute-start | bytes 786440 | tf_op jit(solution)/shard_map/ppermute | solution.py:359
  12.1 11.8 %collective-permute-start.2 = (bf16[128,1024]{1,0:T(8,128)(2,1)}, bf16[128,1024]{1,0:T(8,128)(2,1)}, u32[]{:S(2)}, u32[]{:S(2)}) collective-permute-start(bf16[128,1024]{1,0:T(8,128)(2,1)} %normalize.3.refs_6_.refs_2_), channel_id=1, source_target_pairs={{0,1},{1,2},{2,3},{3,4},{4,5},{5,6},{6,7},{7,0},{8,9},{9,10},{10,1... | collective-permute-start | bytes 786440 | tf_op jit(solution)/shard_map/ppermute | solution.py:359
  18.2 21.3 %copy-start.3 = (bf16[128,1024]{1,0:T(8,128)(2,1)}, bf16[128,1024]{1,0:T(8,128)(2,1)S(1)}, u32[]{:S(2)}) copy-start(bf16[128,1024]{1,0:T(8,128)(2,1)S(1)} %collective-permute-done.refs_3_) | copy-start | bytes 786436
  18.3 21.3 %copy-start.4 = (bf16[128,1024]{1,0:T(8,128)(2,1)}, bf16[128,1024]{1,0:T(8,128)(2,1)S(1)}, u32[]{:S(2)}) copy-start(bf16[128,1024]{1,0:T(8,128)(2,1)S(1)} %collective-permute-done.1.refs_7_.refs_15_) | copy-start | bytes 786436
  18.3 9.2 %collective-permute-start.3 = (bf16[128,1024]{1,0:T(8,128)(2,1)S(1)}, bf16[128,1024]{1,0:T(8,128)(2,1)}, u32[]{:S(2)}, u32[]{:S(2)}) collective-permute-start(bf16[128,1024]{1,0:T(8,128)(2,1)S(1)} %collective-permute-done.refs_3_), channel_id=1, source_target_pairs={{0,1},{1,2},{2,3},{3,4},{4,5},{5,6},{6,7},{7,0},{8,9},{9,10},{10,1... | collective-permute-start | bytes 786440 | tf_op jit(solution)/shard_map/ppermute | solution.py:359
  19.8 10.3 %collective-permute-start.7 = (bf16[128,1024]{1,0:T(8,128)(2,1)S(1)}, bf16[128,1024]{1,0:T(8,128)(2,1)}, u32[]{:S(2)}, u32[]{:S(2)}) collective-permute-start(bf16[128,1024]{1,0:T(8,128)(2,1)S(1)} %collective-permute-done.6.refs_8_.refs_16_), channel_id=1, source_target_pairs={{0,7},{1,0},{2,1},{3,2},{4,3},{5,4},{6,5},{7,6},{8,15},{9,8},{10,9... | collective-permute-start | bytes 786440 | tf_op jit(solution)/shard_map/ppermute | solution.py:359
  23.4 12.4 %collective-permute-start.9 = (bf16[128,1024]{1,0:T(8,128)(2,1)S(1)}, bf16[128,1024]{1,0:T(8,128)(2,1)}, u32[]{:S(2)}, u32[]{:S(2)}) collective-permute-start(bf16[128,1024]{1,0:T(8,128)(2,1)S(1)} %collective-permute-done.1.refs_7_.refs_15_), channel_id=1, source_target_pairs={{0,7},{1,0},{2,1},{3,2},{4,3},{5,4},{6,5},{7,6},{8,15},{9,8},{10,9... | collective-permute-start | bytes 786440 | tf_op jit(solution)/shard_map/ppermute | solution.py:359
  23.9 15.6 %collective-permute-start.4 = (bf16[128,1024]{1,0:T(8,128)(2,1)}, bf16[128,1024]{1,0:T(8,128)(2,1)}, u32[]{:S(2)}, u32[]{:S(2)}) collective-permute-start(bf16[128,1024]{1,0:T(8,128)(2,1)} %collective-permute-done.2.refs_4_), channel_id=1, source_target_pairs={{0,1},{1,2},{2,3},{3,4},{4,5},{5,6},{6,7},{7,0},{8,9},{9,10},{10,1... | collective-permute-start | bytes 786440 | tf_op jit(solution)/shard_map/ppermute | solution.py:359
  27.4 19.2 %collective-permute-start.5 = (bf16[128,1024]{1,0:T(8,128)(2,1)}, bf16[128,1024]{1,0:T(8,128)(2,1)}, u32[]{:S(2)}, u32[]{:S(2)}) collective-permute-start(bf16[128,1024]{1,0:T(8,128)(2,1)} %collective-permute-done.3.refs_5_), channel_id=1, source_target_pairs={{0,1},{1,2},{2,3},{3,4},{4,5},{5,6},{6,7},{7,0},{8,9},{9,10},{10,1... | collective-permute-start | bytes 786440 | tf_op jit(solution)/shard_map/ppermute | solution.py:359
  30.2 16.5 %collective-permute-start.8 = (bf16[128,1024]{1,0:T(8,128)(2,1)}, bf16[128,1024]{1,0:T(8,128)(2,1)}, u32[]{:S(2)}, u32[]{:S(2)}) collective-permute-start(bf16[128,1024]{1,0:T(8,128)(2,1)} %collective-permute-done.7.refs_14_), channel_id=1, source_target_pairs={{0,7},{1,0},{2,1},{3,2},{4,3},{5,4},{6,5},{7,6},{8,15},{9,8},{10,9... | collective-permute-start | bytes 786440 | tf_op jit(solution)/shard_map/ppermute | solution.py:359
  35.8 16.2 %collective-permute-start.13 = (bf16[128,1024]{1,0:T(8,128)(2,1)}, bf16[128,1024]{1,0:T(8,128)(2,1)}, u32[]{:S(2)}, u32[]{:S(2)}) collective-permute-start(bf16[128,1024]{1,0:T(8,128)(2,1)} %collective-permute-done.9.refs_13_), channel_id=1, source_target_pairs={{0,7},{1,0},{2,1},{3,2},{4,3},{5,4},{6,5},{7,6},{8,15},{9,8},{10,9... | collective-permute-start | bytes 786440 | tf_op jit(solution)/shard_map/ppermute | solution.py:359
  39.6 18.6 %collective-permute-start.10 = (bf16[128,1024]{1,0:T(8,128)(2,1)}, bf16[128,1024]{1,0:T(8,128)(2,1)}, u32[]{:S(2)}, u32[]{:S(2)}) collective-permute-start(bf16[128,1024]{1,0:T(8,128)(2,1)} %collective-permute-done.4.refs_6_), channel_id=1, source_target_pairs={{0,1},{1,2},{2,3},{3,4},{4,5},{5,6},{6,7},{7,0},{8,9},{9,10},{10,1... | collective-permute-start | bytes 786440 | tf_op jit(solution)/shard_map/ppermute | solution.py:359
  46.7 11.5 %collective-permute-start.11 = (bf16[128,1024]{1,0:T(8,128)(2,1)}, bf16[128,1024]{1,0:T(8,128)(2,1)S(1)}, u32[]{:S(2)}, u32[]{:S(2)}) collective-permute-start(bf16[128,1024]{1,0:T(8,128)(2,1)} %collective-permute-done.5.refs_7_), channel_id=1, source_target_pairs={{0,1},{1,2},{2,3},{3,4},{4,5},{5,6},{6,7},{7,0},{8,9},{9,10},{10,1... | collective-permute-start | bytes 786440 | tf_op jit(solution)/shard_map/ppermute | solution.py:359
  46.8 11.4 %collective-permute-start.12 = (bf16[128,1024]{1,0:T(8,128)(2,1)}, bf16[128,1024]{1,0:T(8,128)(2,1)}, u32[]{:S(2)}, u32[]{:S(2)}) collective-permute-start(bf16[128,1024]{1,0:T(8,128)(2,1)} %collective-permute-done.8.refs_12_), channel_id=1, source_target_pairs={{0,7},{1,0},{2,1},{3,2},{4,3},{5,4},{6,5},{7,6},{8,15},{9,8},{10,9... | collective-permute-start | bytes 786440 | tf_op jit(solution)/shard_map/ppermute | solution.py:359
  50.0 23.0 %collective-permute-start.14 = (bf16[256,1024]{1,0:T(8,128)(2,1)}, bf16[256,1024]{1,0:T(8,128)(2,1)S(1)}, u32[]{:S(2)}, u32[]{:S(2)}) collective-permute-start(bf16[256,1024]{1,0:T(8,128)(2,1)} %get-tuple-element.59), channel_id=1, source_target_pairs={{0,7},{1,0},{2,1},{3,2},{4,3},{5,4},{6,5},{7,6},{8,15},{9,8},{10,9... | collective-permute-start | bytes 1572872 | tf_op jit(solution)/shard_map/ppermute | solution.py:359
  52.0 21.0 %collective-permute-start.15 = (bf16[256,1024]{1,0:T(8,128)(2,1)}, bf16[256,1024]{1,0:T(8,128)(2,1)}, u32[]{:S(2)}, u32[]{:S(2)}) collective-permute-start(bf16[256,1024]{1,0:T(8,128)(2,1)} %get-tuple-element.60), channel_id=1, source_target_pairs={{0,1},{1,2},{2,3},{3,4},{4,5},{5,6},{6,7},{7,0},{8,9},{9,10},{10,1... | collective-permute-start | bytes 1572872 | tf_op jit(solution)/shard_map/ppermute | solution.py:359
  52.1 24.6 %all-to-all-start = ((bf16[8,64,256]{2,1,0:T(8,128)(2,1)}), bf16[8,64,256]{2,1,0:T(8,128)(2,1)}, u32[]{:S(2)}, u32[]{:S(2)}) async-start(bf16[8,64,256]{2,1,0:T(8,128)(2,1)} %d_out.1), calls=%async_computation | async-start | bytes 524288 | tf_op jit(solution)/shard_map/all_to_all | solution.py:355
  76.7 23.9 %all-to-all-start.1 = ((bf16[8,192,256]{2,1,0:T(8,128)(2,1)}), bf16[8,192,256]{2,1,0:T(8,128)(2,1)S(1)}, u32[]{:S(2)}, u32[]{:S(2)}) async-start(bf16[8,192,256]{2,1,0:T(8,128)(2,1)} %get-tuple-element.65), calls=%async_computation.1 | async-start | bytes 1572864 | tf_op jit(solution)/shard_map/all_to_all | solution.py:355
  101.4 22.0 %all-to-all-start.2 = ((bf16[8,192,256]{2,1,0:T(8,128)(2,1)}), bf16[8,192,256]{2,1,0:T(8,128)(2,1)S(1)}, u32[]{:S(2)}, u32[]{:S(2)}) async-start(bf16[8,192,256]{2,1,0:T(8,128)(2,1)} %attend_backward.1.refs_18_), calls=%async_computation.2 | async-start | bytes 1572864 | tf_op jit(solution)/shard_map/all_to_all | solution.py:355
  114.9 2.8 %collective-permute-start.16 = (bf16[16,224,128]{2,1,0:T(8,128)(2,1)}, bf16[16,224,128]{2,1,0:T(8,128)(2,1)S(1)}, u32[]{:S(2)}, u32[]{:S(2)}) collective-permute-start(bf16[16,224,128]{2,1,0:T(8,128)(2,1)} %get-tuple-element.71), channel_id=1, source_target_pairs={{0,8},{8,0},{1,9},{9,1},{2,10},{10,2},{3,11},{11,3},{4,12},{12,4},... | collective-permute-start | bytes 2752520 | tf_op jit(solution)/shard_map/ppermute | solution.py:464
  123.5 28.9 %copy-start = (bf16[8,192,256]{2,1,0:T(8,128)(2,1)}, bf16[8,192,256]{2,1,0:T(8,128)(2,1)S(1)}, u32[]{:S(2)}) copy-start(bf16[8,192,256]{2,1,0:T(8,128)(2,1)S(1)} %all-to-all-done.2.refs_0_) | copy-start | bytes 2359300
  143.0 21.8 %all-to-all-start.4 = ((bf16[8,224,128]{2,1,0:T(8,128)(2,1)}), bf16[8,224,128]{2,1,0:T(8,128)(2,1)}, u32[]{:S(2)}, u32[]{:S(2)}) async-start(bf16[8,224,128]{2,1,0:T(8,128)(2,1)} %share_sum.1), calls=%async_computation.4 | async-start | bytes 917504 | tf_op jit(solution)/shard_map/all_to_all | solution.py:355
  (4 other events, 22.2 us)

commit v7 on v6

--- a/solution.py
+++ b/solution.py
@@ -49,31 +49,16 @@
         in_specs=specs,
         out_specs=tuple(pl.BlockSpec(memory_space=pltpu.VMEM) for _ in out_shape),
         scratch_shapes=list(scratch),
-        compiler_params=pltpu.CompilerParams(vmem_limit_bytes=63 * 1024 * 1024),
+        compiler_params=pltpu.CompilerParams(vmem_limit_bytes=63 * 1024 * 1024 + 512 * 1024),
         cost_estimate=pl.CostEstimate(flops=flops, bytes_accessed=moved, transcendentals=exps),
         name=name,
     )(*scalars, *far, *arrays)
 
 
-def normalize_kernel(x_ref, gain_ref, out_ref):
-    wide = x_ref[...].astype(jnp.float32)
-    out_ref[...] = (wide * unit_factor(wide, -1) * gain_ref[...]).astype(jnp.bfloat16)
-
-
-def normalize_half(features, gain, half):
-    width = features.shape[1]
-    return pl.pallas_call(
-        normalize_kernel,
-        grid=(1,),
-        in_specs=[
-            pl.BlockSpec((BLOCK, width), lambda i: (half, 0)),
-            pl.BlockSpec((1, width), lambda i: (0, 0)),
-        ],
-        out_specs=pl.BlockSpec((BLOCK, width), lambda i: (0, 0)),
-        out_shape=jax.ShapeDtypeStruct((BLOCK, width), jnp.bfloat16),
-        cost_estimate=pl.CostEstimate(flops=0, bytes_accessed=1 << 19, transcendentals=0),
-        name="normalize",
-    )(features, gain)
+def normalize_kernel(x_ref, gain_ref, *out_refs):
+    for half, out_ref in enumerate(out_refs):
+        wide = x_ref[half * BLOCK : (half + 1) * BLOCK].astype(jnp.float32)
+        out_ref[...] = (wide * unit_factor(wide, -1) * gain_ref[...]).astype(jnp.bfloat16)
 
 
 def d_out_kernel(grad_ref, w_ref, out_ref):
@@ -202,8 +187,12 @@
     v_ext, held, sems = refs[24:]
     wait = fetch_chunks(refs[1:17], held, sems)
     for j in range(N_SEQ):
-        wait(j)
-        proj = matmul(held[j], w_ref[...]).T.astype(jnp.bfloat16)
+        if j % 4 == 0:
+            for i in range(j, j + 4):
+                wait(i)
+            rows = held[j : j + 4].reshape(4 * CHUNK, held.shape[2])
+            group = matmul(rows, w_ref[...]).T.astype(jnp.bfloat16)
+        proj = group[:, j % 4 * CHUNK : (j % 4 + 1) * CHUNK]
         raw_ref[j] = proj[: 2 * HEAD_DIM]
         query = proj[:HEAD_DIM].astype(jnp.float32)
         keyrow = proj[HEAD_DIM : 2 * HEAD_DIM].astype(jnp.float32)
@@ -390,9 +379,10 @@
     wide_shape = ((node_rows, width), f32)
     low_shape = ((node_rows, width), bf16)
 
-    n_a = normalize_half(features, gain, 0)
+    n_a, n_b = call(
+        normalize_kernel, "normalize", (((BLOCK, width), bf16),) * 2, (), (features, gain), moved=1 << 20
+    )
     a_up, a_down = [n_a, up(n_a)], [n_a, down(n_a)]
-    n_b = normalize_half(features, gain, 1)
     b_up, b_down = [n_b, up(n_b)], [n_b, down(n_b)]
     w_head = pick_head(place, w_qkv)
     (d_out,) = call(

time: 168 us -> 165 us (0.982)
  Pallas kernels: 66 us -> 62.8 us
  waiting for transfers between devices: 21.3 us -> 23.7 us
    pallas_call x2 -> x0, Pallas kernels: 3.62 us -> none  [normalize_half(): pl.pallas_call(normalize_kernel, grid=(1,), in_specs=[pl.BlockSpec((BLOCK...]
    ppermute x16, waiting for transfers between devices: 8.02 us -> 10.3 us  [shift(): lax.ppermute(array, 'z', [(i, (i + distance) % N_SEQ) for i in range(N_SE...]
    pallas_call x9 -> x10, Pallas kernels: 59.4 us -> 59.8 us  [call(): pl.pallas_call(kernel, out_shape=tuple((jax.ShapeDtypeStruct(s, t) for s,...]
  transfers between devices with their start and end apart: 21 -> 21, of which waited for: 8 -> 8; matrix products, arithmetic and copies ran while one was open for 4% -> 4% of each run, Pallas kernels for 36% -> 35%
where the time goes in v7:
time: 165 us
  Pallas kernels  62.8 us (38%)
  starting transfers between devices  52.1 us (32%)
  waiting for transfers between devices  23.7 us (14%)
  blocking collectives  17.4 us (11%)
  local copies, waits for them, and re-layouts  5.79 us (4%)
  other arithmetic  2 us (1%)
    pallas_call x10, Pallas kernels, call(): pl.pallas_call(kernel, out_shape=tuple((jax.ShapeDtypeStruct(s, t) for s,...  59.8 us
    ppermute x16, starting transfers between devices, shift(): lax.ppermute(array, 'z', [(i, (i + distance) % N_SEQ) for i in range(N_SE...  26.5 us
    all_to_all x4, starting transfers between devices, exchange(): return lax.all_to_all(array, axis, split_axis=0, concat_axis=0, tiled=True)  25.5 us
    all_to_all x1, blocking collectives, exchange(): return lax.all_to_all(array, axis, split_axis=0, concat_axis=0, tiled=True)  17.4 us
    all_to_all x4, waiting for transfers between devices, exchange(): return lax.all_to_all(array, axis, split_axis=0, concat_axis=0, tiled=True)  10.8 us
    ppermute x16, waiting for transfers between devices, shift(): lax.ppermute(array, 'z', [(i, (i + distance) % N_SEQ) for i in range(N_SE...  10.3 us
  transfers between devices with their start and end apart: 21, of which 8 were waited for; matrix products, arithmetic and copies ran while one was open for 4% of the time, Pallas kernels for 35%

profile of v7, /device:TPU:6, one launch (start us, length us, event | category | flops | bytes accessed | tf_op | source)
XLA Modules:
  0.0 164.5 jit_solution(7503692795756267844)
XLA Ops:
  4.6 3.9 %collective-permute-start.1 = (bf16[128,1024]{1,0:T(8,128)(2,1)}, bf16[128,1024]{1,0:T(8,128)(2,1)}, u32[]{:S(2)}, u32[]{:S(2)}) collective-permute-start(bf16[128,1024]{1,0:T(8,128)(2,1)} %get-tuple-element.46.refs_5_.refs_1_), channel_id=1, source_target_pairs={{0,7},{1,0},{2,1},{3,2},{4,3},{5,4},{6,5},{7,6},{8,15},{9,8},{10,9... | collective-permute-start | bytes 786440 | tf_op jit(solution)/shard_map/ppermute | solution.py:348
  11.1 2.9 %pick_head.1.refs_17_ = bf16[1024,256]{1,0:T(8,128)(2,1)} custom-call(s32[2]{0:T(128)} %pad_add_fusion.place_ref.refs_0_, bf16[1024,1536]{1,0:T(8,128)(2,1)} %refs_1_.3, bf16[1024,1536]{1,0:T(8,128)(2,1)} %refs_1_.3, bf16[1024,1536]{1,0:T(8,128)(2,1)} %refs_1_.3), custom_call_target="tpu_custom_call" | custom-call | bytes 4194304 | tf_op jit(solution)/shard_map/pick_head/pallas_call | solution.py:93
  14.0 2.6 %d_out.1 = bf16[8,64,256]{2,1,0:T(8,128)(2,1)} custom-call(bf16[256,1024]{1,0:T(8,128)(2,1)} %refs_5_.1, bf16[512,1024]{1,0:T(8,128)(2,1)} %refs_19_.1), custom_call_target="tpu_custom_call" | custom-call | flops 268435456 | bytes 2097152 | tf_op jit(solution)/shard_map/d_out/pallas_call | solution.py:46
  16.7 3.3 %collective-permute-done.6.refs_8_.refs_16_ = bf16[128,1024]{1,0:T(8,128)(2,1)} collective-permute-done((bf16[128,1024]{1,0:T(8,128)(2,1)}, bf16[128,1024]{1,0:T(8,128)(2,1)}, u32[]{:S(2)}, u32[]{:S(2)}) %collective-permute-start.6) | collective-permute-done | bytes 262176 | tf_op jit(solution)/shard_map/ppermute | solution.py:348
  20.0 3.7 %collective-permute-start.7 = (bf16[128,1024]{1,0:T(8,128)(2,1)}, bf16[128,1024]{1,0:T(8,128)(2,1)}, u32[]{:S(2)}, u32[]{:S(2)}) collective-permute-start(bf16[128,1024]{1,0:T(8,128)(2,1)} %collective-permute-done.6.refs_8_.refs_16_), channel_id=1, source_target_pairs={{0,7},{1,0},{2,1},{3,2},{4,3},{5,4},{6,5},{7,6},{8,15},{9,8},{10,9... | collective-permute-start | bytes 786440 | tf_op jit(solution)/shard_map/ppermute | solution.py:348
  26.3 4.4 %collective-permute-done.7.refs_14_ = bf16[128,1024]{1,0:T(8,128)(2,1)} collective-permute-done((bf16[128,1024]{1,0:T(8,128)(2,1)}, bf16[128,1024]{1,0:T(8,128)(2,1)}, u32[]{:S(2)}, u32[]{:S(2)}) %collective-permute-start.7) | collective-permute-done | bytes 262176 | tf_op jit(solution)/shard_map/ppermute | solution.py:348
  30.8 3.7 %collective-permute-start.8 = (bf16[128,1024]{1,0:T(8,128)(2,1)}, bf16[128,1024]{1,0:T(8,128)(2,1)}, u32[]{:S(2)}, u32[]{:S(2)}) collective-permute-start(bf16[128,1024]{1,0:T(8,128)(2,1)} %collective-permute-done.7.refs_14_), channel_id=1, source_target_pairs={{0,7},{1,0},{2,1},{3,2},{4,3},{5,4},{6,5},{7,6},{8,15},{9,8},{10,9... | collective-permute-start | bytes 786440 | tf_op jit(solution)/shard_map/ppermute | solution.py:348
  36.4 3.7 %collective-permute-start.13 = (bf16[128,1024]{1,0:T(8,128)(2,1)}, bf16[128,1024]{1,0:T(8,128)(2,1)}, u32[]{:S(2)}, u32[]{:S(2)}) collective-permute-start(bf16[128,1024]{1,0:T(8,128)(2,1)} %collective-permute-done.9.refs_13_), channel_id=1, source_target_pairs={{0,7},{1,0},{2,1},{3,2},{4,3},{5,4},{6,5},{7,6},{8,15},{9,8},{10,9... | collective-permute-start | bytes 786440 | tf_op jit(solution)/shard_map/ppermute | solution.py:348
  40.1 7.1 %messages.1 = (f32[256,1024]{1,0:T(8,128)}, bf16[256,1024]{1,0:T(8,128)(2,1)}, f32[256,1024]{1,0:T(8,128)}, bf16[256,1024]{1,0:T(8,128)(2,1)}) custom-call(s32[2]{0:T(128)} %pad_add_fusion.place_ref.refs_0_, s32[2,4]{1,0:T(2,128)} %refs_1_.2, s32[2]{0:T(128)} %refs_2_.1, bf16[128,1024]{1,0:T(8,128)(2,1)} %copy-done.1, ...), custom_call_target="tpu_custom_call" | custom-call | flops 2147483648 | bytes 8388608 | tf_op jit(solution)/shard_map/messages/pallas_call | solution.py:46
  47.3 3.3 %collective-permute-start.12 = (bf16[128,1024]{1,0:T(8,128)(2,1)}, bf16[128,1024]{1,0:T(8,128)(2,1)}, u32[]{:S(2)}, u32[]{:S(2)}) collective-permute-start(bf16[128,1024]{1,0:T(8,128)(2,1)} %collective-permute-done.8.refs_12_), channel_id=1, source_target_pairs={{0,7},{1,0},{2,1},{3,2},{4,3},{5,4},{6,5},{7,6},{8,15},{9,8},{10,9... | collective-permute-start | bytes 786440 | tf_op jit(solution)/shard_map/ppermute | solution.py:348
  52.6 6.0 %all-to-all-start = ((bf16[8,64,256]{2,1,0:T(8,128)(2,1)}), bf16[8,64,256]{2,1,0:T(8,128)(2,1)}, u32[]{:S(2)}, u32[]{:S(2)}) async-start(bf16[8,64,256]{2,1,0:T(8,128)(2,1)} %d_out.1), calls=%async_computation | async-start | bytes 524288 | tf_op jit(solution)/shard_map/all_to_all | solution.py:344
  59.4 12.5 %attend_forward.1 = (bf16[8,64,256]{2,1,0:T(8,128)(2,1)}, bf16[8,256,128]{2,1,0:T(8,128)(2,1)}, bf16[8,64,256]{2,1,0:T(8,128)(2,1)}, bf16[8,64,256]{2,1,0:T(8,12...) custom-call(s32[2]{0:T(128)} %pad_add_fusion.place_ref.refs_0_, ...), custom_call_target="tpu_custom_call" | custom-call | flops 3221225472 | bytes 8388608 | tf_op jit(solution)/shard_map/attend_forward/pallas_call | solution.py:46
  72.0 2.9 %merge.1 = (bf16[8,192,256]{2,1,0:T(8,128)(2,1)}, bf16[256,1024]{1,0:T(8,128)(2,1)}) custom-call(bf16[8,64,256]{2,1,0:T(8,128)(2,1)} %get-tuple-element.56.heads_ref.refs_1_, f32[256,1024]{1,0:T(8,128)} %get-tuple-element.62.mid_ref, bf16[256,1024]{1,0:T(8,128)(2,1)} %collective-permute-done.14.above_ref, bf16[256,1024]{1,0:T(8,128)(2,1)} %collective-permute-done.15.below_ref), custom_call_target="tpu_custom_call" | custom-call | bytes 4194304 | tf_op jit(solution)/shard_map/merge/pallas_call | solution.py:46
  74.8 7.2 %all-to-all-start.1 = ((bf16[8,192,256]{2,1,0:T(8,128)(2,1)}), bf16[8,192,256]{2,1,0:T(8,128)(2,1)}, u32[]{:S(2)}, u32[]{:S(2)}) async-start(bf16[8,192,256]{2,1,0:T(8,128)(2,1)} %get-tuple-element.69), calls=%async_computation.1 | async-start | bytes 1572864 | tf_op jit(solution)/shard_map/all_to_all | solution.py:344
  82.0 15.3 %attend_backward.1.refs_18_ = bf16[8,192,256]{2,1,0:T(8,128)(2,1)} custom-call(s32[2]{0:T(128)} %pad_add_fusion.place_ref.refs_0_, bf16[8,64,256]{2,1,0:T(8,128)(2,1)} %get-tuple-element.56.heads_ref.refs_1_, bf16[8,256,128]{2,1,0:T(8,128)(2,1)} %get-tuple-element.57.refs_2_, bf16[8,64,256]{2,1,0:T(8,128)(2,1)} %get-tuple-element.58.refs_3_, ...), custom_call_target="tpu_custom_call" | custom-call | flops 6442450944 | bytes 4194304 | tf_op jit(solution)/shard_map/attend_backward/pallas_call | solution.py:46
  98.9 5.7 %all-to-all-start.2 = ((bf16[8,192,256]{2,1,0:T(8,128)(2,1)}), bf16[8,192,256]{2,1,0:T(8,128)(2,1)}, u32[]{:S(2)}, u32[]{:S(2)}) async-start(bf16[8,192,256]{2,1,0:T(8,128)(2,1)} %attend_backward.1.refs_18_), calls=%async_computation.2 | async-start | bytes 1572864 | tf_op jit(solution)/shard_map/all_to_all | solution.py:344
  104.6 7.6 %result.1 = (bf16[256,1024]{1,0:T(8,128)(2,1)}, bf16[16,224,128]{2,1,0:T(8,128)(2,1)}, bf16[16,224,128]{2,1,0:T(8,128)(2,1)}) custom-call(s32[2]{0:T(128)} %pad_add_fusion.place_ref.refs_0_, bf16[128,1024]{1,0:T(8,128)(2,1)} %get-tuple-element.46.refs_5_.refs_1_, bf16[128,1024]{1,0:T(8,128)(2,1)} %get-tuple-element.47.refs_6_.refs_2_, ...), custom_call_target="tpu_custom_call" | custom-call | flops 2147483648 | bytes 10485760 | tf_op jit(solution)/shard_map/result/pallas_call | solution.py:46
  112.3 2.7 %collective-permute-done.16 = bf16[16,224,128]{2,1,0:T(8,128)(2,1)S(1)} collective-permute-done((bf16[16,224,128]{2,1,0:T(8,128)(2,1)}, bf16[16,224,128]{2,1,0:T(8,128)(2,1)S(1)}, u32[]{:S(2)}, u32[]{:S(2)}) %collective-permute-start.16) | collective-permute-done | bytes 917536 | tf_op jit(solution)/shard_map/ppermute | solution.py:454
  116.4 4.5 %all-to-all-done.2.refs_0_ = bf16[8,192,256]{2,1,0:T(8,128)(2,1)} async-done(((bf16[8,192,256]{2,1,0:T(8,128)(2,1)}), bf16[8,192,256]{2,1,0:T(8,128)(2,1)}, u32[]{:S(2)}, u32[]{:S(2)}) %all-to-all-start.2) | async-done | bytes 786464 | tf_op jit(solution)/shard_map/all_to_all | solution.py:344
  120.9 17.4 %all_to_all.25.shares_ref = bf16[16,224,128]{2,1,0:T(8,128)(2,1)} all-to-all(bf16[16,224,128]{2,1,0:T(8,128)(2,1)S(1)} %add_convert_fusion), channel_id=1, replica_groups=mesh['x'=4,'y'=4,'c'=2,'z'=8] {'x','y'}, dimensions={0} | all-to-all | bytes 1835008 | tf_op jit(solution)/shard_map/all_to_all | solution.py:344
  138.3 2.1 %share_sum.1 = bf16[8,224,128]{2,1,0:T(8,128)(2,1)} custom-call(bf16[16,224,128]{2,1,0:T(8,128)(2,1)} %all_to_all.25.shares_ref), custom_call_target="tpu_custom_call" | custom-call | bytes 2097152 | tf_op jit(solution)/shard_map/share_sum/pallas_call | solution.py:46
  140.3 6.5 %all-to-all-start.4 = ((bf16[8,224,128]{2,1,0:T(8,128)(2,1)}), bf16[8,224,128]{2,1,0:T(8,128)(2,1)S(1)}, u32[]{:S(2)}, u32[]{:S(2)}) async-start(bf16[8,224,128]{2,1,0:T(8,128)(2,1)} %share_sum.1), calls=%async_computation.4 | async-start | bytes 917504 | tf_op jit(solution)/shard_map/all_to_all | solution.py:344
  151.2 5.8 %input_grad.1 = bf16[256,1024]{1,0:T(8,128)(2,1)} custom-call(bf16[8,192,256]{2,1,0:T(8,128)(2,1)} %all-to-all-done.2.refs_0_, bf16[1024,1536]{1,0:T(8,128)(2,1)} %refs_1_.3, bf16[256,1024]{1,0:T(8,128)(2,1)} %get-tuple-element.79.refs_2_, bf16[1024,1024]{1,0:T(8,128)(2,1)} %refs_3_.1, bf16[256,1024]{1,0:T(8,128)(2,1)} %refs_4_.1, ...), custom_call_target="tpu_custom_call" | custom-call | flops 805306368 | bytes 8388608 | tf_op jit(solution)/shard_map/input_grad/pallas_call | solution.py:46
  157.0 4.8 %all-to-all-done.4.every_ref = bf16[8,224,128]{2,1,0:T(8,128)(2,1)S(1)} async-done(((bf16[8,224,128]{2,1,0:T(8,128)(2,1)}), bf16[8,224,128]{2,1,0:T(8,128)(2,1)S(1)}, u32[]{:S(2)}, u32[]{:S(2)}) %all-to-all-start.4) | async-done | bytes 458784 | tf_op jit(solution)/shard_map/all_to_all | solution.py:344
  (41 shorter events, 24.1 us)
Async XLA Ops:
  2.6 14.0 %collective-permute-start = (bf16[128,1024]{1,0:T(8,128)(2,1)}, bf16[128,1024]{1,0:T(8,128)(2,1)S(1)}, u32[]{:S(2)}, u32[]{:S(2)}) collective-permute-start(bf16[128,1024]{1,0:T(8,128)(2,1)} %get-tuple-element.46.refs_5_.refs_1_), channel_id=1, source_target_pairs={{0,1},{1,2},{2,3},{3,4},{4,5},{5,6},{6,7},{7,0},{8,9},{9,10},{10,1... | collective-permute-start | bytes 786440 | tf_op jit(solution)/shard_map/ppermute | solution.py:348
  4.6 12.1 %collective-permute-start.1 = (bf16[128,1024]{1,0:T(8,128)(2,1)}, bf16[128,1024]{1,0:T(8,128)(2,1)}, u32[]{:S(2)}, u32[]{:S(2)}) collective-permute-start(bf16[128,1024]{1,0:T(8,128)(2,1)} %get-tuple-element.46.refs_5_.refs_1_), channel_id=1, source_target_pairs={{0,7},{1,0},{2,1},{3,2},{4,3},{5,4},{6,5},{7,6},{8,15},{9,8},{10,9... | collective-permute-start | bytes 786440 | tf_op jit(solution)/shard_map/ppermute | solution.py:348
  8.5 11.5 %collective-permute-start.6 = (bf16[128,1024]{1,0:T(8,128)(2,1)}, bf16[128,1024]{1,0:T(8,128)(2,1)}, u32[]{:S(2)}, u32[]{:S(2)}) collective-permute-start(bf16[128,1024]{1,0:T(8,128)(2,1)} %get-tuple-element.47.refs_6_.refs_2_), channel_id=1, source_target_pairs={{0,7},{1,0},{2,1},{3,2},{4,3},{5,4},{6,5},{7,6},{8,15},{9,8},{10,9... | collective-permute-start | bytes 786440 | tf_op jit(solution)/shard_map/ppermute | solution.py:348
  10.5 13.7 %collective-permute-start.2 = (bf16[128,1024]{1,0:T(8,128)(2,1)}, bf16[128,1024]{1,0:T(8,128)(2,1)}, u32[]{:S(2)}, u32[]{:S(2)}) collective-permute-start(bf16[128,1024]{1,0:T(8,128)(2,1)} %get-tuple-element.47.refs_6_.refs_2_), channel_id=1, source_target_pairs={{0,1},{1,2},{2,3},{3,4},{4,5},{5,6},{6,7},{7,0},{8,9},{9,10},{10,1... | collective-permute-start | bytes 786440 | tf_op jit(solution)/shard_map/ppermute | solution.py:348
  16.6 23.4 %copy-start.1 = (bf16[128,1024]{1,0:T(8,128)(2,1)}, bf16[128,1024]{1,0:T(8,128)(2,1)S(1)}, u32[]{:S(2)}) copy-start(bf16[128,1024]{1,0:T(8,128)(2,1)S(1)} %collective-permute-done.refs_3_) | copy-start | bytes 786436
  16.6 9.7 %collective-permute-start.3 = (bf16[128,1024]{1,0:T(8,128)(2,1)S(1)}, bf16[128,1024]{1,0:T(8,128)(2,1)}, u32[]{:S(2)}, u32[]{:S(2)}) collective-permute-start(bf16[128,1024]{1,0:T(8,128)(2,1)S(1)} %collective-permute-done.refs_3_), channel_id=1, source_target_pairs={{0,1},{1,2},{2,3},{3,4},{4,5},{5,6},{6,7},{7,0},{8,9},{9,10},{10,1... | collective-permute-start | bytes 786440 | tf_op jit(solution)/shard_map/ppermute | solution.py:348
  20.0 10.8 %collective-permute-start.7 = (bf16[128,1024]{1,0:T(8,128)(2,1)}, bf16[128,1024]{1,0:T(8,128)(2,1)}, u32[]{:S(2)}, u32[]{:S(2)}) collective-permute-start(bf16[128,1024]{1,0:T(8,128)(2,1)} %collective-permute-done.6.refs_8_.refs_16_), channel_id=1, source_target_pairs={{0,7},{1,0},{2,1},{3,2},{4,3},{5,4},{6,5},{7,6},{8,15},{9,8},{10,9... | collective-permute-start | bytes 786440 | tf_op jit(solution)/shard_map/ppermute | solution.py:348
  23.7 12.7 %collective-permute-start.9 = (bf16[128,1024]{1,0:T(8,128)(2,1)}, bf16[128,1024]{1,0:T(8,128)(2,1)}, u32[]{:S(2)}, u32[]{:S(2)}) collective-permute-start(bf16[128,1024]{1,0:T(8,128)(2,1)} %collective-permute-done.1.refs_7_.refs_15_), channel_id=1, source_target_pairs={{0,7},{1,0},{2,1},{3,2},{4,3},{5,4},{6,5},{7,6},{8,15},{9,8},{10,9... | collective-permute-start | bytes 786440 | tf_op jit(solution)/shard_map/ppermute | solution.py:348
  24.2 15.9 %collective-permute-start.4 = (bf16[128,1024]{1,0:T(8,128)(2,1)}, bf16[128,1024]{1,0:T(8,128)(2,1)}, u32[]{:S(2)}, u32[]{:S(2)}) collective-permute-start(bf16[128,1024]{1,0:T(8,128)(2,1)} %collective-permute-done.2.refs_4_), channel_id=1, source_target_pairs={{0,1},{1,2},{2,3},{3,4},{4,5},{5,6},{6,7},{7,0},{8,9},{9,10},{10,1... | collective-permute-start | bytes 786440 | tf_op jit(solution)/shard_map/ppermute | solution.py:348
  26.3 20.9 %collective-permute-start.5 = (bf16[128,1024]{1,0:T(8,128)(2,1)}, bf16[128,1024]{1,0:T(8,128)(2,1)}, u32[]{:S(2)}, u32[]{:S(2)}) collective-permute-start(bf16[128,1024]{1,0:T(8,128)(2,1)} %collective-permute-done.3.refs_5_), channel_id=1, source_target_pairs={{0,1},{1,2},{2,3},{3,4},{4,5},{5,6},{6,7},{7,0},{8,9},{9,10},{10,1... | collective-permute-start | bytes 786440 | tf_op jit(solution)/shard_map/ppermute | solution.py:348
  30.8 16.4 %collective-permute-start.8 = (bf16[128,1024]{1,0:T(8,128)(2,1)}, bf16[128,1024]{1,0:T(8,128)(2,1)}, u32[]{:S(2)}, u32[]{:S(2)}) collective-permute-start(bf16[128,1024]{1,0:T(8,128)(2,1)} %collective-permute-done.7.refs_14_), channel_id=1, source_target_pairs={{0,7},{1,0},{2,1},{3,2},{4,3},{5,4},{6,5},{7,6},{8,15},{9,8},{10,9... | collective-permute-start | bytes 786440 | tf_op jit(solution)/shard_map/ppermute | solution.py:348
  36.4 16.2 %collective-permute-start.13 = (bf16[128,1024]{1,0:T(8,128)(2,1)}, bf16[128,1024]{1,0:T(8,128)(2,1)}, u32[]{:S(2)}, u32[]{:S(2)}) collective-permute-start(bf16[128,1024]{1,0:T(8,128)(2,1)} %collective-permute-done.9.refs_13_), channel_id=1, source_target_pairs={{0,7},{1,0},{2,1},{3,2},{4,3},{5,4},{6,5},{7,6},{8,15},{9,8},{10,9... | collective-permute-start | bytes 786440 | tf_op jit(solution)/shard_map/ppermute | solution.py:348
  40.1 18.6 %collective-permute-start.10 = (bf16[128,1024]{1,0:T(8,128)(2,1)}, bf16[128,1024]{1,0:T(8,128)(2,1)}, u32[]{:S(2)}, u32[]{:S(2)}) collective-permute-start(bf16[128,1024]{1,0:T(8,128)(2,1)} %collective-permute-done.4.refs_6_), channel_id=1, source_target_pairs={{0,1},{1,2},{2,3},{3,4},{4,5},{5,6},{6,7},{7,0},{8,9},{9,10},{10,1... | collective-permute-start | bytes 786440 | tf_op jit(solution)/shard_map/ppermute | solution.py:348
  47.2 11.5 %collective-permute-start.11 = (bf16[128,1024]{1,0:T(8,128)(2,1)}, bf16[128,1024]{1,0:T(8,128)(2,1)S(1)}, u32[]{:S(2)}, u32[]{:S(2)}) collective-permute-start(bf16[128,1024]{1,0:T(8,128)(2,1)} %collective-permute-done.5.refs_7_), channel_id=1, source_target_pairs={{0,1},{1,2},{2,3},{3,4},{4,5},{5,6},{6,7},{7,0},{8,9},{9,10},{10,1... | collective-permute-start | bytes 786440 | tf_op jit(solution)/shard_map/ppermute | solution.py:348
  47.3 11.4 %collective-permute-start.12 = (bf16[128,1024]{1,0:T(8,128)(2,1)}, bf16[128,1024]{1,0:T(8,128)(2,1)}, u32[]{:S(2)}, u32[]{:S(2)}) collective-permute-start(bf16[128,1024]{1,0:T(8,128)(2,1)} %collective-permute-done.8.refs_12_), channel_id=1, source_target_pairs={{0,7},{1,0},{2,1},{3,2},{4,3},{5,4},{6,5},{7,6},{8,15},{9,8},{10,9... | collective-permute-start | bytes 786440 | tf_op jit(solution)/shard_map/ppermute | solution.py:348
  50.6 21.3 %collective-permute-start.14 = (bf16[256,1024]{1,0:T(8,128)(2,1)}, bf16[256,1024]{1,0:T(8,128)(2,1)}, u32[]{:S(2)}, u32[]{:S(2)}) collective-permute-start(bf16[256,1024]{1,0:T(8,128)(2,1)} %get-tuple-element.63), channel_id=1, source_target_pairs={{0,7},{1,0},{2,1},{3,2},{4,3},{5,4},{6,5},{7,6},{8,15},{9,8},{10,9... | collective-permute-start | bytes 1572872 | tf_op jit(solution)/shard_map/ppermute | solution.py:348
  52.5 19.4 %collective-permute-start.15 = (bf16[256,1024]{1,0:T(8,128)(2,1)}, bf16[256,1024]{1,0:T(8,128)(2,1)}, u32[]{:S(2)}, u32[]{:S(2)}) collective-permute-start(bf16[256,1024]{1,0:T(8,128)(2,1)} %get-tuple-element.64), channel_id=1, source_target_pairs={{0,1},{1,2},{2,3},{3,4},{4,5},{5,6},{6,7},{7,0},{8,9},{9,10},{10,1... | collective-permute-start | bytes 1572872 | tf_op jit(solution)/shard_map/ppermute | solution.py:348
  52.6 22.2 %all-to-all-start = ((bf16[8,64,256]{2,1,0:T(8,128)(2,1)}), bf16[8,64,256]{2,1,0:T(8,128)(2,1)}, u32[]{:S(2)}, u32[]{:S(2)}) async-start(bf16[8,64,256]{2,1,0:T(8,128)(2,1)} %d_out.1), calls=%async_computation | async-start | bytes 524288 | tf_op jit(solution)/shard_map/all_to_all | solution.py:344
  58.7 0.7 copy-start.2
  74.8 24.0 %all-to-all-start.1 = ((bf16[8,192,256]{2,1,0:T(8,128)(2,1)}), bf16[8,192,256]{2,1,0:T(8,128)(2,1)}, u32[]{:S(2)}, u32[]{:S(2)}) async-start(bf16[8,192,256]{2,1,0:T(8,128)(2,1)} %get-tuple-element.69), calls=%async_computation.1 | async-start | bytes 1572864 | tf_op jit(solution)/shard_map/all_to_all | solution.py:344
  98.9 22.0 %all-to-all-start.2 = ((bf16[8,192,256]{2,1,0:T(8,128)(2,1)}), bf16[8,192,256]{2,1,0:T(8,128)(2,1)}, u32[]{:S(2)}, u32[]{:S(2)}) async-start(bf16[8,192,256]{2,1,0:T(8,128)(2,1)} %attend_backward.1.refs_18_), calls=%async_computation.2 | async-start | bytes 1572864 | tf_op jit(solution)/shard_map/all_to_all | solution.py:344
  112.2 2.8 %collective-permute-start.16 = (bf16[16,224,128]{2,1,0:T(8,128)(2,1)}, bf16[16,224,128]{2,1,0:T(8,128)(2,1)S(1)}, u32[]{:S(2)}, u32[]{:S(2)}) collective-permute-start(bf16[16,224,128]{2,1,0:T(8,128)(2,1)} %get-tuple-element.75), channel_id=1, source_target_pairs={{0,8},{8,0},{1,9},{9,1},{2,10},{10,2},{3,11},{11,3},{4,12},{12,4},... | collective-permute-start | bytes 2752520 | tf_op jit(solution)/shard_map/ppermute | solution.py:454
  140.3 21.5 %all-to-all-start.4 = ((bf16[8,224,128]{2,1,0:T(8,128)(2,1)}), bf16[8,224,128]{2,1,0:T(8,128)(2,1)S(1)}, u32[]{:S(2)}, u32[]{:S(2)}) async-start(bf16[8,224,128]{2,1,0:T(8,128)(2,1)} %share_sum.1), calls=%async_computation.4 | async-start | bytes 917504 | tf_op jit(solution)/shard_map/all_to_all | solution.py:344
  161.8 0.8 copy-start

commit v8 on v7

--- a/solution.py
+++ b/solution.py
@@ -394,6 +394,7 @@
     a_down.append(down(a_down[1]))
     b_up.append(up(b_up[1]))
     b_down.append(down(b_down[1]))
+    d_heads = exchange(after(d_out, a_up[2]), "z")
     a_up.append(up(a_up[2]))
     a_down.append(down(a_down[2]))
     act, to_low, mid, to_high = call(
@@ -403,10 +404,11 @@
         [pltpu.VMEM((6, BLOCK, width), bf16), pltpu.VMEM((6, BLOCK, width), f32)],
         flops=8 * node_rows * width * width, exps=node_rows * width, moved=8 << 20,
     )
-    d_heads = exchange(after(d_out, a_up[3], a_down[3]), "z")
     b_up.append(up(b_up[2]))
     b_down.append(down(b_down[2]))
-    a_up[3], b_down[3], to_low, to_high = lax.optimization_barrier((a_up[3], b_down[3], to_low, to_high))
+    a_up[3], b_down[3], to_low, to_high, d_heads = lax.optimization_barrier(
+        (a_up[3], b_down[3], to_low, to_high, d_heads)
+    )
     c4 = [up(a_up[3]), down(b_down[3])]
     above, below = down(to_low), up(to_high)
     pairs = list(zip(a_up, b_up)) + [c4] + list(zip(a_down, b_down))[:0:-1]

time: 165 us -> 165 us (level)
    all_to_all x4, starting transfers between devices: 25.5 us -> 21 us  [exchange(): return lax.all_to_all(array, axis, split_axis=0, concat_axis=0, tiled=True)]
    ppermute x16, starting transfers between devices: 26.5 us -> 29.8 us  [shift(): lax.ppermute(array, 'z', [(i, (i + distance) % N_SEQ) for i in range(N_SE...]
  transfers between devices with their start and end apart: 21 -> 21, of which waited for: 8 -> 7; matrix products, arithmetic and copies ran while one was open for 4% -> 4% of each run, Pallas kernels for 35% -> 33%
where the time goes in v8:
time: 165 us; the launch traced here: 164 us
  Pallas kernels  62.8 us (38%)
  starting transfers between devices  50.9 us (31%)
  waiting for transfers between devices  24.5 us (15%)
  blocking collectives  17.4 us (11%)
  local copies, waits for them, and re-layouts  5.77 us (3%)
  other arithmetic  2 us (1%)
    pallas_call x10, Pallas kernels, call(): pl.pallas_call(kernel, out_shape=tuple((jax.ShapeDtypeStruct(s, t) for s,...  59.8 us
    ppermute x16, starting transfers between devices, shift(): lax.ppermute(array, 'z', [(i, (i + distance) % N_SEQ) for i in range(N_SE...  29.8 us
    all_to_all x4, starting transfers between devices, exchange(): return lax.all_to_all(array, axis, split_axis=0, concat_axis=0, tiled=True)  21 us
    all_to_all x1, blocking collectives, exchange(): return lax.all_to_all(array, axis, split_axis=0, concat_axis=0, tiled=True)  17.4 us
    all_to_all x4, waiting for transfers between devices, exchange(): return lax.all_to_all(array, axis, split_axis=0, concat_axis=0, tiled=True)  12 us
    ppermute x16, waiting for transfers between devices, shift(): lax.ppermute(array, 'z', [(i, (i + distance) % N_SEQ) for i in range(N_SE...  9.85 us
  transfers between devices with their start and end apart: 21, of which 7 were waited for; matrix products, arithmetic and copies ran while one was open for 4% of the time, Pallas kernels for 33%

profile of v8, /device:TPU:6, one launch (start us, length us, event | category | flops | bytes accessed | tf_op | source)
XLA Modules:
  0.0 164.1 jit_solution(9237815906866263440)
XLA Ops:
  4.5 3.9 %collective-permute-start.1 = (bf16[128,1024]{1,0:T(8,128)(2,1)}, bf16[128,1024]{1,0:T(8,128)(2,1)}, u32[]{:S(2)}, u32[]{:S(2)}) collective-permute-start(bf16[128,1024]{1,0:T(8,128)(2,1)} %get-tuple-element.47.refs_5_.refs_1_), channel_id=1, source_target_pairs={{0,7},{1,0},{2,1},{3,2},{4,3},{5,4},{6,5},{7,6},{8,15},{9,8},{10,9... | collective-permute-start | bytes 786440 | tf_op jit(solution)/shard_map/ppermute | solution.py:348
  8.5 3.2 %collective-permute-start.6 = (bf16[128,1024]{1,0:T(8,128)(2,1)}, bf16[128,1024]{1,0:T(8,128)(2,1)}, u32[]{:S(2)}, u32[]{:S(2)}) collective-permute-start(bf16[128,1024]{1,0:T(8,128)(2,1)} %get-tuple-element.48.refs_6_.refs_2_), channel_id=1, source_target_pairs={{0,7},{1,0},{2,1},{3,2},{4,3},{5,4},{6,5},{7,6},{8,15},{9,8},{10,9... | collective-permute-start | bytes 786440 | tf_op jit(solution)/shard_map/ppermute | solution.py:348
  12.3 2.9 %pick_head.1.refs_17_ = bf16[1024,256]{1,0:T(8,128)(2,1)} custom-call(s32[2]{0:T(128)} %pad_add_fusion.place_ref.refs_0_, bf16[1024,1536]{1,0:T(8,128)(2,1)} %refs_1_.3, bf16[1024,1536]{1,0:T(8,128)(2,1)} %refs_1_.3, bf16[1024,1536]{1,0:T(8,128)(2,1)} %refs_1_.3), custom_call_target="tpu_custom_call" | custom-call | bytes 4194304 | tf_op jit(solution)/shard_map/pick_head/pallas_call | solution.py:93
  15.2 2.6 %d_out.1 = bf16[8,64,256]{2,1,0:T(8,128)(2,1)} custom-call(bf16[256,1024]{1,0:T(8,128)(2,1)} %refs_5_.1, bf16[512,1024]{1,0:T(8,128)(2,1)} %refs_19_.1), custom_call_target="tpu_custom_call" | custom-call | flops 268435456 | bytes 2097152 | tf_op jit(solution)/shard_map/d_out/pallas_call | solution.py:46
  20.0 3.7 %collective-permute-start.7 = (bf16[128,1024]{1,0:T(8,128)(2,1)}, bf16[128,1024]{1,0:T(8,128)(2,1)}, u32[]{:S(2)}, u32[]{:S(2)}) collective-permute-start(bf16[128,1024]{1,0:T(8,128)(2,1)} %collective-permute-done.6.refs_8_.refs_16_), channel_id=1, source_target_pairs={{0,7},{1,0},{2,1},{3,2},{4,3},{5,4},{6,5},{7,6},{8,15},{9,8},{10,9... | collective-permute-start | bytes 786440 | tf_op jit(solution)/shard_map/ppermute | solution.py:348
  23.7 3.2 %collective-permute-start.9 = (bf16[128,1024]{1,0:T(8,128)(2,1)}, bf16[128,1024]{1,0:T(8,128)(2,1)}, u32[]{:S(2)}, u32[]{:S(2)}) collective-permute-start(bf16[128,1024]{1,0:T(8,128)(2,1)} %collective-permute-done.1.refs_7_.refs_15_), channel_id=1, source_target_pairs={{0,7},{1,0},{2,1},{3,2},{4,3},{5,4},{6,5},{7,6},{8,15},{9,8},{10,9... | collective-permute-start | bytes 786440 | tf_op jit(solution)/shard_map/ppermute | solution.py:348
  26.9 5.6 %all-to-all-start = ((bf16[8,64,256]{2,1,0:T(8,128)(2,1)}), bf16[8,64,256]{2,1,0:T(8,128)(2,1)}, u32[]{:S(2)}, u32[]{:S(2)}) async-start(bf16[8,64,256]{2,1,0:T(8,128)(2,1)} %d_out.1), calls=%async_computation | async-start | bytes 524288 | tf_op jit(solution)/shard_map/all_to_all | solution.py:344
  36.5 2.4 %collective-permute-done.9.refs_13_ = bf16[128,1024]{1,0:T(8,128)(2,1)} collective-permute-done((bf16[128,1024]{1,0:T(8,128)(2,1)}, bf16[128,1024]{1,0:T(8,128)(2,1)}, u32[]{:S(2)}, u32[]{:S(2)}) %collective-permute-start.9) | collective-permute-done | bytes 262176 | tf_op jit(solution)/shard_map/ppermute | solution.py:348
  38.9 4.3 %collective-permute-start.13 = (bf16[128,1024]{1,0:T(8,128)(2,1)}, bf16[128,1024]{1,0:T(8,128)(2,1)}, u32[]{:S(2)}, u32[]{:S(2)}) collective-permute-start(bf16[128,1024]{1,0:T(8,128)(2,1)} %collective-permute-done.9.refs_13_), channel_id=1, source_target_pairs={{0,7},{1,0},{2,1},{3,2},{4,3},{5,4},{6,5},{7,6},{8,15},{9,8},{10,9... | collective-permute-start | bytes 786440 | tf_op jit(solution)/shard_map/ppermute | solution.py:348
  43.2 7.1 %messages.1 = (f32[256,1024]{1,0:T(8,128)}, bf16[256,1024]{1,0:T(8,128)(2,1)}, f32[256,1024]{1,0:T(8,128)}, bf16[256,1024]{1,0:T(8,128)(2,1)}) custom-call(s32[2]{0:T(128)} %pad_add_fusion.place_ref.refs_0_, s32[2,4]{1,0:T(2,128)} %refs_1_.2, s32[2]{0:T(128)} %refs_2_.1, bf16[128,1024]{1,0:T(8,128)(2,1)} %copy-done.1, ...), custom_call_target="tpu_custom_call" | custom-call | flops 2147483648 | bytes 8388608 | tf_op jit(solution)/shard_map/messages/pallas_call | solution.py:46
  50.5 3.2 %collective-permute-start.12 = (bf16[128,1024]{1,0:T(8,128)(2,1)}, bf16[128,1024]{1,0:T(8,128)(2,1)}, u32[]{:S(2)}, u32[]{:S(2)}) collective-permute-start(bf16[128,1024]{1,0:T(8,128)(2,1)} %collective-permute-done.8.refs_12_), channel_id=1, source_target_pairs={{0,7},{1,0},{2,1},{3,2},{4,3},{5,4},{6,5},{7,6},{8,15},{9,8},{10,9... | collective-permute-start | bytes 786440 | tf_op jit(solution)/shard_map/ppermute | solution.py:348
  55.7 5.4 %collective-permute-done.11.refs_9_ = bf16[128,1024]{1,0:T(8,128)(2,1)S(1)} collective-permute-done((bf16[128,1024]{1,0:T(8,128)(2,1)}, bf16[128,1024]{1,0:T(8,128)(2,1)S(1)}, u32[]{:S(2)}, u32[]{:S(2)}) %collective-permute-start.11) | collective-permute-done | bytes 262176 | tf_op jit(solution)/shard_map/ppermute | solution.py:348
  61.8 12.5 %attend_forward.1 = (bf16[8,64,256]{2,1,0:T(8,128)(2,1)}, bf16[8,256,128]{2,1,0:T(8,128)(2,1)}, bf16[8,64,256]{2,1,0:T(8,128)(2,1)}, bf16[8,64,256]{2,1,0:T(8,12...) custom-call(s32[2]{0:T(128)} %pad_add_fusion.place_ref.refs_0_, ...), custom_call_target="tpu_custom_call" | custom-call | flops 3221225472 | bytes 8388608 | tf_op jit(solution)/shard_map/attend_forward/pallas_call | solution.py:46
  74.4 2.9 %merge.1 = (bf16[8,192,256]{2,1,0:T(8,128)(2,1)}, bf16[256,1024]{1,0:T(8,128)(2,1)}) custom-call(bf16[8,64,256]{2,1,0:T(8,128)(2,1)} %get-tuple-element.59.heads_ref.refs_1_, f32[256,1024]{1,0:T(8,128)} %get-tuple-element.65.mid_ref, bf16[256,1024]{1,0:T(8,128)(2,1)} %collective-permute-done.14.above_ref, bf16[256,1024]{1,0:T(8,128)(2,1)} %collective-permute-done.15.below_ref), custom_call_target="tpu_custom_call" | custom-call | bytes 4194304 | tf_op jit(solution)/shard_map/merge/pallas_call | solution.py:46
  77.2 4.3 %all-to-all-start.1 = ((bf16[8,192,256]{2,1,0:T(8,128)(2,1)}), bf16[8,192,256]{2,1,0:T(8,128)(2,1)}, u32[]{:S(2)}, u32[]{:S(2)}) async-start(bf16[8,192,256]{2,1,0:T(8,128)(2,1)} %get-tuple-element.71), calls=%async_computation.1 | async-start | bytes 1572864 | tf_op jit(solution)/shard_map/all_to_all | solution.py:344
  81.6 15.3 %attend_backward.1.refs_18_ = bf16[8,192,256]{2,1,0:T(8,128)(2,1)} custom-call(s32[2]{0:T(128)} %pad_add_fusion.place_ref.refs_0_, bf16[8,64,256]{2,1,0:T(8,128)(2,1)} %get-tuple-element.59.heads_ref.refs_1_, bf16[8,256,128]{2,1,0:T(8,128)(2,1)} %get-tuple-element.60.refs_2_, bf16[8,64,256]{2,1,0:T(8,128)(2,1)} %get-tuple-element.61.refs_3_, ...), custom_call_target="tpu_custom_call" | custom-call | flops 6442450944 | bytes 4194304 | tf_op jit(solution)/shard_map/attend_backward/pallas_call | solution.py:46
  98.9 5.2 %all-to-all-start.2 = ((bf16[8,192,256]{2,1,0:T(8,128)(2,1)}), bf16[8,192,256]{2,1,0:T(8,128)(2,1)}, u32[]{:S(2)}, u32[]{:S(2)}) async-start(bf16[8,192,256]{2,1,0:T(8,128)(2,1)} %attend_backward.1.refs_18_), calls=%async_computation.2 | async-start | bytes 1572864 | tf_op jit(solution)/shard_map/all_to_all | solution.py:344
  104.2 7.6 %result.1 = (bf16[256,1024]{1,0:T(8,128)(2,1)}, bf16[16,224,128]{2,1,0:T(8,128)(2,1)}, bf16[16,224,128]{2,1,0:T(8,128)(2,1)}) custom-call(s32[2]{0:T(128)} %pad_add_fusion.place_ref.refs_0_, bf16[128,1024]{1,0:T(8,128)(2,1)} %get-tuple-element.47.refs_5_.refs_1_, bf16[128,1024]{1,0:T(8,128)(2,1)} %get-tuple-element.48.refs_6_.refs_2_, ...), custom_call_target="tpu_custom_call" | custom-call | flops 2147483648 | bytes 10485760 | tf_op jit(solution)/shard_map/result/pallas_call | solution.py:46
  111.8 2.7 %collective-permute-done.16 = bf16[16,224,128]{2,1,0:T(8,128)(2,1)S(1)} collective-permute-done((bf16[16,224,128]{2,1,0:T(8,128)(2,1)}, bf16[16,224,128]{2,1,0:T(8,128)(2,1)S(1)}, u32[]{:S(2)}, u32[]{:S(2)}) %collective-permute-start.16) | collective-permute-done | bytes 917536 | tf_op jit(solution)/shard_map/ppermute | solution.py:456
  115.9 5.2 %all-to-all-done.2.refs_0_ = bf16[8,192,256]{2,1,0:T(8,128)(2,1)} async-done(((bf16[8,192,256]{2,1,0:T(8,128)(2,1)}), bf16[8,192,256]{2,1,0:T(8,128)(2,1)}, u32[]{:S(2)}, u32[]{:S(2)}) %all-to-all-start.2) | async-done | bytes 786464 | tf_op jit(solution)/shard_map/all_to_all | solution.py:344
  121.1 17.4 %all_to_all.25.shares_ref = bf16[16,224,128]{2,1,0:T(8,128)(2,1)} all-to-all(bf16[16,224,128]{2,1,0:T(8,128)(2,1)S(1)} %add_convert_fusion), channel_id=1, replica_groups=mesh['x'=4,'y'=4,'c'=2,'z'=8] {'x','y'}, dimensions={0} | all-to-all | bytes 1835008 | tf_op jit(solution)/shard_map/all_to_all | solution.py:344
  140.6 5.9 %all-to-all-start.4 = ((bf16[8,224,128]{2,1,0:T(8,128)(2,1)}), bf16[8,224,128]{2,1,0:T(8,128)(2,1)S(1)}, u32[]{:S(2)}, u32[]{:S(2)}) async-start(bf16[8,224,128]{2,1,0:T(8,128)(2,1)} %share_sum.1), calls=%async_computation.4 | async-start | bytes 917504 | tf_op jit(solution)/shard_map/all_to_all | solution.py:344
  150.8 5.8 %input_grad.1 = bf16[256,1024]{1,0:T(8,128)(2,1)} custom-call(bf16[8,192,256]{2,1,0:T(8,128)(2,1)} %all-to-all-done.2.refs_0_, bf16[1024,1536]{1,0:T(8,128)(2,1)} %refs_1_.3, bf16[256,1024]{1,0:T(8,128)(2,1)} %get-tuple-element.81.refs_2_, bf16[1024,1024]{1,0:T(8,128)(2,1)} %refs_3_.1, bf16[256,1024]{1,0:T(8,128)(2,1)} %refs_4_.1, ...), custom_call_target="tpu_custom_call" | custom-call | flops 805306368 | bytes 8388608 | tf_op jit(solution)/shard_map/input_grad/pallas_call | solution.py:46
  156.6 4.8 %all-to-all-done.4.every_ref = bf16[8,224,128]{2,1,0:T(8,128)(2,1)S(1)} async-done(((bf16[8,224,128]{2,1,0:T(8,128)(2,1)}), bf16[8,224,128]{2,1,0:T(8,128)(2,1)S(1)}, u32[]{:S(2)}, u32[]{:S(2)}) %all-to-all-start.4) | async-done | bytes 458784 | tf_op jit(solution)/shard_map/all_to_all | solution.py:344
  (41 shorter events, 26.1 us)
Async XLA Ops:
  2.6 15.2 %collective-permute-start = (bf16[128,1024]{1,0:T(8,128)(2,1)}, bf16[128,1024]{1,0:T(8,128)(2,1)S(1)}, u32[]{:S(2)}, u32[]{:S(2)}) collective-permute-start(bf16[128,1024]{1,0:T(8,128)(2,1)} %get-tuple-element.47.refs_5_.refs_1_), channel_id=1, source_target_pairs={{0,1},{1,2},{2,3},{3,4},{4,5},{5,6},{6,7},{7,0},{8,9},{9,10},{10,1... | collective-permute-start | bytes 786440 | tf_op jit(solution)/shard_map/ppermute | solution.py:348
  4.5 13.3 %collective-permute-start.1 = (bf16[128,1024]{1,0:T(8,128)(2,1)}, bf16[128,1024]{1,0:T(8,128)(2,1)}, u32[]{:S(2)}, u32[]{:S(2)}) collective-permute-start(bf16[128,1024]{1,0:T(8,128)(2,1)} %get-tuple-element.47.refs_5_.refs_1_), channel_id=1, source_target_pairs={{0,7},{1,0},{2,1},{3,2},{4,3},{5,4},{6,5},{7,6},{8,15},{9,8},{10,9... | collective-permute-start | bytes 786440 | tf_op jit(solution)/shard_map/ppermute | solution.py:348
  8.5 15.2 %collective-permute-start.2 = (bf16[128,1024]{1,0:T(8,128)(2,1)}, bf16[128,1024]{1,0:T(8,128)(2,1)}, u32[]{:S(2)}, u32[]{:S(2)}) collective-permute-start(bf16[128,1024]{1,0:T(8,128)(2,1)} %get-tuple-element.48.refs_6_.refs_2_), channel_id=1, source_target_pairs={{0,1},{1,2},{2,3},{3,4},{4,5},{5,6},{6,7},{7,0},{8,9},{9,10},{10,1... | collective-permute-start | bytes 786440 | tf_op jit(solution)/shard_map/ppermute | solution.py:348
  8.5 11.5 %collective-permute-start.6 = (bf16[128,1024]{1,0:T(8,128)(2,1)}, bf16[128,1024]{1,0:T(8,128)(2,1)}, u32[]{:S(2)}, u32[]{:S(2)}) collective-permute-start(bf16[128,1024]{1,0:T(8,128)(2,1)} %get-tuple-element.48.refs_6_.refs_2_), channel_id=1, source_target_pairs={{0,7},{1,0},{2,1},{3,2},{4,3},{5,4},{6,5},{7,6},{8,15},{9,8},{10,9... | collective-permute-start | bytes 786440 | tf_op jit(solution)/shard_map/ppermute | solution.py:348
  17.8 25.4 %copy-start.1 = (bf16[128,1024]{1,0:T(8,128)(2,1)}, bf16[128,1024]{1,0:T(8,128)(2,1)S(1)}, u32[]{:S(2)}) copy-start(bf16[128,1024]{1,0:T(8,128)(2,1)S(1)} %collective-permute-done.refs_3_) | copy-start | bytes 786436
  17.8 9.1 %collective-permute-start.3 = (bf16[128,1024]{1,0:T(8,128)(2,1)S(1)}, bf16[128,1024]{1,0:T(8,128)(2,1)}, u32[]{:S(2)}, u32[]{:S(2)}) collective-permute-start(bf16[128,1024]{1,0:T(8,128)(2,1)S(1)} %collective-permute-done.refs_3_), channel_id=1, source_target_pairs={{0,1},{1,2},{2,3},{3,4},{4,5},{5,6},{6,7},{7,0},{8,9},{9,10},{10,1... | collective-permute-start | bytes 786440 | tf_op jit(solution)/shard_map/ppermute | solution.py:348
  20.0 14.5 %collective-permute-start.7 = (bf16[128,1024]{1,0:T(8,128)(2,1)}, bf16[128,1024]{1,0:T(8,128)(2,1)}, u32[]{:S(2)}, u32[]{:S(2)}) collective-permute-start(bf16[128,1024]{1,0:T(8,128)(2,1)} %collective-permute-done.6.refs_8_.refs_16_), channel_id=1, source_target_pairs={{0,7},{1,0},{2,1},{3,2},{4,3},{5,4},{6,5},{7,6},{8,15},{9,8},{10,9... | collective-permute-start | bytes 786440 | tf_op jit(solution)/shard_map/ppermute | solution.py:348
  23.7 12.1 %collective-permute-start.4 = (bf16[128,1024]{1,0:T(8,128)(2,1)}, bf16[128,1024]{1,0:T(8,128)(2,1)}, u32[]{:S(2)}, u32[]{:S(2)}) collective-permute-start(bf16[128,1024]{1,0:T(8,128)(2,1)} %collective-permute-done.2.refs_4_), channel_id=1, source_target_pairs={{0,1},{1,2},{2,3},{3,4},{4,5},{5,6},{6,7},{7,0},{8,9},{9,10},{10,1... | collective-permute-start | bytes 786440 | tf_op jit(solution)/shard_map/ppermute | solution.py:348
  23.7 15.2 %collective-permute-start.9 = (bf16[128,1024]{1,0:T(8,128)(2,1)}, bf16[128,1024]{1,0:T(8,128)(2,1)}, u32[]{:S(2)}, u32[]{:S(2)}) collective-permute-start(bf16[128,1024]{1,0:T(8,128)(2,1)} %collective-permute-done.1.refs_7_.refs_15_), channel_id=1, source_target_pairs={{0,7},{1,0},{2,1},{3,2},{4,3},{5,4},{6,5},{7,6},{8,15},{9,8},{10,9... | collective-permute-start | bytes 786440 | tf_op jit(solution)/shard_map/ppermute | solution.py:348
  26.9 23.4 %all-to-all-start = ((bf16[8,64,256]{2,1,0:T(8,128)(2,1)}), bf16[8,64,256]{2,1,0:T(8,128)(2,1)}, u32[]{:S(2)}, u32[]{:S(2)}) async-start(bf16[8,64,256]{2,1,0:T(8,128)(2,1)} %d_out.1), calls=%async_computation | async-start | bytes 524288 | tf_op jit(solution)/shard_map/all_to_all | solution.py:344
  32.5 17.9 %collective-permute-start.5 = (bf16[128,1024]{1,0:T(8,128)(2,1)}, bf16[128,1024]{1,0:T(8,128)(2,1)}, u32[]{:S(2)}, u32[]{:S(2)}) collective-permute-start(bf16[128,1024]{1,0:T(8,128)(2,1)} %collective-permute-done.3.refs_5_), channel_id=1, source_target_pairs={{0,1},{1,2},{2,3},{3,4},{4,5},{5,6},{6,7},{7,0},{8,9},{9,10},{10,1... | collective-permute-start | bytes 786440 | tf_op jit(solution)/shard_map/ppermute | solution.py:348
  34.5 15.8 %collective-permute-start.8 = (bf16[128,1024]{1,0:T(8,128)(2,1)}, bf16[128,1024]{1,0:T(8,128)(2,1)}, u32[]{:S(2)}, u32[]{:S(2)}) collective-permute-start(bf16[128,1024]{1,0:T(8,128)(2,1)} %collective-permute-done.7.refs_14_), channel_id=1, source_target_pairs={{0,7},{1,0},{2,1},{3,2},{4,3},{5,4},{6,5},{7,6},{8,15},{9,8},{10,9... | collective-permute-start | bytes 786440 | tf_op jit(solution)/shard_map/ppermute | solution.py:348
  35.8 17.9 %collective-permute-start.10 = (bf16[128,1024]{1,0:T(8,128)(2,1)}, bf16[128,1024]{1,0:T(8,128)(2,1)}, u32[]{:S(2)}, u32[]{:S(2)}) collective-permute-start(bf16[128,1024]{1,0:T(8,128)(2,1)} %collective-permute-done.4.refs_6_), channel_id=1, source_target_pairs={{0,1},{1,2},{2,3},{3,4},{4,5},{5,6},{6,7},{7,0},{8,9},{9,10},{10,1... | collective-permute-start | bytes 786440 | tf_op jit(solution)/shard_map/ppermute | solution.py:348
  38.9 16.8 %collective-permute-start.13 = (bf16[128,1024]{1,0:T(8,128)(2,1)}, bf16[128,1024]{1,0:T(8,128)(2,1)}, u32[]{:S(2)}, u32[]{:S(2)}) collective-permute-start(bf16[128,1024]{1,0:T(8,128)(2,1)} %collective-permute-done.9.refs_13_), channel_id=1, source_target_pairs={{0,7},{1,0},{2,1},{3,2},{4,3},{5,4},{6,5},{7,6},{8,15},{9,8},{10,9... | collective-permute-start | bytes 786440 | tf_op jit(solution)/shard_map/ppermute | solution.py:348
  50.4 10.7 %collective-permute-start.11 = (bf16[128,1024]{1,0:T(8,128)(2,1)}, bf16[128,1024]{1,0:T(8,128)(2,1)S(1)}, u32[]{:S(2)}, u32[]{:S(2)}) collective-permute-start(bf16[128,1024]{1,0:T(8,128)(2,1)} %collective-permute-done.5.refs_7_), channel_id=1, source_target_pairs={{0,1},{1,2},{2,3},{3,4},{4,5},{5,6},{6,7},{7,0},{8,9},{9,10},{10,1... | collective-permute-start | bytes 786440 | tf_op jit(solution)/shard_map/ppermute | solution.py:348
  50.5 10.7 %collective-permute-start.12 = (bf16[128,1024]{1,0:T(8,128)(2,1)}, bf16[128,1024]{1,0:T(8,128)(2,1)}, u32[]{:S(2)}, u32[]{:S(2)}) collective-permute-start(bf16[128,1024]{1,0:T(8,128)(2,1)} %collective-permute-done.8.refs_12_), channel_id=1, source_target_pairs={{0,7},{1,0},{2,1},{3,2},{4,3},{5,4},{6,5},{7,6},{8,15},{9,8},{10,9... | collective-permute-start | bytes 786440 | tf_op jit(solution)/shard_map/ppermute | solution.py:348
  53.7 20.7 %collective-permute-start.14 = (bf16[256,1024]{1,0:T(8,128)(2,1)}, bf16[256,1024]{1,0:T(8,128)(2,1)}, u32[]{:S(2)}, u32[]{:S(2)}) collective-permute-start(bf16[256,1024]{1,0:T(8,128)(2,1)} %get-tuple-element.66), channel_id=1, source_target_pairs={{0,7},{1,0},{2,1},{3,2},{4,3},{5,4},{6,5},{7,6},{8,15},{9,8},{10,9... | collective-permute-start | bytes 1572872 | tf_op jit(solution)/shard_map/ppermute | solution.py:348
  53.7 20.7 %collective-permute-start.15 = (bf16[256,1024]{1,0:T(8,128)(2,1)}, bf16[256,1024]{1,0:T(8,128)(2,1)}, u32[]{:S(2)}, u32[]{:S(2)}) collective-permute-start(bf16[256,1024]{1,0:T(8,128)(2,1)} %get-tuple-element.67), channel_id=1, source_target_pairs={{0,1},{1,2},{2,3},{3,4},{4,5},{5,6},{6,7},{7,0},{8,9},{9,10},{10,1... | collective-permute-start | bytes 1572872 | tf_op jit(solution)/shard_map/ppermute | solution.py:348
  61.1 0.7 copy-start.2
  77.2 21.7 %all-to-all-start.1 = ((bf16[8,192,256]{2,1,0:T(8,128)(2,1)}), bf16[8,192,256]{2,1,0:T(8,128)(2,1)}, u32[]{:S(2)}, u32[]{:S(2)}) async-start(bf16[8,192,256]{2,1,0:T(8,128)(2,1)} %get-tuple-element.71), calls=%async_computation.1 | async-start | bytes 1572864 | tf_op jit(solution)/shard_map/all_to_all | solution.py:344
  98.9 22.2 %all-to-all-start.2 = ((bf16[8,192,256]{2,1,0:T(8,128)(2,1)}), bf16[8,192,256]{2,1,0:T(8,128)(2,1)}, u32[]{:S(2)}, u32[]{:S(2)}) async-start(bf16[8,192,256]{2,1,0:T(8,128)(2,1)} %attend_backward.1.refs_18_), calls=%async_computation.2 | async-start | bytes 1572864 | tf_op jit(solution)/shard_map/all_to_all | solution.py:344
  111.7 2.8 %collective-permute-start.16 = (bf16[16,224,128]{2,1,0:T(8,128)(2,1)}, bf16[16,224,128]{2,1,0:T(8,128)(2,1)S(1)}, u32[]{:S(2)}, u32[]{:S(2)}) collective-permute-start(bf16[16,224,128]{2,1,0:T(8,128)(2,1)} %get-tuple-element.77), channel_id=1, source_target_pairs={{0,8},{8,0},{1,9},{9,1},{2,10},{10,2},{3,11},{11,3},{4,12},{12,4},... | collective-permute-start | bytes 2752520 | tf_op jit(solution)/shard_map/ppermute | solution.py:456
  140.6 20.8 %all-to-all-start.4 = ((bf16[8,224,128]{2,1,0:T(8,128)(2,1)}), bf16[8,224,128]{2,1,0:T(8,128)(2,1)S(1)}, u32[]{:S(2)}, u32[]{:S(2)}) async-start(bf16[8,224,128]{2,1,0:T(8,128)(2,1)} %share_sum.1), calls=%async_computation.4 | async-start | bytes 917504 | tf_op jit(solution)/shard_map/all_to_all | solution.py:344
  161.4 0.8 copy-start
